TPU v7x, 32 devices: a whole 2x2x4 slice. The times are simulated.
32 devices in a mesh: bucket: 4 (over z), batch: 8 (over y, x, core).
Axes of the slice: x: 2, y: 2, z: 4, core: 2. Of those that a mesh axis runs over, the one named last changes fastest.
Arguments:
- images: float32 [640, 3, 1024], P(('bucket', 'batch')), may hold values from -4 to 4
- pixel_mask: int32 [640, 1024], P(('bucket', 'batch')), may hold values from 0 to 1, as said below
- timesteps: int32 [640], P(('bucket', 'batch')), may hold values from 0 to 999, as said below
- noise_field: float32 [640, 3, 1024], P(('bucket', 'batch')), may hold values from -5 to 5
- matrices: float32 [5120, 256], P('bucket')
- matrix_moms: float32 [5120, 256], P('bucket'), may hold values from -0.004941059 to 0.004941059
- stem_weight: float32 [27, 128], replicated, may hold values from -1.25 to 1.25
- stem_moms: float32 [27, 128], replicated, may hold values from -0.004941059 to 0.004941059
- head_weight: float32 [3456, 12], replicated, may hold values from -0.109375 to 0.109375
- head_moms: float32 [3456, 12], replicated, may hold values from -0.004941059 to 0.004941059
- vectors: float32 [2956], replicated, may hold values from 0.25 to 1.75
- vector_firsts: float32 [2956], replicated, may hold values from -0.00049410586 to 0.00049410586
- vector_seconds: float32 [2956], replicated, may hold values from 1.5258789e-09 to 6.1035155e-09
Outputs:
- loss_sum: float32 [], replicated
- weight_sum: float32 [], replicated
- new_matrices: float32 [5120, 256], P('bucket')
- new_matrix_moms: float32 [5120, 256], P('bucket')
- matrix_copies: bfloat16 [5120, 256], P('bucket')
- new_stem: float32 [27, 128], replicated
- new_stem_moms: float32 [27, 128], replicated
- stem_copy: bfloat16 [27, 128], replicated
- new_head: float32 [3456, 12], replicated
- new_head_moms: float32 [3456, 12], replicated
- head_copy: bfloat16 [3456, 12], replicated
- new_vectors: float32 [2956], replicated
- new_firsts: float32 [2956], replicated
- new_seconds: float32 [2956], replicated
- vector_copy: bfloat16 [2956], replicated
Inputs may be any that keep to these rules, and one draw needn't show every extreme that they name: `pixel_mask`: 0 or 1; the share of ones differs from image to image. `timesteps`: an image on index b of the bucket axis has a timestep in [b * 1000 / 4, (b + 1) * 1000 / 4).
All inputs are finite; a program needn't handle non-finite values.
Results may differ from a plain program's by a relative error of at most 0.007.
The roundings to bfloat16 on the way count: a program that leaves them out, or rounds other values in their place, can miss the bound.
Values may be sent and summed in bfloat16 or wider, within the bound.
A program may use at most 512 MiB of HBM per device.

v0:
```python
import math

import jax
import jax.numpy as jnp
from jax import lax
from jax.sharding import PartitionSpec as P

C1 = 128
CHANNELS_MID = 256
TEMB = 512
GROUPS = 32
S = 32
TSTEPS = 1000
NS_STEPS = 5
STEP = 10


GN_EPS = 1e-05
NORM_EPS = 1e-12
MOMENTUM = 0.95
LR_MUON = 0.5
DECAY = 0.01
NS_A = 3.4445
NS_B = -4.775
NS_C = 2.0315
BETA_ONE = 0.9
BETA_TWO = 0.999
LR_ADAM = 0.5
ADAM_EPS = 1e-08
EXACT_PRECISION = lax.Precision.HIGHEST
LOWTYPE = jnp.bfloat16


def for_sending(shard):
    return jax.tree.map(lambda a: a.astype(jnp.bfloat16) if a.dtype == jnp.float32 else a, shard)


def segment_rows():
    return [
        9 * C1,
        9 * CHANNELS_MID,
        C1,
        TEMB,
        CHANNELS_MID,
        CHANNELS_MID,
        CHANNELS_MID,
        CHANNELS_MID,
    ]


def unpack(packed, owners):
    blocks = packed.reshape(owners, -1, packed.shape[1])
    pieces = []
    start = 0
    for seg_rows in segment_rows():
        share = seg_rows // owners
        pieces.append(blocks[:, start : start + share, :].reshape(seg_rows, packed.shape[1]))
        start += share
    return pieces


def pack(pieces, owners):
    blocks = [piece.reshape(owners, -1, piece.shape[1]) for piece in pieces]
    return jnp.concatenate(blocks, axis=1).reshape(-1, pieces[0].shape[1])


def split_vector(vectors):
    lengths = [C1, C1, C1] + [CHANNELS_MID] * 10 + [12]
    pieces = []
    start = 0
    for length in lengths:
        pieces.append(vectors[start : start + length])
        start += length
    return pieces


def plan(timesteps):
    frac_t = (timesteps.astype(jnp.float32) / TSTEPS + 0.008) / 1.008
    level = jnp.cos(frac_t * (math.pi / 2)) ** 2
    ratio = level / (1.0 - level)
    return (level, jnp.minimum(1.0, 5.0 / ratio))


def embed(timesteps):
    half_width = TEMB // 2
    freqs = jnp.exp(-math.log(10000.0) * jnp.arange(half_width, dtype=jnp.float32) / half_width)
    angles = timesteps.astype(jnp.float32)[:, None] * freqs[None, :]
    return jnp.concatenate([jnp.sin(angles), jnp.cos(angles)], axis=1)


def swish(values):
    return values * jax.nn.sigmoid(values)


def group_norm(values, gain_v, shift_v):
    samples, places, chans = values.shape
    grouped = values.reshape(samples, places, GROUPS, chans // GROUPS)
    centre = jnp.mean(grouped, axis=(1, 3), keepdims=True)
    centered = grouped - centre
    spread = jnp.mean(centered * centered, axis=(1, 3), keepdims=True)
    normed = (centered * lax.rsqrt(spread + GN_EPS)).reshape(samples, places, chans)
    return normed * gain_v + shift_v


def norm_act(values, gain_v, shift_v):
    return swish(group_norm(values, gain_v, shift_v))


def join_act(output, pooled):
    return swish(jnp.concatenate([output, pooled], axis=2))


def patches(grid):
    samples, height, across, chans = grid.shape
    padded = jnp.pad(grid, ((0, 0), (1, 1), (1, 1), (0, 0)))
    parts = [
        padded[:, shift_y : shift_y + height, shift_x : shift_x + across, :]
        for shift_y in range(3)
        for shift_x in range(3)
    ]
    return jnp.concatenate(parts, axis=3).reshape(samples, height * across, 9 * chans)


def unpatch(grad_cols, height, chans):
    samples = grad_cols.shape[0]
    parts = grad_cols.reshape(samples, height, height, 9, chans)
    total = None
    for shift_y in range(3):
        for shift_x in range(3):
            placed = jnp.pad(
                parts[:, :, :, shift_y * 3 + shift_x, :],
                ((0, 0), (shift_y, 2 - shift_y), (shift_x, 2 - shift_x), (0, 0)),
            )
            total = placed if total is None else total + placed
    return total[:, 1:-1, 1:-1, :].reshape(samples, height * height, chans)


def mult(left, right):
    return jnp.einsum("bpk,kn->bpn", left, right, preferred_element_type=jnp.float32)


def back_mult(grad_out, right):
    return jnp.einsum("bpn,kn->bpk", grad_out, right, preferred_element_type=jnp.float32)


def weight_grad(left, grad_out):
    return jnp.einsum("bpk,bpn->kn", left, grad_out, preferred_element_type=jnp.float32)


def row_total(values):
    return jnp.sum(values, axis=(0, 1))


def ns_update(iterate, gram):
    inner = NS_B * gram + NS_C * jnp.dot(gram, gram, precision=EXACT_PRECISION)
    return NS_A * iterate + jnp.dot(iterate, inner, precision=EXACT_PRECISION)


def local_muon(weight_m, moment, gradient):
    moment_new = MOMENTUM * moment + gradient
    direction = gradient + MOMENTUM * moment_new
    iterate = direction * lax.rsqrt(jnp.sum(direction * direction) + NORM_EPS)
    for step in range(NS_STEPS):
        iterate = ns_update(iterate, jnp.dot(iterate.T, iterate, precision=EXACT_PRECISION))
    return (weight_m * (1.0 - LR_MUON * DECAY) - LR_MUON * iterate, moment_new)


def grams(pieces):
    return list(
        jax.tree.map(
            lambda part: part.astype(jnp.float32),
            lax.psum(
                for_sending(
                    tuple((jnp.dot(piece.T, piece, precision=EXACT_PRECISION) for piece in pieces))
                ),
                "bucket",
            ),
        )
    )


def shards(
    images,
    pixel_mask,
    timesteps,
    noise_field,
    matrices,
    matrix_moms,
    stem_weight,
    stem_moms,
    head_weight,
    head_moms,
    vectors,
    vector_firsts,
    vector_seconds,
):
    owners = lax.axis_size("bucket")
    gathered = lax.all_gather(matrices.astype(LOWTYPE), "bucket", axis=0, tiled=True)
    conv_one, conv_two, skip_w, temb_w, query_w, key_w, value_w, out_w = unpack(gathered, owners)
    proj_all = jnp.concatenate([query_w, key_w, value_w], axis=1)
    stem_low = stem_weight.astype(LOWTYPE)
    head_low = head_weight.astype(LOWTYPE)
    (
        stem_b,
        gain_one,
        shift_one,
        conv_one_b,
        temb_b,
        gain_two,
        shift_two,
        conv_two_b,
        gain_att,
        shift_att,
        query_b,
        value_b,
        out_b,
        head_b,
    ) = split_vector(vectors)
    samples = images.shape[0]
    half_side = S // 2
    level, weight = plan(timesteps)
    counts = jnp.sum(pixel_mask.astype(jnp.float32), axis=1)
    weight_sum = lax.psum(jnp.sum(3.0 * weight * counts), ("bucket", "batch"))
    noisy = (
        jnp.sqrt(level)[:, None, None] * images + jnp.sqrt(1.0 - level)[:, None, None] * noise_field
    )
    grid = noisy.reshape(samples, 3, S, S).transpose(0, 2, 3, 1).astype(LOWTYPE)
    cols_stem = patches(grid)
    stem_out = mult(cols_stem, stem_low) + stem_b
    pooled = jnp.mean(
        stem_out.reshape(samples, half_side, 2, half_side, 2, C1), axis=(2, 4)
    ).reshape(samples, -1, C1)
    pooled_low = pooled.astype(LOWTYPE)
    act_one_f, pull_one = jax.vjp(norm_act, pooled, gain_one, shift_one)
    cols_one = patches(act_one_f.astype(LOWTYPE).reshape(samples, half_side, half_side, C1))
    time_in = swish(embed(timesteps)).astype(LOWTYPE)
    time_proj = jnp.dot(time_in, temb_w, preferred_element_type=jnp.float32) + temb_b
    hidden_one = mult(cols_one, conv_one) + conv_one_b + time_proj[:, None, :]
    act_two_f, pull_two = jax.vjp(norm_act, hidden_one, gain_two, shift_two)
    cols_two = patches(
        act_two_f.astype(LOWTYPE).reshape(samples, half_side, half_side, CHANNELS_MID)
    )
    resid = mult(pooled_low, skip_w) + mult(cols_two, conv_two) + conv_two_b
    normed_f, pull_att = jax.vjp(group_norm, resid, gain_att, shift_att)
    normed = normed_f.astype(LOWTYPE)
    joined = mult(normed, proj_all)
    query_rows = (joined[:, :, :CHANNELS_MID] + query_b).astype(LOWTYPE)
    key_rows_reduced = joined[:, :, CHANNELS_MID : 2 * CHANNELS_MID].astype(LOWTYPE)
    value_rows_reduced = (joined[:, :, 2 * CHANNELS_MID :] + value_b).astype(LOWTYPE)
    query_scale = CHANNELS_MID ** (-0.5)
    attention_logits = (
        jnp.einsum("upo,uwo->upw", query_rows, key_rows_reduced, preferred_element_type=jnp.float32)
        * query_scale
    )
    attn_f = jax.nn.softmax(attention_logits, axis=-1)
    attention_reduced = attn_f.astype(LOWTYPE)
    attention_output = jnp.einsum(
        "lap,lph->lah", attention_reduced, value_rows_reduced, preferred_element_type=jnp.float32
    ).astype(LOWTYPE)
    output = resid + mult(attention_output, out_w) + out_b
    joined_f, pull_join = jax.vjp(join_act, output, pooled)
    cols_head = patches(
        joined_f.astype(LOWTYPE).reshape(samples, half_side, half_side, CHANNELS_MID + C1)
    )
    head_out = mult(cols_head, head_low) + head_b
    predicted = (
        head_out.reshape(samples, half_side, half_side, 2, 2, 3)
        .transpose(0, 5, 1, 3, 2, 4)
        .reshape(samples, 3, S * S)
    )
    error = predicted - noise_field
    masked = pixel_mask.astype(jnp.float32)[:, None, :] * weight[:, None, None]
    loss_local = jnp.sum(masked * error * error)
    grad_pred = 2.0 * masked * error / weight_sum
    grad_head_out = (
        grad_pred.reshape(samples, 3, half_side, 2, half_side, 2)
        .transpose(0, 2, 4, 3, 5, 1)
        .reshape(samples, -1, 12)
    )
    g_head_b = row_total(grad_head_out)
    grad_head_low = grad_head_out.astype(LOWTYPE)
    g_head = weight_grad(cols_head, grad_head_low)
    grad_joined = unpatch(back_mult(grad_head_low, head_low), half_side, CHANNELS_MID + C1)
    grad_output, grad_pool_head = pull_join(grad_joined)
    g_out_b = row_total(grad_output)
    grad_out_low = grad_output.astype(LOWTYPE)
    g_out = weight_grad(attention_output, grad_out_low)
    attention_gradient = back_mult(grad_out_low, out_w).astype(LOWTYPE)
    grad_weights = jnp.einsum(
        "upo,uwo->upw", attention_gradient, value_rows_reduced, preferred_element_type=jnp.float32
    )
    value_gradient = jnp.einsum(
        "fep,fet->fpt", attention_reduced, attention_gradient, preferred_element_type=jnp.float32
    )
    grad_scores = attn_f * (grad_weights - jnp.sum(grad_weights * attn_f, axis=-1, keepdims=True))
    unscaled_gradient = (grad_scores * query_scale).astype(LOWTYPE)
    grad_queries = jnp.einsum(
        "lap,lph->lah", unscaled_gradient, key_rows_reduced, preferred_element_type=jnp.float32
    )
    key_gradient = jnp.einsum(
        "fep,fet->fpt", unscaled_gradient, query_rows, preferred_element_type=jnp.float32
    )
    g_query_b = row_total(grad_queries)
    g_value_b = row_total(value_gradient)
    grad_joined_low = jnp.concatenate([grad_queries, key_gradient, value_gradient], axis=2).astype(
        LOWTYPE
    )
    g_proj = weight_grad(normed, grad_joined_low)
    grad_normed = back_mult(grad_joined_low, proj_all)
    grad_resid_att, g_gain_att, g_shift_att = pull_att(grad_normed)
    grad_resid = grad_output + grad_resid_att
    grad_resid_low = grad_resid.astype(LOWTYPE)
    g_skip = weight_grad(pooled_low, grad_resid_low)
    grad_pool_skip = back_mult(grad_resid_low, skip_w)
    g_conv_two_b = row_total(grad_resid)
    g_conv_two = weight_grad(cols_two, grad_resid_low)
    grad_act_two = unpatch(back_mult(grad_resid_low, conv_two), half_side, CHANNELS_MID)
    grad_hidden, g_gain_two, g_shift_two = pull_two(grad_act_two)
    g_conv_one_b = row_total(grad_hidden)
    grad_time = jnp.sum(grad_hidden, axis=1)
    g_temb_b = jnp.sum(grad_time, axis=0)
    g_temb = jnp.dot(time_in.T, grad_time.astype(LOWTYPE), preferred_element_type=jnp.float32)
    grad_hidden_low = grad_hidden.astype(LOWTYPE)
    g_conv_one = weight_grad(cols_one, grad_hidden_low)
    grad_act_one = unpatch(back_mult(grad_hidden_low, conv_one), half_side, C1)
    grad_pool_one, g_gain_one, g_shift_one = pull_one(grad_act_one)
    grad_pooled = grad_pool_head + grad_pool_skip + grad_pool_one
    grad_stem_out = jnp.broadcast_to(
        grad_pooled.reshape(samples, half_side, 1, half_side, 1, C1) * 0.25,
        (samples, half_side, 2, half_side, 2, C1),
    ).reshape(samples, S * S, C1)
    g_stem_b = row_total(grad_stem_out)
    g_stem = weight_grad(cols_stem, grad_stem_out.astype(LOWTYPE))
    grad_pack = pack(
        [
            g_conv_one,
            g_conv_two,
            g_skip,
            g_temb,
            g_proj[:, :CHANNELS_MID],
            g_proj[:, CHANNELS_MID : 2 * CHANNELS_MID],
            g_proj[:, 2 * CHANNELS_MID :],
            g_out,
        ],
        owners,
    )
    rows_dev = matrices.shape[0]
    summed = lax.psum(grad_pack, ("bucket", "batch"))
    grad_mine = lax.dynamic_slice_in_dim(summed, lax.axis_index("bucket") * rows_dev, rows_dev, 0)
    grad_vec = jnp.concatenate(
        [
            g_stem_b,
            g_gain_one,
            g_shift_one,
            g_conv_one_b,
            g_temb_b,
            g_gain_two,
            g_shift_two,
            g_conv_two_b,
            g_gain_att,
            g_shift_att,
            g_query_b,
            g_value_b,
            g_out_b,
            g_head_b,
        ]
    )
    grad_stem, grad_headw, grad_vec, loss_sum = lax.psum(
        (g_stem, g_head, grad_vec, loss_local), ("bucket", "batch")
    )
    shares = [seg_rows // owners for seg_rows in segment_rows()]
    weight_parts, moment_parts, grad_parts = ([], [], [])
    start = 0
    for share in shares:
        weight_parts.append(matrices[start : start + share])
        moment_parts.append(matrix_moms[start : start + share])
        grad_parts.append(grad_mine[start : start + share])
        start += share
    moments_new = [
        MOMENTUM * moment + gradient for moment, gradient in zip(moment_parts, grad_parts)
    ]
    directions = [gradient + MOMENTUM * moment for gradient, moment in zip(grad_parts, moments_new)]
    squares = lax.psum(
        tuple((jnp.sum(direction * direction) for direction in directions)), "bucket"
    )
    iterates = [
        direction * lax.rsqrt(square + NORM_EPS) for direction, square in zip(directions, squares)
    ]
    gram_now = grams(iterates)
    for step in range(NS_STEPS):
        if step > 0:
            gram_now = grams(iterates)
        iterates = [ns_update(iterate, gram) for iterate, gram in zip(iterates, gram_now)]
    new_matrices = jnp.concatenate(
        [
            weight_m * (1.0 - LR_MUON * DECAY) - LR_MUON * iterate
            for weight_m, iterate in zip(weight_parts, iterates)
        ],
        axis=0,
    )
    new_matrix_moms = jnp.concatenate(moments_new, axis=0)
    new_stem, new_stem_moms = local_muon(stem_weight, stem_moms, grad_stem)
    new_head, new_head_moms = local_muon(head_weight, head_moms, grad_headw)
    new_firsts = BETA_ONE * vector_firsts + (1.0 - BETA_ONE) * grad_vec
    new_seconds = BETA_TWO * vector_seconds + (1.0 - BETA_TWO) * grad_vec * grad_vec
    step_dir = (
        new_firsts
        / (1.0 - BETA_ONE**STEP)
        / (jnp.sqrt(new_seconds / (1.0 - BETA_TWO**STEP)) + ADAM_EPS)
    )
    new_vectors = vectors - LR_ADAM * step_dir
    return (
        loss_sum,
        weight_sum,
        new_matrices,
        new_matrix_moms,
        new_matrices.astype(LOWTYPE),
        new_stem,
        new_stem_moms,
        new_stem.astype(LOWTYPE),
        new_head,
        new_head_moms,
        new_head.astype(LOWTYPE),
        new_vectors,
        new_firsts,
        new_seconds,
        new_vectors.astype(LOWTYPE),
    )


def solution(mesh):
    return jax.shard_map(
        shards,
        mesh=mesh,
        in_specs=(
            P(("bucket", "batch"), None, None),
            P(("bucket", "batch"), None),
            P(("bucket", "batch")),
            P(("bucket", "batch"), None, None),
            P("bucket", None),
            P("bucket", None),
            P(),
            P(),
            P(),
            P(),
            P(),
            P(),
            P(),
        ),
        out_specs=(
            P(),
            P(),
            P("bucket", None),
            P("bucket", None),
            P("bucket", None),
            P(),
            P(),
            P(),
            P(),
            P(),
            P(),
            P(),
            P(),
            P(),
            P(),
        ),
        check_vma=False,
    )
```

profile of v0, /device:TPU:0, one launch (start us, length us, event | category | flops | bytes accessed | tf_op | source)
XLA Modules:
  0.0 1380.9 jit_solution(6189370163811929161)
XLA Ops:
  39.5 11.6 reduce_sum.516
  54.2 42.4 %psum.379 = f32[]{:T(128)} all-reduce(f32[]{:T(128)} %get-tuple-element.115), channel_id=1, replica_groups=mesh['bucket'=4,'batch'=8] {'bucket','batch'}, use_global_device_ids=true, to_apply=%region_19.20 | all-reduce | flops 1 | bytes 8 | tf_op jit(solution)/shard_map/psum | solution.py:223
  115.0 16.3 %copy.226 = bf16[1152,20,256]{2,0,1:T(8,128)(2,1)} copy(bf16[1152,20,256]{0,2,1:T(8,128)(2,1)} %bitcast.60) | data formatting | bytes 23592960 | tf_op jit(solution)/shard_map/bpk,bpn->kn/dot_general | solution.py:147
  143.5 11.0 fusion.9
  194.8 11.6 fusion.241
  237.3 16.6 %online-softmax = f32[20,256,256]{2,1,0:T(8,128)} custom-call(f32[20,256,256]{2,1,0:T(8,128)} %broadcast_multiply_fusion, f32[20,256,256]{2,1,0:T(8,128)} %slice_add_fusion), custom_call_target="tpu_custom_call" | custom-call | tf_op online-softmax
  262.4 21.7 %pad_slice_fusion = (bf16[20,16,16,384]{3,2,1,0:T(8,128)(2,1)S(1)}, bf16[20,16,16,384]{3,2,1,0:T(8,128)(2,1)}, bf16[20,16,16,384]{3,2,1,0:T(8,128)(2,1)}, bf16[2...) fusion(bf16[20,16,16,384]{3,2,1,0:T(8,128)(2,1)} %multiply_conv, ...), kind=kLoop, calls=%fused_computation.4 | loop fusion | bytes 35389440 | tf_op jit(solution)/shard_map/slice | solution.py:117
  312.2 15.8 %convolution_add_fusion.15 = f32[20,256,12]{1,2,0:T(8,128)S(1)} fusion(bf16[20,256,3456]{2,1,0:T(8,128)(2,1)} %constant_dynamic-update-slice_fusion.18, f32[12]{0:T(128)S(1)} %copy-done.115, bf16[3456,12]{0,1:T(8,128)(2,1)S(1)} %convert_element_type.446), kind=kOutput, calls=%fused_computation.209 | convolution fusion | flops 424734720 | bytes 35718192 | tf_op jit(solution)/shard_map/bpk,kn->bpn/dot_general | solution.py:139
  348.4 26.7 %fusion.171 = f32[20,16,16,9,384]{4,2,3,1,0:T(8,128)} fusion(bf16[20,16,16,12,1]{3,2,4,1,0:T(8,128)(2,1)} %copy.281, bf16[9,384,12,1,1]{1,0,2,4,3:T(8,128)(2,1)S(1)} %bitcast.710), kind=kOutput, calls=%fused_computation.502 | convolution fusion | flops 424673280 | bytes 70984704 | tf_op jit(solution)/shard_map/bpn,kn->bpk/dot_general | solution.py:143
  375.1 46.4 %slice_bitcast_fusion.8 = (f32[20,16,16,384]{3,2,1,0:T(8,128)}, f32[20,16,16,384]{3,2,1,0:T(8,128)}, f32[20,16,16,384]{3,2,1,0:T(8,128)}, f32[20,16,16,384]{3,2,...) fusion(f32[20,16,16,9,384]{4,2,3,1,0:T(8,128)} %fusion.171), kind=kLoop, calls=%fused_computation.29 | loop fusion | bytes 141557760 | tf_op jit(solution)/shard_map/squeeze | solution.py:131
  421.5 14.5 %pad_add_fusion = f32[20,18,18,384]{3,2,1,0:T(8,128)} fusion(f32[20,16,16,384]{3,2,1,0:T(8,128)} %get-tuple-element.123, f32[20,16,16,384]{3,2,1,0:T(8,128)} %get-tuple-element.124, f32[20,16,16,384]{3,2,1,0:T(8,128)} %get-tuple-element.118), kind=kLoop, calls=%fused_computation.2 | loop fusion | flops 4976640 | bytes 33546240 | tf_op jit(solution)/shard_map/add | solution.py:134
  436.0 23.3 %pad_add_fusion.2 = f32[20,16,16,384]{3,2,1,0:T(8,128)} fusion(f32[20,16,16,384]{3,2,1,0:T(8,128)} %get-tuple-element.125, f32[20,16,16,384]{3,2,1,0:T(8,128)} %get-tuple-element.126, f32[20,16,16,384]{3,2,1,0:T(8,128)} %get-tuple-element.119, f32[20,16,16,384]{3,2,1,0:T(8,128)} %get-tuple-element.120, f32[20,16,16,384]{3,2,1,0:T(8,128)} %get-tuple-element.121, ...), kind=kLoop, calls=%fused_computation.15 | loop fusion | flops 11796480 | bytes 62914560 | tf_op jit(solution)/shard_map/add | solution.py:134
  485.0 35.6 %fusion.229 = (f32[256]{0:T(256)}, bf16[20,256,256]{2,1,0:T(8,128)(2,1)}) fusion(f32[20,256,768]{2,1,0:T(8,128)} %copy-done.5, f32[20,256,256]{2,1,0:T(8,128)} %fusion.39, f32[20,256,256]{2,1,0:T(8,128)} %get-tuple-element.217, f32[20,256]{1,0:T(8,128)S(1)} %get-tuple-element.216), kind=kOutput, calls=%fused_computation.623 | convolution fusion | flops 682890240 | bytes 26264576 | tf_op jit(solution)/shard_map/lap,lph->lah/dot_general | solution.py:297
  520.5 38.1 %fusion.45 = bf16[20,256,256]{2,1,0:T(8,128)(2,1)} fusion(f32[20,256,256]{2,1,0:T(8,128)} %fusion.39, f32[20,256,768]{2,1,0:T(8,128)} %copy-done.5, f32[256]{0:T(256)S(1)} %copy-done.109, f32[20,256,256]{2,1,0:T(8,128)} %get-tuple-element.217, f32[20,256]{1,0:T(8,128)S(1)} %get-tuple-element.216), kind=kOutput, calls=%fused_computation.178 | convolution fusion | flops 684201216 | bytes 28886016 | tf_op jit(solution)/shard_map/fep,fet->fpt/dot_general | solution.py:300
  558.7 16.9 %fusion.228 = (f32[256]{0:T(256)}, bf16[20,256,256]{2,1,0:T(8,128)(2,1)}) fusion(bf16[20,256,256]{2,1,0:T(8,128)(2,1)} %copy-done.21, f32[20,256]{1,0:T(8,128)S(1)} %get-tuple-element.216, f32[20,256,256]{2,1,0:T(8,128)} %broadcast_multiply_fusion), kind=kOutput, calls=%fused_computation.622 | convolution fusion | flops 677647360 | bytes 10507264 | tf_op jit(solution)/shard_map/fep,fet->fpt/dot_general | solution.py:292
  590.1 14.7 %convolution_bitcast_fusion = f32[3456,12]{0,1:T(8,128)} fusion(bf16[20,256,3456]{2,1,0:T(8,128)(2,1)} %constant_dynamic-update-slice_fusion.18, bf16[20,256,12]{1,2,0:T(8,128)(2,1)S(1)} %reshape.454), kind=kOutput, calls=%fused_computation.106 | convolution fusion | flops 424673280 | bytes 35678208 | tf_op jit(solution)/shard_map/bpk,bpn->kn/dot_general | solution.py:147
  620.4 20.3 %fusion.242 = f32[20,16,16,9,256]{4,2,3,1,0:T(8,128)} fusion(bf16[20,16,16,256,1]{3,2,4,1,0:T(8,128)(2,1)S(1)} %bitcast.649, bf16[9,256,256,1,1]{2,1,0,4,3:T(8,128)(2,1)} %bitcast.686), kind=kOutput, calls=%fused_computation.634 | convolution fusion | flops 6039797760 | bytes 50987008 | tf_op jit(solution)/shard_map/bpn,kn->bpk/dot_general | solution.py:143
  640.7 31.6 %slice_bitcast_fusion.17 = (f32[20,16,16,256]{3,2,1,0:T(8,128)}, f32[20,16,16,256]{3,2,1,0:T(8,128)}, f32[20,16,16,256]{3,2,1,0:T(8,128)}, f32[20,16,16,256]{3,2...) fusion(f32[20,16,16,9,256]{4,2,3,1,0:T(8,128)} %fusion.242), kind=kLoop, calls=%fused_computation.65 | loop fusion | bytes 94371840 | tf_op jit(solution)/shard_map/squeeze | solution.py:131
  672.3 9.0 pad_add_fusion.1
  681.3 16.7 %pad_add_fusion.8 = f32[20,16,16,256]{3,2,1,0:T(8,128)} fusion(f32[20,16,16,256]{3,2,1,0:T(8,128)} %get-tuple-element.134, f32[20,16,16,256]{3,2,1,0:T(8,128)} %get-tuple-element.135, f32[20,16,16,256]{3,2,1,0:T(8,128)} %get-tuple-element.128, f32[20,16,16,256]{3,2,1,0:T(8,128)} %get-tuple-element.129, f32[20,16,16,256]{3,2,1,0:T(8,128)} %get-tuple-element.130, ...), kind=kLoop, calls=%fused_computation.51 | loop fusion | flops 7864320 | bytes 41943040 | tf_op jit(solution)/shard_map/add | solution.py:134
  714.8 30.7 %copy.260 = bf16[2304,20,256]{2,0,1:T(8,128)(2,1)} copy(bf16[2304,20,256]{0,2,1:T(8,128)(2,1)} %bitcast.105) | data formatting | bytes 47185920 | tf_op jit(solution)/shard_map/bpk,bpn->kn/dot_general | solution.py:147
  756.5 9.8 fusion.243
  766.3 14.8 %slice_bitcast_fusion.26 = (f32[20,16,16,128]{3,2,1,0:T(8,128)S(1)}, f32[20,16,16,128]{3,2,1,0:T(8,128)}, f32[20,16,16,128]{3,2,1,0:T(8,128)}, f32[20,16,16,128]...) fusion(f32[20,16,16,9,128]{4,2,3,1,0:T(8,128)} %fusion.243), kind=kLoop, calls=%fused_computation.149 | loop fusion | bytes 47185920 | tf_op jit(solution)/shard_map/squeeze | solution.py:131
  806.9 12.5 bitcast_dynamic-update-slice_fusion
  832.1 42.3 %all-reduce.31 = (f32[]{:T(128)}, f32[27,128]{1,0:T(8,128)S(1)}, f32[2956]{0:T(1024)S(1)}) all-reduce(f32[]{:T(128)} %get-tuple-element.168, f32[27,128]{1,0:T(8,128)S(1)} %convolution_bitcast_fusion.1, f32[2956]{0:T(1024)S(1)} %constant_dynamic-update-slice_fusion.47), channel_id=1, replica_groups=mesh['bucket'=4,'batch'=8] {'bucket','batch'}, use_global_device_ids=true, to_apply=%region_16.17 | all-reduce | flops 6413 | bytes 51304 | tf_op jit(solution)/shard_map/psum | solution.py:368
  877.4 97.7 %all-reduce.46.cloned.1.call-done = (f32[5120,256]{1,0:T(8,128)}, f32[3456,12]{0,1:T(8,128)}) async-done(((f32[5120,256]{1,0:T(8,128)}, f32[3456,12]{0,1:T(8,128)}), (f32[5120,256]{1,0:T(8,128)}, f32[3456,12]{0,1:T(8,128)})) %all-reduce.46.cloned.1.call-update) | async-done | bytes 5408784 | tf_op jit(solution)/shard_map/psum | solution.py:348
  988.2 10.4 all-reduce.33
  1015.3 51.5 %all-reduce.56.cloned.1.call-done = (bf16[256,256]{1,0:T(8,128)(2,1)}, bf16[256,256]{1,0:T(8,128)(2,1)}, bf16[256,256]{1,0:T(8,128)(2,1)}, bf16[256,256]{1,0:T(8...) async-done(((bf16[256,256]{1,0:T(8,128)(2,1)}, bf16[256,256]{1,0:T(8,128)(2,1)}, ...) | async-done | bytes 1048592 | tf_op jit(solution)/shard_map/psum | solution.py:172
  1089.8 50.2 %all-reduce.54.cloned.1.call-done = (bf16[256,256]{1,0:T(8,128)(2,1)}, bf16[256,256]{1,0:T(8,128)(2,1)}, bf16[256,256]{1,0:T(8,128)(2,1)}, bf16[256,256]{1,0:T(8...) async-done(((bf16[256,256]{1,0:T(8,128)(2,1)}, bf16[256,256]{1,0:T(8,128)(2,1)}, ...) | async-done | bytes 1048592 | tf_op jit(solution)/shard_map/psum | solution.py:172
  1161.1 52.0 %all-reduce.52.cloned.1.call-done = (bf16[256,256]{1,0:T(8,128)(2,1)}, bf16[256,256]{1,0:T(8,128)(2,1)}, bf16[256,256]{1,0:T(8,128)(2,1)}, bf16[256,256]{1,0:T(8...) async-done(((bf16[256,256]{1,0:T(8,128)(2,1)}, bf16[256,256]{1,0:T(8,128)(2,1)}, ...) | async-done | bytes 1048592 | tf_op jit(solution)/shard_map/psum | solution.py:172
  1234.6 51.7 %all-reduce.50.cloned.1.call-done = (bf16[256,256]{1,0:T(8,128)(2,1)}, bf16[256,256]{1,0:T(8,128)(2,1)}, bf16[256,256]{1,0:T(8,128)(2,1)}, bf16[256,256]{1,0:T(8...) async-done(((bf16[256,256]{1,0:T(8,128)(2,1)}, bf16[256,256]{1,0:T(8,128)(2,1)}, ...) | async-done | bytes 1048592 | tf_op jit(solution)/shard_map/psum | solution.py:172
  1308.9 50.7 %all-reduce.48.cloned.1.call-done = (bf16[256,256]{1,0:T(8,128)(2,1)}, bf16[256,256]{1,0:T(8,128)(2,1)}, bf16[256,256]{1,0:T(8,128)(2,1)}, bf16[256,256]{1,0:T(8...) async-done(((bf16[256,256]{1,0:T(8,128)(2,1)}, bf16[256,256]{1,0:T(8,128)(2,1)}, ...) | async-done | bytes 1048592 | tf_op jit(solution)/shard_map/psum | solution.py:172
  (637 shorter events, 441.7 us)
Async XLA Ops:
  7.2 128.8 %all-gather.2.cloned.1.call-start = ((), (), s32[]{:S(2)}) async-start(), calls=%async_computation | async-start | bytes 3276800 | tf_op jit(solution)/shard_map/all_gather | solution.py:198
  9.5 965.7 %all-reduce.46.cloned.1.call-start = ((), (), s32[]{:S(2)}) async-start(), calls=%async_computation.1 | async-start | bytes 10928128 | tf_op jit(solution)/shard_map/psum | solution.py:348
  10.3 97.6 %copy-start.98 = (f32[128]{0:T(128)}, f32[128]{0:T(128)S(1)}, u32[]{:S(2)}) copy-start(f32[128]{0:T(128)S(1)} %get-tuple-element.205) | copy-start | bytes 1540
  10.3 97.6 %copy-start.105 = (f32[128]{0:T(128)}, f32[128]{0:T(128)S(1)}, u32[]{:S(2)}) copy-start(f32[128]{0:T(128)S(1)} %get-tuple-element.206) | copy-start | bytes 1540
  51.1 47.8 %copy-start = (f32[20,16,16,128]{3,2,1,0:T(8,128)}, f32[20,16,16,128]{3,2,1,0:T(8,128)S(1)}, u32[]{:S(2)}) copy-start(f32[20,16,16,128]{3,2,1,0:T(8,128)S(1)} %reduce_sum.516) | copy-start | bytes 7864324
  51.1 45.6 %copy-start.38 = (f32[3456,12]{0,1:T(8,128)S(1)}, f32[3456,12]{0,1:T(8,128)}, u32[]{:S(2)}) copy-start(f32[3456,12]{0,1:T(8,128)} %param.21) | copy-start | bytes 497668
  51.1 45.7 %copy-start.66 = (s32[20,1024]{1,0:T(8,128)S(1)}, s32[20,1024]{1,0:T(8,128)}, u32[]{:S(2)}) copy-start(s32[20,1024]{1,0:T(8,128)} %param.14) | copy-start | bytes 245764
  51.6 56.4 %copy-start.64 = (f32[20,128]{1,0:T(8,128)}, f32[20,128]{1,0:T(8,128)S(1)}, u32[]{:S(2)}) copy-start(f32[20,128]{1,0:T(8,128)S(1)} %copy.209) | copy-start | bytes 30724
  54.2 42.7 %copy-start.75 = (f32[20,32]{0,1:T(8,128)}, f32[20,32]{0,1:T(8,128)S(1)}, u32[]{:S(2)}) copy-start(f32[20,32]{0,1:T(8,128)S(1)} %reduce_sum.522) | copy-start | bytes 7684
  135.7 48.4 %copy-start.91 = (f32[256]{0:T(256)}, f32[256]{0:T(256)S(1)}, u32[]{:S(2)}) copy-start(f32[256]{0:T(256)S(1)} %get-tuple-element.204) | copy-start | bytes 3076
  135.7 48.4 %copy-start.93 = (f32[256]{0:T(256)}, f32[256]{0:T(256)S(1)}, u32[]{:S(2)}) copy-start(f32[256]{0:T(256)S(1)} %get-tuple-element.202) | copy-start | bytes 3076
  135.7 48.4 %copy-start.96 = (f32[256]{0:T(256)}, f32[256]{0:T(256)S(1)}, u32[]{:S(2)}) copy-start(f32[256]{0:T(256)S(1)} %get-tuple-element.201) | copy-start | bytes 3076
  135.7 86.3 %copy-start.103 = (f32[256]{0:T(256)}, f32[256]{0:T(256)S(1)}, u32[]{:S(2)}) copy-start(f32[256]{0:T(256)S(1)} %get-tuple-element.199) | copy-start | bytes 3076
  141.5 65.0 %copy-start.71 = (bf16[4,32,256]{2,1,0:T(8,128)(2,1)}, bf16[4,32,256]{2,1,0:T(8,128)(2,1)S(1)}, u32[]{:S(2)}) copy-start(bf16[4,32,256]{2,1,0:T(8,128)(2,1)S(1)} %slice.461) | copy-start | bytes 196612
  143.4 110.5 %copy-start.32 = (bf16[4,64,256]{2,1,0:T(8,128)(2,1)}, bf16[4,64,256]{2,1,0:T(8,128)(2,1)S(1)}, u32[]{:S(2)}) copy-start(bf16[4,64,256]{2,1,0:T(8,128)(2,1)S(1)} %get-tuple-element.170) | copy-start | bytes 393220
  143.5 40.6 %copy-start.41 = (f32[20,256]{1,0:T(8,128)}, f32[20,256]{1,0:T(8,128)S(1)}, u32[]{:S(2)}) copy-start(f32[20,256]{1,0:T(8,128)S(1)} %convolution_add_fusion.46) | copy-start | bytes 61444
  158.7 25.5 %copy-start.39 = (f32[20,256]{1,0:T(8,128)}, f32[20,256]{1,0:T(8,128)S(1)}, u32[]{:S(2)}) copy-start(f32[20,256]{1,0:T(8,128)S(1)} %copy.215) | copy-start | bytes 61444
  258.8 38.6 %copy-start.3 = (f32[20,256,256]{2,1,0:T(8,128)}, f32[20,256,256]{2,1,0:T(8,128)S(1)}, u32[]{:S(2)}) copy-start(f32[20,256,256]{2,1,0:T(8,128)S(1)} %add_add_fusion.3) | copy-start | bytes 15728644
  485.0 35.6 %copy-start.109 = (f32[256]{0:T(256)S(1)}, f32[256]{0:T(256)}, u32[]{:S(2)}) copy-start(f32[256]{0:T(256)} %get-tuple-element.197) | copy-start | bytes 3076
  558.7 24.2 %slice-start = ((s8[5242880]{0:T(1024)(128)(4,1)}), s8[1048576]{0:T(1024)(128)(4,1)S(1)}, s32[]{:S(2)}) async-start(s8[5242880]{0:T(1024)(128)(4,1)} %bitcast.627), calls=%async_computation.7 | async-start | bytes 2097152
  672.2 25.8 %slice-start.4 = ((s8[5242880]{0:T(1024)(128)(4,1)}), s8[4194304]{0:T(1024)(128)(4,1)S(1)}, s32[]{:S(2)}) async-start(s8[5242880]{0:T(1024)(128)(4,1)} %bitcast.631), calls=%async_computation.11 | async-start | bytes 8388608
  824.4 242.4 %all-reduce.56.cloned.1.call-start = ((), (), s32[]{:S(2)}) async-start(), calls=%async_computation.6 | async-start | bytes 2097152 | tf_op jit(solution)/shard_map/psum | solution.py:172
  825.7 48.7 %copy-start.95 = (f32[27,128]{1,0:T(8,128)S(1)}, f32[27,128]{1,0:T(8,128)}, u32[]{:S(2)}) copy-start(f32[27,128]{1,0:T(8,128)} %param.20) | copy-start | bytes 41476
  875.1 139.5 %copy-start.81 = (f32[27,128]{1,0:T(8,128)}, f32[27,128]{1,0:T(8,128)S(1)}, u32[]{:S(2)}) copy-start(f32[27,128]{1,0:T(8,128)S(1)} %get-tuple-element.88) | copy-start | bytes 41476
  988.2 26.7 %copy-start.86 = (f32[1280,256]{1,0:T(8,128)}, f32[1280,256]{1,0:T(8,128)S(1)}, u32[]{:S(2)}) copy-start(f32[1280,256]{1,0:T(8,128)S(1)} %get-tuple-element.146) | copy-start | bytes 3932164
  1014.0 126.1 %all-reduce.54.cloned.1.call-start = ((), (), s32[]{:S(2)}) async-start(), calls=%async_computation.5 | async-start | bytes 2097152 | tf_op jit(solution)/shard_map/psum | solution.py:172
  1086.2 127.0 %all-reduce.52.cloned.1.call-start = ((), (), s32[]{:S(2)}) async-start(), calls=%async_computation.4 | async-start | bytes 2097152 | tf_op jit(solution)/shard_map/psum | solution.py:172
  1089.1 71.1 %copy-start.30 = (f32[3456,12]{0,1:T(8,128)}, f32[3456,12]{0,1:T(8,128)S(1)}, u32[]{:S(2)}) copy-start(f32[3456,12]{0,1:T(8,128)S(1)} %get-tuple-element.86) | copy-start | bytes 497668
  1159.3 127.1 %all-reduce.50.cloned.1.call-start = ((), (), s32[]{:S(2)}) async-start(), calls=%async_computation.3 | async-start | bytes 2097152 | tf_op jit(solution)/shard_map/psum | solution.py:172
  1231.0 68.5 %copy-start.50 = (f32[32,256]{1,0:T(8,128)S(1)}, f32[32,256]{1,0:T(8,128)}, u32[]{:S(2)}) copy-start(f32[32,256]{1,0:T(8,128)} %copy-done.49) | copy-start | bytes 98308
  1232.5 127.0 %all-reduce.48.cloned.1.call-start = ((), (), s32[]{:S(2)}) async-start(), calls=%async_computation.2 | async-start | bytes 2097152 | tf_op jit(solution)/shard_map/psum | solution.py:172
  1298.0 62.8 %copy-start.22 = (f32[1280,256]{1,0:T(8,128)S(1)}, f32[1280,256]{1,0:T(8,128)}, u32[]{:S(2)}) copy-start(f32[1280,256]{1,0:T(8,128)} %param.17) | copy-start | bytes 3932164
  (106 other events, 977.7 us)
Sparse Core Ops, SparseCore 0:
  10.2 57.5 all-gather.1
  824.5 150.6 all-reduce.45
  1014.1 52.6 all-reduce.55
  1086.3 53.6 all-reduce.53
  1159.4 53.6 all-reduce.51
  1232.7 53.6 all-reduce.49
  1305.9 53.6 all-reduce.47
where the time goes:
time: 1390 us; the launch traced here: 1380 us
  matrix products  384 us (28%)
  waiting for transfers between devices  354 us (25%)
  local copies, waits for them, and re-layouts  302 us (22%)
  other arithmetic  203 us (15%)
  blocking collectives  95.2 us (7%)
  between operations  24 us (2%)
  Pallas kernels  16.6 us (1%)
    psum x5, waiting for transfers between devices, grams(): lax.psum(for_sending(tuple((jnp.dot(piece.T, piece, precision=EXACT_PRECI...  256 us
    psum x1, waiting for transfers between devices, shards(): summed = lax.psum(grad_pack, ('bucket', 'batch'))  97.7 us
    squeeze x3, local copies, waits for them, and re-layouts, unpatch(): parts[:, :, :, shift_y * 3 + shift_x, :]  92.8 us
    dot_general x6, matrix products, back_mult(): jnp.einsum('bpn,kn->bpk', grad_out, right, preferred_element_type=jnp.flo...  70.2 us
    unnamed x309, local copies, waits for them, and re-layouts  67.4 us
    add x5, other arithmetic, unpatch(): total = placed if total is None else total + placed  66.6 us
    dot_general x7, matrix products, mult(): jnp.einsum('bpk,kn->bpn', left, right, preferred_element_type=jnp.float32)  56.4 us
    dot_general x7, matrix products, weight_grad(): jnp.einsum('bpk,bpn->kn', left, grad_out, preferred_element_type=jnp.floa...  50.6 us
  transfers between devices with their start and end apart: 7, of which 6 were waited for; matrix products, arithmetic and copies ran while one was open for 7% of the time, Pallas kernels for 0%

commit v1 on v0

--- a/solution.py
+++ b/solution.py
@@ -165,18 +165,19 @@
     return (weight_m * (1.0 - LR_MUON * DECAY) - LR_MUON * iterate, moment_new)
 
 
-def grams(pieces):
-    return list(
-        jax.tree.map(
-            lambda part: part.astype(jnp.float32),
-            lax.psum(
-                for_sending(
-                    tuple((jnp.dot(piece.T, piece, precision=EXACT_PRECISION) for piece in pieces))
-                ),
-                "bucket",
-            ),
+def ns_product(gram):
+    eye = jnp.eye(gram.shape[0], dtype=jnp.float32)
+    product = None
+    for step in range(NS_STEPS):
+        square = jnp.dot(gram, gram, precision=EXACT_PRECISION)
+        factor = NS_A * eye + NS_B * gram + NS_C * square
+        product = (
+            factor if product is None else jnp.dot(product, factor, precision=EXACT_PRECISION)
         )
-    )
+        if step < NS_STEPS - 1:
+            half = jnp.dot(gram, factor, precision=EXACT_PRECISION)
+            gram = jnp.dot(factor, half, precision=EXACT_PRECISION)
+    return product
 
 
 def shards(
@@ -220,7 +221,7 @@
     half_side = S // 2
     level, weight = plan(timesteps)
     counts = jnp.sum(pixel_mask.astype(jnp.float32), axis=1)
-    weight_sum = lax.psum(jnp.sum(3.0 * weight * counts), ("bucket", "batch"))
+    weight_local = jnp.sum(3.0 * weight * counts)
     noisy = (
         jnp.sqrt(level)[:, None, None] * images + jnp.sqrt(1.0 - level)[:, None, None] * noise_field
     )
@@ -271,7 +272,7 @@
     error = predicted - noise_field
     masked = pixel_mask.astype(jnp.float32)[:, None, :] * weight[:, None, None]
     loss_local = jnp.sum(masked * error * error)
-    grad_pred = 2.0 * masked * error / weight_sum
+    grad_pred = 2.0 * masked * error
     grad_head_out = (
         grad_pred.reshape(samples, 3, half_side, 2, half_side, 2)
         .transpose(0, 2, 4, 3, 5, 1)
@@ -344,9 +345,6 @@
         ],
         owners,
     )
-    rows_dev = matrices.shape[0]
-    summed = lax.psum(grad_pack, ("bucket", "batch"))
-    grad_mine = lax.dynamic_slice_in_dim(summed, lax.axis_index("bucket") * rows_dev, rows_dev, 0)
     grad_vec = jnp.concatenate(
         [
             g_stem_b,
@@ -365,9 +363,16 @@
             g_head_b,
         ]
     )
-    grad_stem, grad_headw, grad_vec, loss_sum = lax.psum(
-        (g_stem, g_head, grad_vec, loss_local), ("bucket", "batch")
-    )
+    rows_dev = matrices.shape[0]
+    summed, grad_stem, grad_headw, grad_vec, loss_sum, weight_sum = lax.psum(
+        (grad_pack, g_stem, g_head, grad_vec, loss_local, weight_local), ("bucket", "batch")
+    )
+    inverse = 1.0 / weight_sum
+    summed = summed * inverse
+    grad_stem = grad_stem * inverse
+    grad_headw = grad_headw * inverse
+    grad_vec = grad_vec * inverse
+    grad_mine = lax.dynamic_slice_in_dim(summed, lax.axis_index("bucket") * rows_dev, rows_dev, 0)
     shares = [seg_rows // owners for seg_rows in segment_rows()]
     weight_parts, moment_parts, grad_parts = ([], [], [])
     start = 0
@@ -380,17 +385,15 @@
         MOMENTUM * moment + gradient for moment, gradient in zip(moment_parts, grad_parts)
     ]
     directions = [gradient + MOMENTUM * moment for gradient, moment in zip(grad_parts, moments_new)]
-    squares = lax.psum(
-        tuple((jnp.sum(direction * direction) for direction in directions)), "bucket"
-    )
-    iterates = [
-        direction * lax.rsqrt(square + NORM_EPS) for direction, square in zip(directions, squares)
-    ]
-    gram_now = grams(iterates)
-    for step in range(NS_STEPS):
-        if step > 0:
-            gram_now = grams(iterates)
-        iterates = [ns_update(iterate, gram) for iterate, gram in zip(iterates, gram_now)]
+    gram_sums = lax.psum(
+        tuple(jnp.dot(d.T, d, precision=EXACT_PRECISION) for d in directions), "bucket"
+    )
+    iterates = []
+    for direction, gram in zip(directions, gram_sums):
+        scale = lax.rsqrt(jnp.trace(gram) + NORM_EPS)
+        iterates.append(
+            jnp.dot(direction * scale, ns_product(gram * (scale * scale)), precision=EXACT_PRECISION)
+        )
     new_matrices = jnp.concatenate(
         [
             weight_m * (1.0 - LR_MUON * DECAY) - LR_MUON * iterate

time: 1390 us -> 1200 us (0.86)
  waiting for transfers between devices: 354 us -> 228 us
  blocking collectives: 95.2 us -> 42.9 us
  matrix products: 384 us -> 370 us
    psum x6 -> x2, waiting for transfers between devices: 354 us -> 228 us  [the longest x1 145 us: shards(): lax.psum((grad_pack, g_stem, g_head, grad_vec, loss_local, weight_local),...]
    psum x3 -> x1, blocking collectives: 95.2 us -> 42.9 us  [shards(): lax.psum((grad_pack, g_stem, g_head, grad_vec, loss_local, weight_local),...]
    dot_general x40 -> x152, matrix products: 49 us -> 88.3 us  [the longest x40 22.5 us: ns_product(): square = jnp.dot(gram, gram, precision=EXACT_PRECISION)]
    dot_general x50 -> x10, matrix products: 38.9 us -> 1.7 us  [ns_update(): inner = NS_B * gram + NS_C * jnp.dot(gram, gram, precision=EXACT_PRECISION)]
    unnamed x309 -> x331, local copies, waits for them, and re-layouts: 67.4 us -> 68.6 us
  transfers between devices with their start and end apart: 7 -> 3, of which waited for: 6 -> 2; matrix products, arithmetic and copies ran while one was open for 7% -> 8% of each run, Pallas kernels for 0% -> 0%
where the time goes in v1:
time: 1200 us; the launch traced here: 1190 us
  matrix products  370 us (31%)
  local copies, waits for them, and re-layouts  301 us (25%)
  waiting for transfers between devices  228 us (19%)
  other arithmetic  205 us (17%)
  blocking collectives  42.9 us (4%)
  between operations  24.7 us (2%)
  Pallas kernels  16.6 us (1%)
    psum x1, waiting for transfers between devices, shards(): lax.psum((grad_pack, g_stem, g_head, grad_vec, loss_local, weight_local),...  145 us
    squeeze x3, local copies, waits for them, and re-layouts, unpatch(): parts[:, :, :, shift_y * 3 + shift_x, :]  92.3 us
    psum x1, waiting for transfers between devices, shards(): lax.psum(tuple((jnp.dot(d.T, d, precision=EXACT_PRECISION) for d in direc...  82.7 us
    dot_general x6, matrix products, back_mult(): jnp.einsum('bpn,kn->bpk', grad_out, right, preferred_element_type=jnp.flo...  69.3 us
    unnamed x331, local copies, waits for them, and re-layouts  68.6 us
    add x5, other arithmetic, unpatch(): total = placed if total is None else total + placed  66.6 us
    dot_general x7, matrix products, mult(): jnp.einsum('bpk,kn->bpn', left, right, preferred_element_type=jnp.float32)  56.4 us
    dot_general x7, matrix products, weight_grad(): jnp.einsum('bpk,bpn->kn', left, grad_out, preferred_element_type=jnp.floa...  50.2 us
  transfers between devices with their start and end apart: 3, of which 2 were waited for; matrix products, arithmetic and copies ran while one was open for 8% of the time, Pallas kernels for 0%

profile of v1, /device:TPU:0, one launch (start us, length us, event | category | flops | bytes accessed | tf_op | source)
XLA Modules:
  0.0 1189.3 jit_solution(14531191042476011920)
XLA Ops:
  40.2 11.6 reduce_sum.496
  78.6 16.7 %copy.226 = bf16[1152,20,256]{2,0,1:T(8,128)(2,1)} copy(bf16[1152,20,256]{0,2,1:T(8,128)(2,1)} %bitcast.60) | data formatting | bytes 23592960 | tf_op jit(solution)/shard_map/bpk,bpn->kn/dot_general | solution.py:147
  103.9 11.0 fusion.9
  154.8 11.6 fusion.280
  199.0 16.6 %online-softmax = f32[20,256,256]{2,1,0:T(8,128)} custom-call(f32[20,256,256]{2,1,0:T(8,128)} %copy-done.6, f32[20,256,256]{2,1,0:T(8,128)} %slice_add_fusion), custom_call_target="tpu_custom_call" | custom-call | tf_op online-softmax
  224.3 21.8 %pad_slice_fusion = (bf16[20,16,16,384]{3,2,1,0:T(8,128)(2,1)S(1)}, bf16[20,16,16,384]{3,2,1,0:T(8,128)(2,1)}, bf16[20,16,16,384]{3,2,1,0:T(8,128)(2,1)}, bf16[2...) fusion(bf16[20,16,16,384]{3,2,1,0:T(8,128)(2,1)} %multiply_conv, ...), kind=kLoop, calls=%fused_computation.4 | loop fusion | bytes 35389440 | tf_op jit(solution)/shard_map/slice | solution.py:117
  273.9 15.8 %convolution_add_fusion.5 = f32[20,256,12]{1,2,0:T(8,128)S(1)} fusion(bf16[20,256,3456]{2,1,0:T(8,128)(2,1)} %constant_dynamic-update-slice_fusion.18, f32[12]{0:T(128)S(1)} %copy-done.126, bf16[3456,12]{0,1:T(8,128)(2,1)S(1)} %copy-done.61), kind=kOutput, calls=%fused_computation.239 | convolution fusion | flops 424734720 | bytes 35718192 | tf_op jit(solution)/shard_map/bpk,kn->bpn/dot_general | solution.py:139
  313.9 27.0 %fusion.198 = f32[20,16,16,9,384]{4,2,3,1,0:T(8,128)} fusion(bf16[20,16,16,12,1]{3,2,4,1,0:T(8,128)(2,1)} %copy.281, bf16[9,384,12,1,1]{1,0,2,4,3:T(8,128)(2,1)S(1)} %bitcast.748), kind=kOutput, calls=%fused_computation.505 | convolution fusion | flops 424673280 | bytes 70984704 | tf_op jit(solution)/shard_map/bpn,kn->bpk/dot_general | solution.py:143
  340.9 46.0 %slice_bitcast_fusion.8 = (f32[20,16,16,384]{3,2,1,0:T(8,128)}, f32[20,16,16,384]{3,2,1,0:T(8,128)}, f32[20,16,16,384]{3,2,1,0:T(8,128)}, f32[20,16,16,384]{3,2,...) fusion(f32[20,16,16,9,384]{4,2,3,1,0:T(8,128)} %fusion.198), kind=kLoop, calls=%fused_computation.29 | loop fusion | bytes 141557760 | tf_op jit(solution)/shard_map/squeeze | solution.py:131
  386.9 14.5 %pad_add_fusion = f32[20,18,18,384]{3,2,1,0:T(8,128)} fusion(f32[20,16,16,384]{3,2,1,0:T(8,128)} %get-tuple-element.70, f32[20,16,16,384]{3,2,1,0:T(8,128)} %get-tuple-element.71, f32[20,16,16,384]{3,2,1,0:T(8,128)} %get-tuple-element.65), kind=kLoop, calls=%fused_computation.2 | loop fusion | flops 4976640 | bytes 33546240 | tf_op jit(solution)/shard_map/add | solution.py:134
  401.4 23.3 %pad_add_fusion.2 = f32[20,16,16,384]{3,2,1,0:T(8,128)} fusion(f32[20,16,16,384]{3,2,1,0:T(8,128)} %get-tuple-element.72, f32[20,16,16,384]{3,2,1,0:T(8,128)} %get-tuple-element.73, f32[20,16,16,384]{3,2,1,0:T(8,128)} %get-tuple-element.66, f32[20,16,16,384]{3,2,1,0:T(8,128)} %get-tuple-element.67, f32[20,16,16,384]{3,2,1,0:T(8,128)} %get-tuple-element.68, ...), kind=kLoop, calls=%fused_computation.15 | loop fusion | flops 11796480 | bytes 62914560 | tf_op jit(solution)/shard_map/add | solution.py:134
  444.8 15.7 %fusion.267 = (f32[256]{0:T(256)}, bf16[20,256,256]{2,1,0:T(8,128)(2,1)}) fusion(bf16[20,256,256]{2,1,0:T(8,128)(2,1)S(1)} %convolution_convert_fusion, f32[20,256]{1,0:T(8,128)S(1)} %copy-done.105, f32[20,256,256]{2,1,0:T(8,128)} %copy-done.6), kind=kOutput, calls=%fused_computation.632 | convolution fusion | flops 677647360 | bytes 10507264 | tf_op jit(solution)/shard_map/fep,fet->fpt/dot_general | solution.py:293
  460.4 38.0 %fusion.45 = bf16[20,256,256]{2,1,0:T(8,128)(2,1)} fusion(f32[20,256,256]{2,1,0:T(8,128)} %fusion.39, f32[20,256,768]{2,1,0:T(8,128)} %copy-done.5, f32[256]{0:T(256)S(1)} %copy-done.122, f32[20,256,256]{2,1,0:T(8,128)} %get-tuple-element.156, f32[20,256]{1,0:T(8,128)S(1)} %copy-done.105), kind=kOutput, calls=%fused_computation.218 | convolution fusion | flops 684201216 | bytes 28886016 | tf_op jit(solution)/shard_map/fep,fet->fpt/dot_general | solution.py:301
  498.5 35.8 %fusion.268 = (f32[256]{0:T(256)}, bf16[20,256,256]{2,1,0:T(8,128)(2,1)}) fusion(f32[20,256,768]{2,1,0:T(8,128)} %copy-done.5, f32[20,256,256]{2,1,0:T(8,128)} %fusion.39, f32[20,256,256]{2,1,0:T(8,128)} %get-tuple-element.156, f32[20,256]{1,0:T(8,128)S(1)} %copy-done.105), kind=kOutput, calls=%fused_computation.633 | convolution fusion | flops 682890240 | bytes 26264576 | tf_op jit(solution)/shard_map/lap,lph->lah/dot_general | solution.py:298
  534.3 7.2 fusion.63
  547.8 30.7 %copy.260 = bf16[2304,20,256]{2,0,1:T(8,128)(2,1)} copy(bf16[2304,20,256]{0,2,1:T(8,128)(2,1)} %bitcast.105) | data formatting | bytes 47185920 | tf_op jit(solution)/shard_map/bpk,bpn->kn/dot_general | solution.py:147
  580.1 14.3 %convolution_bitcast_fusion = f32[3456,12]{0,1:T(8,128)} fusion(bf16[20,256,3456]{2,1,0:T(8,128)(2,1)} %constant_dynamic-update-slice_fusion.18, bf16[20,256,12]{1,2,0:T(8,128)(2,1)S(1)} %reshape.454), kind=kOutput, calls=%fused_computation.106 | convolution fusion | flops 424673280 | bytes 35678208 | tf_op jit(solution)/shard_map/bpk,bpn->kn/dot_general | solution.py:147
  595.5 8.3 fusion.265
  609.4 20.4 %fusion.281 = f32[20,16,16,9,256]{4,2,3,1,0:T(8,128)} fusion(bf16[20,16,16,256,1]{3,2,4,1,0:T(8,128)(2,1)S(1)} %bitcast.687, bf16[9,256,256,1,1]{2,1,0,4,3:T(8,128)(2,1)} %bitcast.724), kind=kOutput, calls=%fused_computation.644 | convolution fusion | flops 6039797760 | bytes 50987008 | tf_op jit(solution)/shard_map/bpn,kn->bpk/dot_general | solution.py:143
  629.8 31.4 %slice_bitcast_fusion.17 = (f32[20,16,16,256]{3,2,1,0:T(8,128)}, f32[20,16,16,256]{3,2,1,0:T(8,128)}, f32[20,16,16,256]{3,2,1,0:T(8,128)}, f32[20,16,16,256]{3,2...) fusion(f32[20,16,16,9,256]{4,2,3,1,0:T(8,128)} %fusion.281), kind=kLoop, calls=%fused_computation.65 | loop fusion | bytes 94371840 | tf_op jit(solution)/shard_map/squeeze | solution.py:131
  661.2 9.1 pad_add_fusion.1
  670.4 16.7 %pad_add_fusion.8 = f32[20,16,16,256]{3,2,1,0:T(8,128)} fusion(f32[20,16,16,256]{3,2,1,0:T(8,128)} %get-tuple-element.81, f32[20,16,16,256]{3,2,1,0:T(8,128)} %get-tuple-element.82, f32[20,16,16,256]{3,2,1,0:T(8,128)} %get-tuple-element.75, f32[20,16,16,256]{3,2,1,0:T(8,128)} %get-tuple-element.76, f32[20,16,16,256]{3,2,1,0:T(8,128)} %get-tuple-element.77, ...), kind=kLoop, calls=%fused_computation.51 | loop fusion | flops 7864320 | bytes 41943040 | tf_op jit(solution)/shard_map/add | solution.py:134
  687.2 7.5 multiply_reduce_fusion.1
  695.0 8.6 fusion.263
  707.8 7.2 fusion.56
  715.0 9.7 fusion.370
  724.8 14.9 %slice_bitcast_fusion.26 = (f32[20,16,16,128]{3,2,1,0:T(8,128)S(1)}, f32[20,16,16,128]{3,2,1,0:T(8,128)}, f32[20,16,16,128]{3,2,1,0:T(8,128)}, f32[20,16,16,128]...) fusion(f32[20,16,16,9,128]{4,2,3,1,0:T(8,128)} %fusion.370), kind=kLoop, calls=%fused_computation.189 | loop fusion | bytes 47185920 | tf_op jit(solution)/shard_map/squeeze | solution.py:131
  744.5 7.1 multiply_reduce_fusion.8
  768.7 42.9 %all-reduce.31 = (f32[]{:T(128)}, f32[]{:T(128)}, f32[27,128]{1,0:T(8,128)S(1)}, f32[2956]{0:T(1024)S(1)}) all-reduce(f32[]{:T(128)} %get-tuple-element.107, f32[]{:T(128)} %get-tuple-element.62, f32[27,128]{1,0:T(8,128)S(1)} %convolution_bitcast_fusion.1, ...), channel_id=1, replica_groups=mesh['bucket'=4,'batch'=8] {'bucket','batch'}, use_global_device_ids=true, to_apply=%region_16.17 | all-reduce | flops 6414 | bytes 51312 | tf_op jit(solution)/shard_map/psum | solution.py:367
  815.3 12.4 %bitcast_dynamic-update-slice_fusion = f32[4,1280,256]{2,1,0:T(8,128)} fusion(f32[4,1280,256]{2,1,0:T(8,128)} %fusion.56, bf16[4,576,20,256]{3,1,0,2:T(8,128)(2,1)} %bitcast.688, bf16[20,256,256]{2,1,0:T(8,128)(2,1)S(1)} %copy-done.8), kind=kOutput, calls=%fused_computation.217 | convolution fusion | flops 6039797760 | bytes 28573696 | tf_op jit(solution)/shard_map/bpk,bpn->kn/dot_general | solution.py:147
  837.0 145.3 %all-reduce.37.cloned.1.call-done = (f32[5120,256]{1,0:T(8,128)}, f32[3456,12]{0,1:T(8,128)}) async-done(((f32[5120,256]{1,0:T(8,128)}, f32[3456,12]{0,1:T(8,128)}), (f32[5120,256]{1,0:T(8,128)}, f32[3456,12]{0,1:T(8,128)})) %all-reduce.37.cloned.1.call-update) | async-done | bytes 5408784 | tf_op jit(solution)/shard_map/psum | solution.py:367
  1007.9 82.7 %all-reduce.39.cloned.1.call-done = (f32[256,256]{1,0:T(8,128)}, f32[256,256]{1,0:T(8,128)}, f32[256,256]{1,0:T(8,128)}, f32[256,256]{1,0:T(8,128)}, f32[256,256...) async-done(((f32[256,256]{1,0:T(8,128)}, f32[256,256]{1,0:T(8,128)}, f32[256,256]{1,0:T(8,128)}, f32[256,256]{1,0:T(8,128)}, ...) | async-done | bytes 2097168 | tf_op jit(solution)/shard_map/psum | solution.py:388
  (681 shorter events, 382.9 us)
Async XLA Ops:
  7.2 88.9 %all-gather.2.cloned.1.call-start = ((), (), s32[]{:S(2)}) async-start(), calls=%async_computation | async-start | bytes 3276800 | tf_op jit(solution)/shard_map/all_gather | solution.py:199
  9.5 972.8 %all-reduce.37.cloned.1.call-start = ((), (), s32[]{:S(2)}) async-start(), calls=%async_computation.1 | async-start | bytes 10928128 | tf_op jit(solution)/shard_map/psum | solution.py:367
  11.6 59.8 %copy-start.109 = (f32[128]{0:T(128)}, f32[128]{0:T(128)S(1)}, u32[]{:S(2)}) copy-start(f32[128]{0:T(128)S(1)} %get-tuple-element.144) | copy-start | bytes 1540
  11.6 59.8 %copy-start.117 = (f32[128]{0:T(128)}, f32[128]{0:T(128)S(1)}, u32[]{:S(2)}) copy-start(f32[128]{0:T(128)S(1)} %get-tuple-element.145) | copy-start | bytes 1540
  52.2 19.2 %copy-start.74 = (f32[20,128]{1,0:T(8,128)}, f32[20,128]{1,0:T(8,128)S(1)}, u32[]{:S(2)}) copy-start(f32[20,128]{1,0:T(8,128)S(1)} %copy.209) | copy-start | bytes 30724
  95.9 48.1 %copy-start.101 = (f32[256]{0:T(256)}, f32[256]{0:T(256)S(1)}, u32[]{:S(2)}) copy-start(f32[256]{0:T(256)S(1)} %get-tuple-element.143) | copy-start | bytes 3076
  95.9 48.1 %copy-start.103 = (f32[256]{0:T(256)}, f32[256]{0:T(256)S(1)}, u32[]{:S(2)}) copy-start(f32[256]{0:T(256)S(1)} %get-tuple-element.141) | copy-start | bytes 3076
  96.1 18.8 %copy-start.93 = (f32[20,256]{1,0:T(8,128)}, f32[20,256]{1,0:T(8,128)S(1)}, u32[]{:S(2)}) copy-start(f32[20,256]{1,0:T(8,128)S(1)} %get-tuple-element.147) | copy-start | bytes 61444
  96.1 18.8 %copy-start.95 = (f32[20,256]{1,0:T(8,128)}, f32[20,256]{1,0:T(8,128)S(1)}, u32[]{:S(2)}) copy-start(f32[20,256]{1,0:T(8,128)S(1)} %get-tuple-element.148) | copy-start | bytes 61444
  97.0 69.4 %copy-start.82 = (bf16[4,32,256]{2,1,0:T(8,128)(2,1)}, bf16[4,32,256]{2,1,0:T(8,128)(2,1)S(1)}, u32[]{:S(2)}) copy-start(bf16[4,32,256]{2,1,0:T(8,128)(2,1)S(1)} %slice.461) | copy-start | bytes 196612
  99.9 80.1 %copy-start.69 = (bf16[4,64,256]{2,1,0:T(8,128)(2,1)}, bf16[4,64,256]{2,1,0:T(8,128)(2,1)S(1)}, u32[]{:S(2)}) copy-start(bf16[4,64,256]{2,1,0:T(8,128)(2,1)S(1)} %get-tuple-element.108) | copy-start | bytes 393220
  99.9 115.8 %copy-start.36 = (bf16[4,64,256]{2,1,0:T(8,128)(2,1)}, bf16[4,64,256]{2,1,0:T(8,128)(2,1)S(1)}, u32[]{:S(2)}) copy-start(bf16[4,64,256]{2,1,0:T(8,128)(2,1)S(1)} %get-tuple-element.109) | copy-start | bytes 393220
  103.8 40.2 %copy-start.65 = (f32[20,256]{1,0:T(8,128)}, f32[20,256]{1,0:T(8,128)S(1)}, u32[]{:S(2)}) copy-start(f32[20,256]{1,0:T(8,128)S(1)} %convolution_add_fusion.6) | copy-start | bytes 61444
  119.0 25.1 %copy-start.63 = (f32[20,256]{1,0:T(8,128)}, f32[20,256]{1,0:T(8,128)S(1)}, u32[]{:S(2)}) copy-start(f32[20,256]{1,0:T(8,128)S(1)} %copy.215) | copy-start | bytes 61444
  126.4 17.6 %copy-start.67 = (f32[20,256]{1,0:T(8,128)}, f32[20,256]{1,0:T(8,128)S(1)}, u32[]{:S(2)}) copy-start(f32[20,256]{1,0:T(8,128)S(1)} %copy.217) | copy-start | bytes 61444
  220.6 38.8 %copy-start.3 = (f32[20,256,256]{2,1,0:T(8,128)}, f32[20,256,256]{2,1,0:T(8,128)S(1)}, u32[]{:S(2)}) copy-start(f32[20,256,256]{2,1,0:T(8,128)S(1)} %add_add_fusion.3) | copy-start | bytes 15728644
  498.5 35.8 %copy-start.78 = (f32[20,256]{1,0:T(8,128)S(1)}, f32[20,256]{1,0:T(8,128)}, u32[]{:S(2)}) copy-start(f32[20,256]{1,0:T(8,128)} %copy-done.77) | copy-start | bytes 61444
  498.5 35.8 %copy-start.86 = (f32[20,256]{1,0:T(8,128)S(1)}, f32[20,256]{1,0:T(8,128)}, u32[]{:S(2)}) copy-start(f32[20,256]{1,0:T(8,128)} %copy-done.85) | copy-start | bytes 61444
  498.5 35.8 %copy-start.116 = (f32[256]{0:T(256)S(1)}, f32[256]{0:T(256)}, u32[]{:S(2)}) copy-start(f32[256]{0:T(256)} %get-tuple-element.138) | copy-start | bytes 3076
  498.5 35.8 %copy-start.120 = (f32[256]{0:T(256)S(1)}, f32[256]{0:T(256)}, u32[]{:S(2)}) copy-start(f32[256]{0:T(256)} %get-tuple-element.137) | copy-start | bytes 3076
  498.5 43.0 %slice-start = ((s8[5242880]{0:T(1024)(128)(4,1)}), s8[1048576]{0:T(1024)(128)(4,1)S(1)}, s32[]{:S(2)}) async-start(s8[5242880]{0:T(1024)(128)(4,1)} %bitcast.667), calls=%async_computation.3 | async-start | bytes 2097152
  547.8 30.7 %copy-start.111 = (f32[2,2,3]{1,0,2:T(2,128)S(1)}, f32[2,2,3]{1,0,2:T(2,128)}, u32[]{:S(2)}) copy-start(f32[2,2,3]{1,0,2:T(2,128)} %reduce_sum.561) | copy-start | bytes 148
  547.8 31.4 %copy-start.32 = (bf16[20,16,16,2,2,3]{2,1,5,4,3,0:T(8,128)(2,1)S(1)}, bf16[20,16,16,2,2,3]{2,1,5,4,3,0:T(8,128)(2,1)}, u32[]{:S(2)}) copy-start(bf16[20,16,16,2,2,3]{2,1,5,4,3,0:T(8,128)(2,1)} %copy.299) | copy-start | bytes 368644
  609.4 20.4 %copy-start.7 = (bf16[20,256,256]{2,1,0:T(8,128)(2,1)}, bf16[20,256,256]{2,1,0:T(8,128)(2,1)S(1)}, u32[]{:S(2)}) copy-start(bf16[20,256,256]{2,1,0:T(8,128)(2,1)S(1)} %get-tuple-element.92) | copy-start | bytes 7864324
  661.2 25.9 %slice-start.4 = ((s8[5242880]{0:T(1024)(128)(4,1)}), s8[4194304]{0:T(1024)(128)(4,1)S(1)}, s32[]{:S(2)}) async-start(s8[5242880]{0:T(1024)(128)(4,1)} %bitcast.671), calls=%async_computation.7 | async-start | bytes 8388608
  670.3 16.8 %copy-start.68 = (f32[20,256]{1,0:T(8,128)S(1)}, f32[20,256]{1,0:T(8,128)}, u32[]{:S(2)}) copy-start(f32[20,256]{1,0:T(8,128)} %copy-done.67) | copy-start | bytes 61444
  670.3 16.8 %copy-start.102 = (f32[256]{0:T(256)S(1)}, f32[256]{0:T(256)}, u32[]{:S(2)}) copy-start(f32[256]{0:T(256)} %copy-done.101) | copy-start | bytes 3076
  764.3 48.1 %copy-start.106 = (f32[27,128]{1,0:T(8,128)S(1)}, f32[27,128]{1,0:T(8,128)}, u32[]{:S(2)}) copy-start(f32[27,128]{1,0:T(8,128)} %param.20) | copy-start | bytes 41476
  764.3 51.0 %copy-start.8 = (bf16[20,256,256]{2,1,0:T(8,128)(2,1)S(1)}, bf16[20,256,256]{2,1,0:T(8,128)(2,1)}, u32[]{:S(2)}) copy-start(bf16[20,256,256]{2,1,0:T(8,128)(2,1)} %copy-done.7) | copy-start | bytes 7864324
  831.2 152.5 %copy-start.15 = (f32[1280,256]{1,0:T(8,128)S(1)}, f32[1280,256]{1,0:T(8,128)}, u32[]{:S(2)}) copy-start(f32[1280,256]{1,0:T(8,128)} %param.18) | copy-start | bytes 3932164
  832.8 161.9 %copy-start.84 = (f32[3456,12]{0,1:T(8,128)S(1)}, f32[3456,12]{0,1:T(8,128)}, u32[]{:S(2)}) copy-start(f32[3456,12]{0,1:T(8,128)} %param.22) | copy-start | bytes 497668
  832.8 257.8 %all-reduce.39.cloned.1.call-start = ((), (), s32[]{:S(2)}) async-start(), calls=%async_computation.2 | async-start | bytes 4194304 | tf_op jit(solution)/shard_map/psum | solution.py:388
  (113 other events, 773.8 us)
Sparse Core Ops, SparseCore 0:
  10.2 57.4 all-gather.1
  832.9 149.3 all-reduce.36
  1002.0 88.5 all-reduce.38

commit v2 on v1

v2 whole, which is shorter than its diff:
```python
import functools
import math

import jax
import jax.numpy as jnp
import numpy as np
from jax import lax
from jax.experimental import pallas as pl
from jax.experimental.pallas import tpu as pltpu
from jax.sharding import PartitionSpec as P

C1 = 128
CHANNELS_MID = 256
TEMB = 512
GROUPS = 32
S = 32
TSTEPS = 1000
NS_STEPS = 5
STEP = 10


GN_EPS = 1e-05
NORM_EPS = 1e-12
MOMENTUM = 0.95
LR_MUON = 0.5
DECAY = 0.01
NS_A = 3.4445
NS_B = -4.775
NS_C = 2.0315
BETA_ONE = 0.9
BETA_TWO = 0.999
LR_ADAM = 0.5
ADAM_EPS = 1e-08
EXACT_PRECISION = lax.Precision.HIGHEST
LOWTYPE = jnp.bfloat16


def segment_rows():
    return [
        9 * C1,
        9 * CHANNELS_MID,
        C1,
        TEMB,
        CHANNELS_MID,
        CHANNELS_MID,
        CHANNELS_MID,
        CHANNELS_MID,
    ]


def unpack(packed, owners):
    blocks = packed.reshape(owners, -1, packed.shape[1])
    pieces = []
    start = 0
    for seg_rows in segment_rows():
        share = seg_rows // owners
        pieces.append(blocks[:, start : start + share, :].reshape(seg_rows, packed.shape[1]))
        start += share
    return pieces


def pack(pieces, owners):
    blocks = [piece.reshape(owners, -1, piece.shape[1]) for piece in pieces]
    return jnp.concatenate(blocks, axis=1).reshape(-1, pieces[0].shape[1])


def plan(timesteps):
    frac_t = (timesteps.astype(jnp.float32) / TSTEPS + 0.008) / 1.008
    level = jnp.cos(frac_t * (math.pi / 2)) ** 2
    ratio = level / (1.0 - level)
    return (level, jnp.minimum(1.0, 5.0 / ratio))


def embed(timesteps):
    half_width = TEMB // 2
    freqs = jnp.exp(-math.log(10000.0) * jnp.arange(half_width, dtype=jnp.float32) / half_width)
    angles = timesteps.astype(jnp.float32)[:, None] * freqs[None, :]
    return jnp.concatenate([jnp.sin(angles), jnp.cos(angles)], axis=1)


def swish(values):
    return values * jax.nn.sigmoid(values)


F32 = jnp.float32
PLACES = 256
SIDE = 16
HALO = 288
TAPS = 9
ROWS12 = 16
CHUNK = 64
VMEM_BYTES = 56 * 1024 * 1024
SEG_OFF = (0, 1152, 3456, 3584, 4096, 4352, 4608, 4864, 5120)


def dot_nn(a, b, precision=None):
    return lax.dot_general(
        a, b, (((1,), (0,)), ((), ())), preferred_element_type=F32, precision=precision
    )


def dot_nt(a, b):
    return lax.dot_general(a, b, (((1,), (1,)), ((), ())), preferred_element_type=F32)


def dot_tn(a, b):
    return lax.dot_general(a, b, (((0,), (0,)), ((), ())), preferred_element_type=F32)


def sigmoid(v):
    return 1.0 / (1.0 + jnp.exp(-v))


def fold8(v):
    rows, chans = v.shape
    return jnp.sum(v.reshape(rows // 8, 8, chans), axis=0)


def shift_lanes(x, di, dj):
    lane = lax.broadcasted_iota(jnp.int32, x.shape, 1)
    row, col = lane // SIDE + di, lane % SIDE + dj
    offset = (-(SIDE * di + dj)) % PLACES
    moved = x if offset == 0 else pltpu.roll(x, offset, 1)
    valid = (row >= 0) & (row < SIDE) & (col >= 0) & (col < SIDE)
    return jnp.where(valid, moved, 0.0)


def tap_offsets():
    return [(di, dj) for di in (-1, 0, 1) for dj in (-1, 0, 1)]


def unet_body(
    group,
    steps,
    noisy_ref,
    noise_ref,
    maskw_ref,
    time_ref,
    stemw_ref,
    headw_ref,
    conv1_ref,
    conv1b_ref,
    conv2_ref,
    conv2b_ref,
    skip_ref,
    temb_ref,
    qkv_ref,
    outw_ref,
    vec_ref,
    headb_ref,
    same128_ref,
    same256_ref,
    acc_ref,
    gstem_ref,
    ghead_ref,
    gvec_ref,
    ghb_ref,
    loss_ref,
    x0,
    hid,
    res,
    outp,
    attn,
    a1,
    a2,
    normed,
    qkv,
    plow,
    attl,
    joined,
    patch,
    pad1,
    pad2,
    shiftf,
    dyf,
    dout,
    dq3,
    dpool,
    tproj,
    gtime,
):
    step = pl.program_id(0)
    mid = CHANNELS_MID
    chunks = range(0, PLACES, CHUNK)
    images = range(group)

    @pl.when(step == 0)
    def _():
        acc_ref[...] = jnp.zeros_like(acc_ref)
        gstem_ref[...] = jnp.zeros_like(gstem_ref)
        ghead_ref[...] = jnp.zeros_like(ghead_ref)
        gvec_ref[...] = jnp.zeros_like(gvec_ref)
        ghb_ref[...] = jnp.zeros_like(ghb_ref)
        loss_ref[...] = jnp.zeros_like(loss_ref)
        gtime[...] = jnp.zeros_like(gtime)
        for ref in (a1, a2, pad1, pad2):
            for g in images:
                ref[g, :SIDE, :] = jnp.zeros((SIDE, ref.shape[2]), ref.dtype)
                ref[g, HALO - SIDE :, :] = jnp.zeros((SIDE, ref.shape[2]), ref.dtype)
        shiftf[...] = jnp.zeros_like(shiftf)
        tproj[...] = dot_nn(time_ref[...], temb_ref[...])

    def vec(row, chans=mid):
        return vec_ref[row : row + 1, :chans]

    def add_vec(row, value):
        gvec_ref[row : row + 1, : value.shape[1]] += value

    def total(parts):
        return jnp.concatenate([jnp.sum(p, axis=0, keepdims=True) for p in parts], axis=0)

    def grouped(stats, chans):
        same = same128_ref if chans == C1 else same256_ref
        return dot_nn(stats, same[...], precision=EXACT_PRECISION)

    def gn_stats(ref, sums, chans):
        mean = grouped(sums, chans)
        parts = []
        for g in images:
            acc = jnp.zeros((8, chans), F32)
            for r in chunks:
                c = ref[g, r : r + CHUNK, :] - mean[g : g + 1]
                acc += fold8(c * c)
            parts.append(acc)
        return mean, lax.rsqrt(grouped(total(parts), chans) + GN_EPS)

    def edge(chans, left):
        col = lax.broadcasted_iota(jnp.int32, (CHUNK, chans), 0) % SIDE
        return (col > 0) if left else (col < SIDE - 1)

    def act_shift(ref, mean, rstd, gain, shift, dest, chans):
        for g in images:
            for r in chunks:
                y = (ref[g, r : r + CHUNK, :] - mean[g : g + 1]) * rstd[g : g + 1] * gain + shift
                a = y * sigmoid(y)
                shiftf[g, 8 + r : 8 + r + CHUNK, :chans] = a
                dest[g, SIDE + r : SIDE + r + CHUNK, chans : 2 * chans] = a.astype(LOWTYPE)
            for r in chunks:
                before = shiftf[g, 7 + r : 7 + r + CHUNK, :chans]
                after = shiftf[g, 9 + r : 9 + r + CHUNK, :chans]
                rows = slice(SIDE + r, SIDE + r + CHUNK)
                dest[g, rows, :chans] = jnp.where(edge(chans, True), before, 0.0).astype(LOWTYPE)
                dest[g, rows, 2 * chans :] = jnp.where(edge(chans, False), after, 0.0).astype(
                    LOWTYPE
                )

    def dy_cat(ref, g, order):
        return jnp.concatenate(
            [ref[g, SIDE * k : SIDE * k + PLACES, :] for k in order], axis=1
        )

    def stack(parts):
        return jnp.concatenate(parts, axis=0) if len(parts) > 1 else parts[0]

    for g in images:
        noisy = noisy_ref[g].astype(F32)
        for tap, (di, dj) in enumerate(tap_offsets()):
            patch[g, tap * ROWS12 : (tap + 1) * ROWS12, :] = shift_lanes(noisy, di, dj).astype(
                LOWTYPE
            )
    sums = []
    for g in images:
        wide = dot_tn(patch[g], stemw_ref[...])
        acc = jnp.zeros((8, C1), F32)
        for r in chunks:
            w = wide[r : r + CHUNK]
            v = (w[:, :C1] + w[:, C1 : 2 * C1]) + w[:, 2 * C1 :] + vec(0, C1)
            x0[g, r : r + CHUNK, :] = v
            acc += fold8(v)
        sums.append(acc)
    mean1, rstd1 = gn_stats(x0, total(sums), C1)
    gain1, shift1 = vec(1, C1), vec(2, C1)
    act_shift(x0, mean1, rstd1, gain1, shift1, a1, C1)

    wide = dot_nn(stack([dy_cat(a1, g, (0, 1, 2)) for g in images]), conv1_ref[...])
    sums = []
    for g in images:
        bias = vec(3) + vec(4) + tproj[pl.ds(step * group + g, 1), :]
        acc = jnp.zeros((8, mid), F32)
        for r in chunks:
            v = wide[g * PLACES + r : g * PLACES + r + CHUNK] + bias
            hid[g, r : r + CHUNK, :] = v
            acc += fold8(v)
        sums.append(acc)
    mean2, rstd2 = gn_stats(hid, total(sums), mid)
    gain2, shift2 = vec(5), vec(6)
    act_shift(hid, mean2, rstd2, gain2, shift2, a2, mid)

    wide = dot_nn(stack([dy_cat(a2, g, (0, 1, 2)) for g in images]), conv2_ref[...])
    low0 = stack([x0[g].astype(LOWTYPE) for g in images])
    wide = wide + dot_nn(low0, skip_ref[...])
    sums = []
    for g in images:
        acc = jnp.zeros((8, mid), F32)
        for r in chunks:
            v = wide[g * PLACES + r : g * PLACES + r + CHUNK] + vec(7)
            res[g, r : r + CHUNK, :] = v
            acc += fold8(v)
        sums.append(acc)
    mean3, rstd3 = gn_stats(res, total(sums), mid)
    gain3, shift3 = vec(8), vec(9)
    for g in images:
        for r in chunks:
            y = (res[g, r : r + CHUNK, :] - mean3[g : g + 1]) * rstd3[g : g + 1] * gain3 + shift3
            normed[g * PLACES + r : g * PLACES + r + CHUNK, :] = y.astype(LOWTYPE)

    wide = dot_nn(normed[...], qkv_ref[...])
    qkv[:, :mid] = (wide[:, :mid] + vec(10)).astype(LOWTYPE)
    qkv[:, mid : 2 * mid] = wide[:, mid : 2 * mid].astype(LOWTYPE)
    qkv[:, 2 * mid :] = (wide[:, 2 * mid :] + vec(11)).astype(LOWTYPE)
    scale = mid ** (-0.5)
    for g in images:
        rows = slice(g * PLACES, (g + 1) * PLACES)
        logits = dot_nt(qkv[rows, :mid], qkv[rows, mid : 2 * mid])
        for r in chunks:
            s = logits[r : r + CHUNK] * scale
            e = jnp.exp(s - jnp.max(s, axis=1, keepdims=True))
            p = e / jnp.sum(e, axis=1, keepdims=True)
            attn[g, r : r + CHUNK, :] = p
            plow[g, r : r + CHUNK, :] = p.astype(LOWTYPE)
        attl[rows, :] = dot_nn(plow[g], qkv[rows, 2 * mid :]).astype(LOWTYPE)
    wide = dot_nn(attl[...], outw_ref[...])
    for g in images:
        for r in chunks:
            rows = slice(g * PLACES + r, g * PLACES + r + CHUNK)
            o = res[g, r : r + CHUNK, :] + wide[rows] + vec(12)
            outp[g, r : r + CHUNK, :] = o
            joined[rows, :mid] = (o * sigmoid(o)).astype(LOWTYPE)
            x = x0[g, r : r + CHUNK, :]
            joined[rows, mid:] = (x * sigmoid(x)).astype(LOWTYPE)

    for g in images:
        rows = slice(g * PLACES, (g + 1) * PLACES)
        taps = dot_nt(headw_ref[...], joined[rows, :])
        head = headb_ref[:, :1] + jnp.zeros((ROWS12, PLACES), F32)
        for tap, (di, dj) in enumerate(tap_offsets()):
            head = head + shift_lanes(taps[tap * ROWS12 : (tap + 1) * ROWS12, :], di, dj)
        error = head - noise_ref[g]
        masked = maskw_ref[g] * error
        loss_ref[...] += masked * error
        grad = 2.0 * masked
        ghb_ref[...] += grad
        gradl = grad.astype(LOWTYPE).astype(F32)
        dtap = jnp.concatenate(
            [shift_lanes(gradl, -di, -dj).astype(LOWTYPE) for di, dj in tap_offsets()], axis=0
        )
        ghead_ref[...] += dot_nn(dtap, joined[rows, :])
        wide = dot_tn(dtap, headw_ref[...])
        acc = jnp.zeros((8, mid), F32)
        for r in chunks:
            o = outp[g, r : r + CHUNK, :]
            s = sigmoid(o)
            d = wide[r : r + CHUNK, :mid] * (s * (1.0 + o * (1.0 - s)))
            outp[g, r : r + CHUNK, :] = d
            dout[g * PLACES + r : g * PLACES + r + CHUNK, :] = d.astype(LOWTYPE)
            acc += fold8(d)
            x = x0[g, r : r + CHUNK, :]
            s = sigmoid(x)
            dpool[g, r : r + CHUNK, :] = wide[r : r + CHUNK, mid:] * (s * (1.0 + x * (1.0 - s)))
        add_vec(12, jnp.sum(acc, axis=0, keepdims=True))

    lowt = dout[...].T
    acc_ref[:, SEG_OFF[7] : SEG_OFF[8]] += dot_nn(lowt, attl[...])
    datt = dot_nt(dout[...], outw_ref[...]).astype(LOWTYPE)
    for g in images:
        rows = slice(g * PLACES, (g + 1) * PLACES)
        datt_g = datt[rows]
        gweights = dot_nt(datt_g, qkv[rows, 2 * mid :])
        dval = dot_tn(plow[g], datt_g)
        for r in chunks:
            p = attn[g, r : r + CHUNK, :]
            gw = gweights[r : r + CHUNK]
            ds = p * (gw - jnp.sum(gw * p, axis=1, keepdims=True))
            plow[g, r : r + CHUNK, :] = (ds * scale).astype(LOWTYPE)
        dqry = dot_nn(plow[g], qkv[rows, mid : 2 * mid])
        dkey = dot_tn(plow[g], qkv[rows, :mid])
        add_vec(10, jnp.sum(fold8(dqry), axis=0, keepdims=True))
        add_vec(11, jnp.sum(fold8(dval), axis=0, keepdims=True))
        dq3[rows, :mid] = dqry.astype(LOWTYPE)
        dq3[rows, mid : 2 * mid] = dkey.astype(LOWTYPE)
        dq3[rows, 2 * mid :] = dval.astype(LOWTYPE)
    for k in range(3):
        lowt = dq3[:, k * mid : (k + 1) * mid].T
        acc_ref[:, SEG_OFF[4 + k] : SEG_OFF[5 + k]] += dot_nn(lowt, normed[...])
    wide = dot_nt(dq3[...], qkv_ref[...])

    ones, twos = [], []
    for g in images:
        one, two = jnp.zeros((8, mid), F32), jnp.zeros((8, mid), F32)
        for r in chunks:
            xh = (res[g, r : r + CHUNK, :] - mean3[g : g + 1]) * rstd3[g : g + 1]
            d = wide[g * PLACES + r : g * PLACES + r + CHUNK]
            res[g, r : r + CHUNK, :] = xh
            dyf[g, r : r + CHUNK, :] = d
            one += fold8(d)
            two += fold8(d * xh)
        ones.append(one)
        twos.append(two)
    ones, twos = total(ones), total(twos)
    add_vec(9, jnp.sum(ones, axis=0, keepdims=True))
    add_vec(8, jnp.sum(twos, axis=0, keepdims=True))
    m1, m2 = grouped(ones * gain3, mid), grouped(twos * gain3, mid)
    for g in images:
        r1 = rstd3[g : g + 1]
        acc = jnp.zeros((8, mid), F32)
        for r in chunks:
            d = dyf[g, r : r + CHUNK, :] * (gain3 * r1)
            d = d - m1[g : g + 1] * r1 - res[g, r : r + CHUNK, :] * (m2[g : g + 1] * r1)
            d = d + outp[g, r : r + CHUNK, :]
            acc += fold8(d)
            pad2[g, SIDE + r : SIDE + r + CHUNK, :] = d.astype(LOWTYPE)
        add_vec(7, jnp.sum(acc, axis=0, keepdims=True))

    low = stack([pad2[g, SIDE : SIDE + PLACES, :] for g in images])
    lowt = low.T
    acc_ref[:, SEG_OFF[2] : SEG_OFF[3]] += dot_nn(lowt, low0)
    acc_ref[:, SEG_OFF[1] : SEG_OFF[2]] += dot_nn(
        lowt, stack([dy_cat(a2, g, (0, 1, 2)) for g in images])
    )
    dskip = dot_nt(low, skip_ref[...])
    for g in images:
        dpool[g] += dskip[g * PLACES : (g + 1) * PLACES]

    def conv_back(pad, weights, g, chans, apply):
        wide = dot_nt(dy_cat(pad, g, (2, 1, 0)), weights)
        shiftf[g, 8 : 8 + PLACES, :chans] = wide[:, :chans]
        dyf[g, :, :chans] = wide[:, chans : 2 * chans]
        for r in chunks:
            after = shiftf[g, 9 + r : 9 + r + CHUNK, :chans]
            dyf[g, r : r + CHUNK, :chans] += jnp.where(edge(chans, False), after, 0.0)
        shiftf[g, 8 : 8 + PLACES, :chans] = wide[:, 2 * chans :]
        for r in chunks:
            before = shiftf[g, 7 + r : 7 + r + CHUNK, :chans]
            apply(r, dyf[g, r : r + CHUNK, :chans] + jnp.where(edge(chans, True), before, 0.0))

    def norm_back(pad, weights, ref, mean, rstd, gain, shift, chans):
        ones, twos = [], []
        for g in images:
            sums = [jnp.zeros((8, chans), F32), jnp.zeros((8, chans), F32)]

            def apply(r, da, g=g, sums=sums):
                xh = (ref[g, r : r + CHUNK, :] - mean[g : g + 1]) * rstd[g : g + 1]
                y = xh * gain + shift
                s = sigmoid(y)
                d = da * (s * (1.0 + y * (1.0 - s)))
                ref[g, r : r + CHUNK, :] = xh
                dyf[g, r : r + CHUNK, :chans] = d
                sums[0] += fold8(d)
                sums[1] += fold8(d * xh)

            conv_back(pad, weights, g, chans, apply)
            ones.append(sums[0])
            twos.append(sums[1])
        ones, twos = total(ones), total(twos)
        m1, m2 = grouped(ones * gain, chans), grouped(twos * gain, chans)
        return jnp.sum(ones, axis=0, keepdims=True), jnp.sum(twos, axis=0, keepdims=True), m1, m2

    one, two, m1, m2 = norm_back(pad2, conv2b_ref[...], hid, mean2, rstd2, gain2, shift2, mid)
    add_vec(6, one)
    add_vec(5, two)
    for g in images:
        r1 = rstd2[g : g + 1]
        acc = jnp.zeros((8, mid), F32)
        for r in chunks:
            d = dyf[g, r : r + CHUNK, :] * (gain2 * r1)
            d = d - m1[g : g + 1] * r1 - hid[g, r : r + CHUNK, :] * (m2[g : g + 1] * r1)
            acc += fold8(d)
            pad1[g, SIDE + r : SIDE + r + CHUNK, :] = d.astype(LOWTYPE)
        acc = jnp.sum(acc, axis=0, keepdims=True)
        add_vec(3, acc)
        add_vec(4, acc)
        gtime[pl.ds(step * group + g, 1), :] = acc

    lowt = stack([pad1[g, SIDE : SIDE + PLACES, :] for g in images]).T
    acc_ref[:, SEG_OFF[0] : SEG_OFF[1]] += dot_nn(
        lowt, stack([dy_cat(a1, g, (0, 1, 2)) for g in images])
    )
    one, two, m1, m2 = norm_back(pad1, conv1b_ref[...], x0, mean1, rstd1, gain1, shift1, C1)
    add_vec(2, one)
    add_vec(1, two)
    for g in images:
        r1 = rstd1[g : g + 1]
        acc = jnp.zeros((8, C1), F32)
        lows = []
        for r in chunks:
            d = dyf[g, r : r + CHUNK, :C1] * (gain1 * r1)
            d = d - m1[g : g + 1] * r1 - x0[g, r : r + CHUNK, :] * (m2[g : g + 1] * r1)
            d = d + dpool[g, r : r + CHUNK, :]
            acc += fold8(d)
            lows.append(d.astype(LOWTYPE))
        add_vec(0, jnp.sum(acc, axis=0, keepdims=True))
        gstem_ref[...] += dot_nn(patch[g], stack(lows))

    @pl.when(step == steps - 1)
    def _():
        acc_ref[:, SEG_OFF[3] : SEG_OFF[4]] = dot_tn(gtime[...].astype(LOWTYPE), time_ref[...])


def unet_call(samples, operands):
    group = 2 if samples % 2 == 0 else 1
    steps = samples // group
    time_rows = operands[3].shape[0]
    mid = CHANNELS_MID
    places = group * PLACES

    def image_spec():
        return pl.BlockSpec((group, ROWS12, PLACES), lambda i: (i, 0, 0))

    def whole(shape):
        return pl.BlockSpec(shape, lambda i: (0,) * len(shape))

    out_shapes = [(mid, 5120), (TAPS * ROWS12, C1), (TAPS * ROWS12, mid + C1)] + [
        (ROWS12, mid)
    ] * 3
    scratch = [
        ((group, PLACES, C1), F32),
        ((group, PLACES, mid), F32),
        ((group, PLACES, mid), F32),
        ((group, PLACES, mid), F32),
        ((group, PLACES, mid), F32),
        ((group, HALO, 3 * C1), LOWTYPE),
        ((group, HALO, 3 * mid), LOWTYPE),
        ((places, mid), LOWTYPE),
        ((places, 3 * mid), LOWTYPE),
        ((group, PLACES, mid), LOWTYPE),
        ((places, mid), LOWTYPE),
        ((places, mid + C1), LOWTYPE),
        ((group, TAPS * ROWS12, PLACES), LOWTYPE),
        ((group, HALO, mid), LOWTYPE),
        ((group, HALO, mid), LOWTYPE),
        ((group, PLACES + 16, mid), F32),
        ((group, PLACES, mid), F32),
        ((places, mid), LOWTYPE),
        ((places, 3 * mid), LOWTYPE),
        ((group, PLACES, C1), F32),
        ((time_rows, mid), F32),
        ((time_rows, mid), F32),
    ]
    return pl.pallas_call(
        functools.partial(unet_body, group, steps),
        grid=(steps,),
        out_shape=[jax.ShapeDtypeStruct(shape, F32) for shape in out_shapes],
        in_specs=[image_spec()] * 3 + [whole(a.shape) for a in operands[3:]],
        out_specs=[whole(shape) for shape in out_shapes],
        scratch_shapes=[pltpu.VMEM(shape, kind) for shape, kind in scratch],
        compiler_params=pltpu.CompilerParams(vmem_limit_bytes=VMEM_BYTES),
    )(*operands)


def phase_order():
    pixel = np.arange(S * S)
    row, col = pixel // S, pixel % S
    lane = (row % 2 * 2 + col % 2) * PLACES + row // 2 * SIDE + col // 2
    return jnp.asarray(lane, jnp.int32)


def stem_spread():
    counts = np.zeros((3, 2, 3))
    for block in range(3):
        for inner in range(2):
            for sub in range(2):
                tap = 2 * (block - 1) + inner - sub + 1
                if 0 <= tap <= 2:
                    counts[block, inner, tap] += 1
    full = np.zeros((3, 3, 4, 4, 3, 3, 3))
    for c in range(3):
        both = np.einsum("ayt,bxu->abyxtu", counts, counts) * 0.25
        full[:, :, c, :, :, :, c] = both.reshape(3, 3, 4, 3, 3)
    return jnp.asarray(full.reshape(TAPS * ROWS12, 27), F32)


def split_three(values):
    first = lax.reduce_precision(values, 8, 7)
    second = lax.reduce_precision(values - first, 8, 7)
    third = values - first - second
    return jnp.concatenate([first, second, third], axis=1).astype(LOWTYPE)


def pad_rows(values, rows):
    return jnp.pad(values, [(0, 0)] * (values.ndim - 2) + [(0, rows - values.shape[-2]), (0, 0)])


def by_column(weights, chans):
    return weights.reshape(3, 3 * chans, CHANNELS_MID).transpose(1, 0, 2).reshape(3 * chans, -1)


def same_group(chans):
    group = np.arange(chans) // (chans // GROUPS)
    same = (group[:, None] == group[None, :]) / (PLACES * (chans // GROUPS))
    return jnp.asarray(same, F32)


def ns_update(iterate, gram):
    inner = NS_B * gram + NS_C * jnp.dot(gram, gram, precision=EXACT_PRECISION)
    return NS_A * iterate + jnp.dot(iterate, inner, precision=EXACT_PRECISION)


def local_muon(weight_m, moment, gradient):
    moment_new = MOMENTUM * moment + gradient
    direction = gradient + MOMENTUM * moment_new
    iterate = direction * lax.rsqrt(jnp.sum(direction * direction) + NORM_EPS)
    for step in range(NS_STEPS):
        iterate = ns_update(iterate, jnp.dot(iterate.T, iterate, precision=EXACT_PRECISION))
    return (weight_m * (1.0 - LR_MUON * DECAY) - LR_MUON * iterate, moment_new)


def ns_product(gram):
    eye = jnp.eye(gram.shape[0], dtype=jnp.float32)
    product = None
    for step in range(NS_STEPS):
        square = jnp.dot(gram, gram, precision=EXACT_PRECISION)
        factor = NS_A * eye + NS_B * gram + NS_C * square
        product = (
            factor if product is None else jnp.dot(product, factor, precision=EXACT_PRECISION)
        )
        if step < NS_STEPS - 1:
            half = jnp.dot(gram, factor, precision=EXACT_PRECISION)
            gram = jnp.dot(factor, half, precision=EXACT_PRECISION)
    return product


def shards(
    images,
    pixel_mask,
    timesteps,
    noise_field,
    matrices,
    matrix_moms,
    stem_weight,
    stem_moms,
    head_weight,
    head_moms,
    vectors,
    vector_firsts,
    vector_seconds,
):
    owners = lax.axis_size("bucket")
    gathered = lax.all_gather(matrices.astype(LOWTYPE), "bucket", axis=0, tiled=True)
    conv_one, conv_two, skip_w, temb_w, query_w, key_w, value_w, out_w = unpack(gathered, owners)
    samples = images.shape[0]
    level, weight = plan(timesteps)
    counts = jnp.sum(pixel_mask.astype(jnp.float32), axis=1)
    weight_local = jnp.sum(3.0 * weight * counts)
    noisy = (
        jnp.sqrt(level)[:, None, None] * images + jnp.sqrt(1.0 - level)[:, None, None] * noise_field
    )
    mask_weight = pixel_mask.astype(jnp.float32) * weight[:, None]
    rows = jnp.concatenate(
        [
            lax.reduce_precision(noisy, 8, 7).reshape(-1, S * S),
            noise_field.reshape(-1, S * S),
            mask_weight,
        ],
        axis=0,
    )
    order = (phase_order()[:, None] == jnp.arange(S * S, dtype=jnp.int32)[None, :]).astype(F32)
    phased = jnp.dot(rows, order, precision=EXACT_PRECISION)
    planes = 3 * samples
    noisy_low = pad_rows(phased[:planes].reshape(samples, 12, PLACES), ROWS12).astype(LOWTYPE)
    noise_planes = pad_rows(phased[planes : 2 * planes].reshape(samples, 12, PLACES), ROWS12)
    mask_planes = jnp.broadcast_to(
        phased[2 * planes :].reshape(samples, 1, 4, PLACES), (samples, 3, 4, PLACES)
    ).reshape(samples, 12, PLACES)
    mask_planes = pad_rows(mask_planes, ROWS12)
    time_in = pad_rows(swish(embed(timesteps)).astype(LOWTYPE), -(-samples // 16) * 16)
    spread = stem_spread()
    stem_blocks = split_three(
        jnp.dot(spread, lax.reduce_precision(stem_weight, 8, 7), precision=EXACT_PRECISION)
    )
    head_rows = head_weight.astype(LOWTYPE).reshape(TAPS, CHANNELS_MID + C1, 4, 3)
    head_rows = pad_rows(
        head_rows.transpose(0, 3, 2, 1).reshape(TAPS, 12, CHANNELS_MID + C1), ROWS12
    ).reshape(TAPS * ROWS12, -1)
    vec_rows = jnp.concatenate(
        [
            jnp.pad(vectors[: 3 * C1].reshape(3, C1), ((0, 0), (0, CHANNELS_MID - C1))),
            vectors[3 * C1 : -12].reshape(10, CHANNELS_MID),
        ],
        axis=0,
    )
    head_bias = jnp.broadcast_to(
        pad_rows(vectors[-12:].reshape(4, 3).T.reshape(12, 1), ROWS12), (ROWS12, C1)
    )
    acc, gstem_rows, ghead_rows, gvec, ghead_bias, loss_rows = unet_call(
        samples,
        [
            noisy_low,
            noise_planes,
            mask_planes,
            time_in,
            stem_blocks,
            head_rows,
            conv_one,
            by_column(conv_one, C1),
            conv_two,
            by_column(conv_two, CHANNELS_MID),
            skip_w,
            temb_w,
            jnp.concatenate([query_w, key_w, value_w], axis=1),
            out_w,
            pad_rows(vec_rows, ROWS12),
            head_bias,
            same_group(C1),
            same_group(CHANNELS_MID),
        ],
    )
    loss_local = jnp.sum(loss_rows)
    g_stem = jnp.dot(spread.T, gstem_rows, precision=EXACT_PRECISION)
    g_head = (
        ghead_rows.reshape(TAPS, ROWS12, -1)[:, :12]
        .reshape(TAPS, 3, 4, CHANNELS_MID + C1)
        .transpose(0, 3, 2, 1)
        .reshape(-1, 12)
    )
    grad_vec = jnp.concatenate(
        [
            gvec[:3, :C1].reshape(-1),
            gvec[3:13].reshape(-1),
            jnp.sum(ghead_bias[:12], axis=1).reshape(3, 4).T.reshape(-1),
        ]
    )
    natural = acc.T
    grad_pack = pack([natural[a:b] for a, b in zip(SEG_OFF[:-1], SEG_OFF[1:])], owners)
    rows_dev = matrices.shape[0]
    summed, grad_stem, grad_headw, grad_vec, loss_sum, weight_sum = lax.psum(
        (grad_pack, g_stem, g_head, grad_vec, loss_local, weight_local), ("bucket", "batch")
    )
    inverse = 1.0 / weight_sum
    summed = summed * inverse
    grad_stem = grad_stem * inverse
    grad_headw = grad_headw * inverse
    grad_vec = grad_vec * inverse
    grad_mine = lax.dynamic_slice_in_dim(summed, lax.axis_index("bucket") * rows_dev, rows_dev, 0)
    shares = [seg_rows // owners for seg_rows in segment_rows()]
    weight_parts, moment_parts, grad_parts = ([], [], [])
    start = 0
    for share in shares:
        weight_parts.append(matrices[start : start + share])
        moment_parts.append(matrix_moms[start : start + share])
        grad_parts.append(grad_mine[start : start + share])
        start += share
    moments_new = [
        MOMENTUM * moment + gradient for moment, gradient in zip(moment_parts, grad_parts)
    ]
    directions = [gradient + MOMENTUM * moment for gradient, moment in zip(grad_parts, moments_new)]
    gram_sums = lax.psum(
        tuple(jnp.dot(d.T, d, precision=EXACT_PRECISION) for d in directions), "bucket"
    )
    iterates = []
    for direction, gram in zip(directions, gram_sums):
        scale = lax.rsqrt(jnp.trace(gram) + NORM_EPS)
        iterates.append(
            jnp.dot(direction * scale, ns_product(gram * (scale * scale)), precision=EXACT_PRECISION)
        )
    new_matrices = jnp.concatenate(
        [
            weight_m * (1.0 - LR_MUON * DECAY) - LR_MUON * iterate
            for weight_m, iterate in zip(weight_parts, iterates)
        ],
        axis=0,
    )
    new_matrix_moms = jnp.concatenate(moments_new, axis=0)
    new_stem, new_stem_moms = local_muon(stem_weight, stem_moms, grad_stem)
    new_head, new_head_moms = local_muon(head_weight, head_moms, grad_headw)
    new_firsts = BETA_ONE * vector_firsts + (1.0 - BETA_ONE) * grad_vec
    new_seconds = BETA_TWO * vector_seconds + (1.0 - BETA_TWO) * grad_vec * grad_vec
    step_dir = (
        new_firsts
        / (1.0 - BETA_ONE**STEP)
        / (jnp.sqrt(new_seconds / (1.0 - BETA_TWO**STEP)) + ADAM_EPS)
    )
    new_vectors = vectors - LR_ADAM * step_dir
    return (
        loss_sum,
        weight_sum,
        new_matrices,
        new_matrix_moms,
        new_matrices.astype(LOWTYPE),
        new_stem,
        new_stem_moms,
        new_stem.astype(LOWTYPE),
        new_head,
        new_head_moms,
        new_head.astype(LOWTYPE),
        new_vectors,
        new_firsts,
        new_seconds,
        new_vectors.astype(LOWTYPE),
    )


def solution(mesh):
    return jax.shard_map(
        shards,
        mesh=mesh,
        in_specs=(
            P(("bucket", "batch"), None, None),
            P(("bucket", "batch"), None),
            P(("bucket", "batch")),
            P(("bucket", "batch"), None, None),
            P("bucket", None),
            P("bucket", None),
            P(),
            P(),
            P(),
            P(),
            P(),
            P(),
            P(),
        ),
        out_specs=(
            P(),
            P(),
            P("bucket", None),
            P("bucket", None),
            P("bucket", None),
            P(),
            P(),
            P(),
            P(),
            P(),
            P(),
            P(),
            P(),
            P(),
            P(),
        ),
        check_vma=False,
    )
```

time: 1200 us -> 660 us (0.55)
  matrix products: 370 us -> 96.9 us
  local copies, waits for them, and re-layouts: 301 us -> 58.6 us
  other arithmetic: 205 us -> 24.6 us
  Pallas kernels: 16.6 us -> 133 us
  waiting for transfers between devices: 228 us -> 276 us
    dot_general x27 -> x3, matrix products: 272 us -> 3.16 us  [the longest x1 1.74 us: shards(): phased = jnp.dot(rows, order, precision=EXACT_PRECISION)]
    pallas_call x0 -> x1, Pallas kernels: none -> 133 us  [unet_call(): pl.pallas_call(functools.partial(unet_body, group, steps), grid=(steps,),...]
    squeeze x3 -> x0, local copies, waits for them, and re-layouts: 92.3 us -> none  [unpatch(): parts[:, :, :, shift_y * 3 + shift_x, :]]
    add x6 -> x0, other arithmetic: 69.9 us -> none  [the longest x5 66.6 us: unpatch(): total = placed if total is None else total + placed]
    reduce_sum x25 -> x2, other arithmetic: 71.4 us -> 2.67 us  [the longest x1 1.34 us: shards(): jnp.sum(ghead_bias[:12], axis=1).reshape(3, 4).T.reshape(-1)]
    unnamed x331 -> x132, local copies, waits for them, and re-layouts: 68.6 us -> 9.48 us
    dot_general x4 -> x0, local copies, waits for them, and re-layouts: 50.5 us -> none  [the longest x3 49.8 us: weight_grad(): jnp.einsum('bpk,bpn->kn', left, grad_out, preferred_element_type=jnp.floa...]
    all_gather x1, waiting for transfers between devices: 0.02 us -> 48.4 us  [shards(): lax.all_gather(matrices.astype(LOWTYPE), 'bucket', axis=0, tiled=True)]
  transfers between devices with their start and end apart: 3 -> 3, of which waited for: 2 -> 3; matrix products, arithmetic and copies ran while one was open for 8% -> 3% of each run, Pallas kernels for 0% -> 0%
where the time goes in v2:
time: 660 us; the launch traced here: 654 us
  waiting for transfers between devices  276 us (42%)
  Pallas kernels  133 us (20%)
  matrix products  96.9 us (15%)
  local copies, waits for them, and re-layouts  58.6 us (9%)
  blocking collectives  40 us (6%)
  other arithmetic  24.6 us (4%)
  between operations  23.9 us (4%)
    psum x1, waiting for transfers between devices, shards(): lax.psum((grad_pack, g_stem, g_head, grad_vec, loss_local, weight_local),...  145 us
    pallas_call x1, Pallas kernels, unet_call(): pl.pallas_call(functools.partial(unet_body, group, steps), grid=(steps,),...  133 us
    psum x1, waiting for transfers between devices, shards(): lax.psum(tuple((jnp.dot(d.T, d, precision=EXACT_PRECISION) for d in direc...  82.6 us
    all_gather x1, waiting for transfers between devices, shards(): lax.all_gather(matrices.astype(LOWTYPE), 'bucket', axis=0, tiled=True)  48.4 us
    psum x1, blocking collectives, shards(): lax.psum((grad_pack, g_stem, g_head, grad_vec, loss_local, weight_local),...  40 us
    dot_general x32, matrix products, ns_product(): half = jnp.dot(gram, factor, precision=EXACT_PRECISION)  20.5 us
    dot_general x40, matrix products, ns_product(): square = jnp.dot(gram, gram, precision=EXACT_PRECISION)  20.2 us
    slice x12, local copies, waits for them, and re-layouts, shards(): natural[a:b]  19.9 us
  transfers between devices with their start and end apart: 3, of which 3 were waited for; matrix products, arithmetic and copies ran while one was open for 3% of the time, Pallas kernels for 0%

profile of v2, /device:TPU:0, one launch (start us, length us, event | category | flops | bytes accessed | tf_op | source)
XLA Modules:
  0.0 653.8 jit_solution(13306411997168613056)
XLA Ops:
  7.3 2.3 convert_element_type.58
  11.4 1.7 fusion.2
  19.3 48.4 %all-gather.2.cloned.1.call-done = bf16[5120,256]{1,0:T(8,128)(2,1)} async-done(((bf16[1280,256]{1,0:T(8,128)(2,1)}), bf16[5120,256]{1,0:T(8,128)(2,1)}) %all-gather.2.cloned.1.call-update) | async-done | bytes 2621456 | tf_op jit(solution)/shard_map/all_gather | solution.py:638
  69.2 1.6 slice.207
  70.9 1.8 fusion.177
  73.8 1.6 slice.205
  80.5 132.9 %shard_map.280 = (f32[256,5120]{1,0:T(8,128)}, f32[144,128]{1,0:T(8,128)}, f32[144,384]{1,0:T(8,128)}, f32[16,256]{1,0:T(8,128)}, f32[16,256]{1,0:T(8,128)}, /*index=5*/f32[16,256]{1,0:T(8,128)}) custom-call(bf16[20,16,256]{2,1,0:T(8,128)(2,1)} %pad.31.noisy_ref, f32[20,16,256]{2,1,0:T(8,128)} %pad.32.noise_ref, f32[20,16,256]{2,1,0:T(8,128)} %pad.33.maskw_ref, ...), custom_call_target="tpu_custom_call" | custom-call | tf_op jit(solution)/shard_map/pallas_call | solution.py:539
  215.4 1.6 slice.214
  217.0 1.9 slice.215
  218.9 2.2 fusion.176
  222.4 1.8 slice.213
  233.9 40.0 %all-reduce.8 = (f32[]{:T(128)}, f32[]{:T(128)}, f32[27,128]{1,0:T(8,128)}, f32[2956]{0:T(1024)}) all-reduce(f32[]{:T(128)} %reduce_sum.86, f32[]{:T(128)} %get-tuple-element.51, f32[27,128]{1,0:T(8,128)S(1)} %fusion.269, f32[2956]{0:T(1024)} %pad_maximum_fusion.3), channel_id=1, replica_groups=mesh['bucket'=4,'batch'=8] {'bucket','batch'}, use_global_device_ids=true, to_apply=%region_1.0 | all-reduce | flops 6414 | bytes 51312 | tf_op jit(solution)/shard_map/psum | solution.py:725
  274.7 1.9 multiply_reduce_fusion.1
  279.7 1.7 copy.67
  281.4 1.7 reshape.193
  284.8 2.0 copy.75
  286.8 1.8 copy.71
  288.6 1.8 copy.70
  290.4 1.8 copy.69
  292.2 1.8 copy.68
  294.0 2.0 copy.66
  298.4 1.6 constant_dynamic-update-slice_fusion.6
  309.0 145.2 %all-reduce.14.cloned.1.call-done = (f32[5120,256]{1,0:T(8,128)}, f32[3456,12]{0,1:T(8,128)}) async-done(((f32[5120,256]{1,0:T(8,128)}, f32[3456,12]{0,1:T(8,128)}), (f32[5120,256]{1,0:T(8,128)}, f32[3456,12]{0,1:T(8,128)})) %all-reduce.14.cloned.1.call-update) | async-done | bytes 5408784 | tf_op jit(solution)/shard_map/psum | solution.py:725
  454.2 1.5 dynamic-slice_multiply_fusion
  462.7 1.5 fusion.128
  464.2 2.0 fusion.107
  479.2 82.6 %all-reduce.16.cloned.1.call-done = (f32[256,256]{1,0:T(8,128)}, f32[256,256]{1,0:T(8,128)}, f32[256,256]{1,0:T(8,128)}, f32[256,256]{1,0:T(8,128)}, f32[256,256...) async-done(((f32[256,256]{1,0:T(8,128)}, f32[256,256]{1,0:T(8,128)}, f32[256,256]{1,0:T(8,128)}, f32[256,256]{1,0:T(8,128)}, ...) | async-done | bytes 2097168 | tf_op jit(solution)/shard_map/psum | solution.py:746
  561.9 1.7 select_reduce_fusion
  564.3 1.6 fusion.12
  589.2 1.6 fusion.37
  596.5 1.5 fusion.42
  603.3 1.6 fusion.47
  (391 shorter events, 133.3 us)
Async XLA Ops:
  7.2 2.5 copy-start.54
  7.2 2.5 copy-start.59
  7.2 2.5 copy-start.15
  7.2 2.7 copy-start.46
  7.2 3.5 copy-start.48
  7.2 60.5 %all-gather.2.cloned.1.call-start = ((), (), s32[]{:S(2)}) async-start(), calls=%async_computation | async-start | bytes 3276800 | tf_op jit(solution)/shard_map/all_gather | solution.py:638
  9.6 444.6 %all-reduce.14.cloned.1.call-start = ((), (), s32[]{:S(2)}) async-start(), calls=%async_computation.1 | async-start | bytes 10928128 | tf_op jit(solution)/shard_map/psum | solution.py:725
  11.4 2.1 copy-start.42
  16.1 2.3 copy-start.47
  16.2 2.3 copy-start.52
  73.8 1.9 copy-start.3
  75.3 2.3 copy-start.1
  296.3 2.1 copy-start.2
  298.4 1.6 copy-start.45
  298.4 2.3 copy-start.13
  300.0 2.3 copy-start.32
  300.0 3.0 copy-start.31
  300.7 3.1 copy-start.30
  304.6 3.6 copy-start.53
  304.6 257.3 %all-reduce.16.cloned.1.call-start = ((), (), s32[]{:S(2)}) async-start(), calls=%async_computation.2 | async-start | bytes 4194304 | tf_op jit(solution)/shard_map/psum | solution.py:746
  454.2 1.7 copy-start
  464.2 2.7 copy-start.49
  464.2 2.7 copy-start.50
  473.3 4.8 copy-start.43
  561.9 4.0 copy-start.41
  566.7 3.3 copy-start.40
  571.1 2.8 copy-start.38
  571.1 2.8 copy-start.39
  580.9 2.6 copy-start.36
  580.9 2.6 copy-start.37
  592.5 2.6 copy-start.34
  592.5 2.6 copy-start.35
  (32 other events, 36.0 us)
Sparse Core Ops, SparseCore 0:
  10.2 57.4 all-gather.1
  304.7 149.4 all-reduce.13
  473.3 88.5 all-reduce.15

commit v3 on v2

--- a/solution.py
+++ b/solution.py
@@ -59,11 +59,6 @@
     return pieces
 
 
-def pack(pieces, owners):
-    blocks = [piece.reshape(owners, -1, piece.shape[1]) for piece in pieces]
-    return jnp.concatenate(blocks, axis=1).reshape(-1, pieces[0].shape[1])
-
-
 def plan(timesteps):
     frac_t = (timesteps.astype(jnp.float32) / TSTEPS + 0.008) / 1.008
     level = jnp.cos(frac_t * (math.pi / 2)) ** 2
@@ -89,6 +84,7 @@
 TAPS = 9
 ROWS12 = 16
 CHUNK = 64
+SMALL_ROWS = 240
 VMEM_BYTES = 56 * 1024 * 1024
 SEG_OFF = (0, 1152, 3456, 3584, 4096, 4352, 4608, 4864, 5120)
 
@@ -132,6 +128,8 @@
 def unet_body(
     group,
     steps,
+    owners,
+    peers,
     noisy_ref,
     noise_ref,
     maskw_ref,
@@ -150,12 +148,16 @@
     headb_ref,
     same128_ref,
     same256_ref,
+    spread_ref,
+    rows_ref,
+    misc_ref,
     acc_ref,
     gstem_ref,
     ghead_ref,
     gvec_ref,
     ghb_ref,
     loss_ref,
+    wsum_ref,
     x0,
     hid,
     res,
@@ -192,6 +194,7 @@
         gvec_ref[...] = jnp.zeros_like(gvec_ref)
         ghb_ref[...] = jnp.zeros_like(ghb_ref)
         loss_ref[...] = jnp.zeros_like(loss_ref)
+        wsum_ref[...] = jnp.zeros_like(wsum_ref)
         gtime[...] = jnp.zeros_like(gtime)
         for ref in (a1, a2, pad1, pad2):
             for g in images:
@@ -201,7 +204,10 @@
         tproj[...] = dot_nn(time_ref[...], temb_ref[...])
 
     def vec(row, chans=mid):
-        return vec_ref[row : row + 1, :chans]
+        if chans == C1:
+            return vec_ref[row : row + 1, :]
+        row = 2 * row - 3
+        return jnp.concatenate([vec_ref[row : row + 1, :], vec_ref[row + 1 : row + 2, :]], axis=1)
 
     def add_vec(row, value):
         gvec_ref[row : row + 1, : value.shape[1]] += value
@@ -338,6 +344,7 @@
         error = head - noise_ref[g]
         masked = maskw_ref[g] * error
         loss_ref[...] += masked * error
+        wsum_ref[...] += maskw_ref[g]
         grad = 2.0 * masked
         ghb_ref[...] += grad
         gradl = grad.astype(LOWTYPE).astype(F32)
@@ -494,9 +501,81 @@
     @pl.when(step == steps - 1)
     def _():
         acc_ref[:, SEG_OFF[3] : SEG_OFF[4]] = dot_tn(gtime[...].astype(LOWTYPE), time_ref[...])
-
-
-def unet_call(samples, operands):
+        if rows_ref.shape[0] > 5120 + SMALL_ROWS:
+            rows_ref[...] = jnp.zeros_like(rows_ref)
+        pieces = gradient_pieces(owners, peers)
+        for block in range(0, 5120, C1):
+            turned = acc_ref[:, block : block + C1].T
+            for source, size, target in pieces:
+                low, high = max(source, block), min(source + size, block + C1)
+                if low < high:
+                    start = target + low - source
+                    rows_ref[start : start + high - low, :] = turned[low - block : high - block]
+        stem = lax.dot_general(
+            spread_ref[...],
+            gstem_ref[...],
+            (((0,), (0,)), ((), ())),
+            preferred_element_type=F32,
+            precision=EXACT_PRECISION,
+        )
+        head = ghead_ref[...]
+        none = jnp.zeros((ROWS12, C1), F32)
+        tiles = [head[k : k + 16, :mid] for k in range(0, 144, 16)]
+        for k in range(0, 80, 16):
+            other = head[80 + k : 96 + k, mid:] if k < 64 else none
+            tiles.append(jnp.concatenate([head[k : k + 16, mid:], other], axis=1))
+        tiles.append(jnp.concatenate([stem[:16], stem[16:]], axis=1))
+        for tile, (start, _) in zip(tiles, small_tiles(owners, peers)):
+            rows_ref[start : start + 16, :] = tile
+        misc_ref[:, :mid] = gvec_ref[...]
+        misc_ref[13:14, :mid] = jnp.sum(loss_ref[...], axis=0, keepdims=True)
+        misc_ref[14:15, :mid] = jnp.sum(wsum_ref[...], axis=0, keepdims=True)
+        misc_ref[:, mid:] = ghb_ref[:, :C1] + ghb_ref[:, C1:]
+
+
+def chunk_rows(owners, peers):
+    share = -(-5120 // (owners * peers))
+    return -(-share // 16) * 16, -(-(-(-SMALL_ROWS // peers)) // 16) * 16
+
+
+def block_rows(owners, peers):
+    chunk, small = chunk_rows(owners, peers)
+    return owners * chunk + small
+
+
+def slot_of(peer, peers):
+    return peer % 2 * (peers // 2) + peer // 2
+
+
+def gradient_pieces(owners, peers):
+    chunk, _ = chunk_rows(owners, peers)
+    block = block_rows(owners, peers)
+    pieces = []
+    for owner in range(owners):
+        packed = 0
+        for seg, seg_rows in enumerate(segment_rows()):
+            share = seg_rows // owners
+            done = 0
+            while done < share:
+                row = packed + done
+                size = min(share - done, chunk - row % chunk)
+                target = slot_of(row // chunk, peers) * block + owner * chunk + row % chunk
+                pieces.append((SEG_OFF[seg] + owner * share + done, size, target))
+                done += size
+            packed += share
+    return pieces
+
+
+def small_tiles(owners, peers):
+    chunk, small = chunk_rows(owners, peers)
+    tiles = []
+    for row in range(0, SMALL_ROWS, 16):
+        slot = slot_of(row // small, peers)
+        tiles.append((slot * block_rows(owners, peers) + owners * chunk + row % small, slot))
+    return tiles
+
+
+def unet_call(samples, owners, peers, operands):
     group = 2 if samples % 2 == 0 else 1
     steps = samples // group
     time_rows = operands[3].shape[0]
@@ -509,10 +588,15 @@
     def whole(shape):
         return pl.BlockSpec(shape, lambda i: (0,) * len(shape))
 
-    out_shapes = [(mid, 5120), (TAPS * ROWS12, C1), (TAPS * ROWS12, mid + C1)] + [
-        (ROWS12, mid)
-    ] * 3
+    out_shapes = [(peers * block_rows(owners, peers), mid), (ROWS12, mid + C1)]
     scratch = [
+        ((mid, 5120), F32),
+        ((TAPS * ROWS12, C1), F32),
+        ((TAPS * ROWS12, mid + C1), F32),
+        ((ROWS12, mid), F32),
+        ((ROWS12, mid), F32),
+        ((ROWS12, mid), F32),
+        ((ROWS12, mid), F32),
         ((group, PLACES, C1), F32),
         ((group, PLACES, mid), F32),
         ((group, PLACES, mid), F32),
@@ -537,13 +621,442 @@
         ((time_rows, mid), F32),
     ]
     return pl.pallas_call(
-        functools.partial(unet_body, group, steps),
+        functools.partial(unet_body, group, steps, owners, peers),
         grid=(steps,),
         out_shape=[jax.ShapeDtypeStruct(shape, F32) for shape in out_shapes],
         in_specs=[image_spec()] * 3 + [whole(a.shape) for a in operands[3:]],
         out_specs=[whole(shape) for shape in out_shapes],
         scratch_shapes=[pltpu.VMEM(shape, kind) for shape, kind in scratch],
         compiler_params=pltpu.CompilerParams(vmem_limit_bytes=VMEM_BYTES),
+    )(*operands)
+
+
+TASKS = ((1, 0), (0, 0), (0, 1), (2, 0), (1, 1), (2, 1), (3, 0), (3, 1))
+MESH = pl.DeviceIdType.MESH
+SMALL_LANES = 9 * (CHANNELS_MID + C1)
+
+
+def ns_chain(gram, eye):
+    product = None
+    for step in range(NS_STEPS):
+        square = dot_nn(gram, gram, EXACT_PRECISION)
+        factor = NS_A * eye + NS_B * gram + NS_C * square
+        product = factor if product is None else dot_nn(product, factor, EXACT_PRECISION)
+        if step < NS_STEPS - 1:
+            gram = dot_nn(factor, dot_nn(gram, factor, EXACT_PRECISION), EXACT_PRECISION)
+    return product
+
+
+def identity(size):
+    rows = lax.broadcasted_iota(jnp.int32, (size, size), 0)
+    cols = lax.broadcasted_iota(jnp.int32, (size, size), 1)
+    return (rows == cols).astype(F32)
+
+
+def muon_body(
+    owners,
+    peers,
+    rows_ref,
+    misc_ref,
+    weight_ref,
+    moment_ref,
+    stem_ref,
+    stemm_ref,
+    head_ref,
+    headm_ref,
+    vec_ref,
+    first_ref,
+    second_ref,
+    new_ref,
+    newm_ref,
+    copy_ref,
+    nstem_ref,
+    nstemm_ref,
+    nhead_ref,
+    nheadm_ref,
+    nvec_ref,
+    nfirst_ref,
+    nsecond_ref,
+    sums_ref,
+    recv1,
+    own2,
+    send2,
+    recv2,
+    send3,
+    recv3,
+    recvs3,
+    gathered,
+    misc1,
+    misc2,
+    misc3,
+    direction,
+    mine_u,
+    gram_part,
+    gram_recv,
+    gram_all,
+    small,
+    x_zero,
+    x_one,
+    sem1,
+    sem2,
+    sem3,
+    sems3,
+    sema,
+    semb,
+    semg,
+    semh,
+    semx,
+    semy,
+    semm1,
+    semm2,
+    semm3,
+):
+    mid = CHANNELS_MID
+    chips = peers // 2
+    chunk, small_chunk = chunk_rows(owners, peers)
+    block = block_rows(owners, peers)
+    held = chunk + small_chunk
+    own_rows = weight_ref.shape[0]
+    z = lax.axis_index("bucket")
+    peer = lax.axis_index("batch")
+    chip, core = peer // 2, peer % 2
+    partner = {"batch": chip * 2 + 1 - core}
+    started = []
+
+    def same_core(k):
+        return {"batch": lax.rem(chip + k, chips) * 2 + core}
+
+    def along(k):
+        return {"bucket": lax.rem(z + k, owners)}
+
+    def send(source, target, sems, slot, device, begin=True):
+        copy = pltpu.make_async_remote_copy(
+            src_ref=source,
+            dst_ref=target,
+            send_sem=sems.at[0, slot],
+            recv_sem=sems.at[1, slot],
+            device_id=device,
+            device_id_type=MESH,
+        )
+        copy.start()
+        if begin:
+            started.append(copy)
+        return copy
+
+    barrier = pltpu.get_barrier_semaphore()
+    friends = [partner] + [same_core(k) for k in range(1, chips)]
+    friends += [along(k) for k in range(1, owners)]
+    for friend in friends:
+        pl.semaphore_signal(barrier, inc=1, device_id=friend, device_id_type=MESH)
+    pl.semaphore_wait(barrier, len(friends))
+
+    misc_copy = send(misc_ref, misc1, semm1, 0, partner)
+    first = []
+    order = list(range(1, chips)) + [0]
+    for k in order:
+        other = lax.rem(chip + k, chips)
+        start = pl.multiple_of(((1 - core) * chips + other) * block, 16)
+        first.append(send(rows_ref.at[pl.ds(start, block), :], recv1.at[k], sem1, k, partner))
+
+    misc_copy.wait_recv()
+    misc2[chip] = misc_ref[...] + misc1[...]
+    misc_copies = [
+        send(misc2.at[chip], misc2.at[chip], semm2, k - 1, same_core(k)) for k in range(1, chips)
+    ]
+    second = []
+    for k, copy in zip(order, first):
+        copy.wait_recv()
+        other = lax.rem(chip + k, chips)
+        start = pl.multiple_of((core * chips + other) * block, 16)
+        total = rows_ref[pl.ds(start, block), :] + recv1[k]
+        if k == 0:
+            own2[...] = total
+        else:
+            send2[k - 1] = total
+            second.append(send(send2.at[k - 1], recv2.at[k - 1], sem2, k - 1, same_core(k)))
+
+    for copy in misc_copies:
+        copy.wait_recv()
+    misc3[z] = sum([misc2[k] for k in range(1, chips)], misc2[0])
+    misc_copies = [
+        send(misc3.at[z], misc3.at[z], semm3, k - 1, along(k)) for k in range(1, owners)
+    ]
+    for copy in second:
+        copy.wait_recv()
+    third = []
+    for k in list(range(1, owners)) + [0]:
+        start = pl.multiple_of(lax.rem(z + k, owners) * chunk, 16)
+        rows = pl.ds(start, chunk)
+        total = own2[rows, :]
+        for other in range(chips - 1):
+            total = total + recv2[other, rows, :]
+        if k == 0:
+            own2[rows, :] = total
+        else:
+            send3[k - 1] = total
+            third.append(send(send3.at[k - 1], recv3.at[k - 1], sem3, k - 1, along(k)))
+    tail = slice(owners * chunk, block)
+    total = own2[tail, :]
+    for other in range(chips - 1):
+        total = total + recv2[other, tail, :]
+    recvs3[z] = total
+    third += [
+        send(recvs3.at[z], recvs3.at[z], sems3, k - 1, along(k)) for k in range(1, owners)
+    ]
+    for copy in third:
+        copy.wait_recv()
+    total = own2[pl.ds(pl.multiple_of(z * chunk, 16), chunk), :]
+    for other in range(owners - 1):
+        total = total + recv3[other]
+    slot = core * chips + chip
+    gathered[slot, :chunk, :] = total
+    total = recvs3[0]
+    for other in range(1, owners):
+        total = total + recvs3[other]
+    gathered[slot, chunk:, :] = total
+
+    here = gathered.at[slot]
+    plane = [send(here, here, sema, k - 1, same_core(k)) for k in range(1, chips)]
+    cross = [send(here, here, semb, 0, partner)]
+
+    for copy in misc_copies:
+        copy.wait_recv()
+    misc = sum([misc3[k] for k in range(1, owners)], misc3[0])
+    weight_sum = jnp.sum(misc[14:15, :mid], axis=1, keepdims=True)
+    inverse = 1.0 / weight_sum
+    loss_sum = jnp.sum(misc[13:14, :mid], axis=1, keepdims=True)
+    lane = lax.broadcasted_iota(jnp.int32, (8, C1), 1)
+    sums_ref[...] = jnp.where(lane == 0, loss_sum, weight_sum)
+    head_bias = jnp.sum(misc[:, mid:].T, axis=0, keepdims=True)
+    nvec_ref[...] = jnp.zeros_like(nvec_ref)
+    nvec_ref[:3, :] = misc[:3, :C1]
+    for row in range(3, 13):
+        nvec_ref[2 * row - 3 : 2 * row - 2, :] = misc[row : row + 1, :C1]
+        nvec_ref[2 * row - 2 : 2 * row - 1, :] = misc[row : row + 1, C1:mid]
+    nvec_ref[23:24, :ROWS12] = head_bias
+    grad = nvec_ref[...] * inverse
+    firsts = BETA_ONE * first_ref[...] + (1.0 - BETA_ONE) * grad
+    seconds = BETA_TWO * second_ref[...] + (1.0 - BETA_TWO) * grad * grad
+    nfirst_ref[...] = firsts
+    nsecond_ref[...] = seconds
+    change = (
+        firsts
+        / (1.0 - BETA_ONE**STEP)
+        / (jnp.sqrt(seconds / (1.0 - BETA_TWO**STEP)) + ADAM_EPS)
+    )
+    nvec_ref[...] = vec_ref[...] - LR_ADAM * change
+
+    for k, copy in zip(range(1, chips), plane):
+        copy.wait_recv()
+        other = gathered.at[core * chips + lax.rem(chip + chips - k, chips)]
+        cross.append(send(other, other, semb, k, partner))
+    for copy in cross:
+        copy.wait_recv()
+
+    for owner_peer in range(peers):
+        start = owner_peer * chunk
+        size = min(chunk, own_rows - start)
+        if size > 0:
+            grad = gathered[slot_of(owner_peer, peers), :size, :] * inverse
+            rows = slice(start, start + size)
+            moment = MOMENTUM * moment_ref[rows, :] + grad
+            newm_ref[rows, :] = moment
+            direction[rows, :] = grad + MOMENTUM * moment
+    shares = [rows // owners for rows in segment_rows()]
+    starts = [sum(shares[:k]) for k in range(len(shares))]
+    for (task_chip, task_core), share, start in zip(TASKS, shares, starts):
+
+        @pl.when((lax.rem(chip, 4) == task_chip) & (core == task_core))
+        def _(share=share, start=start):
+            mine_u[:share, :] = direction[start : start + share, :]
+            if share < mine_u.shape[0]:
+                mine_u[share:, :] = jnp.zeros((mine_u.shape[0] - share, mid), F32)
+
+    mine = mine_u[...]
+    gram_part[...] = lax.dot_general(
+        mine,
+        mine,
+        (((0,), (0,)), ((), ())),
+        preferred_element_type=F32,
+        precision=EXACT_PRECISION,
+    )
+    part = mid // owners
+    copies = []
+    for k in range(1, owners):
+        start = pl.multiple_of(lax.rem(z + k, owners) * part, 8)
+        copies.append(send(gram_part.at[pl.ds(start, part), :], gram_recv.at[z], semg, k - 1, along(k)))
+    own_part = pl.ds(pl.multiple_of(z * part, 8), part)
+    gram_recv[z] = gram_part[own_part, :]
+
+    chunk_s = small_chunk
+    tiles = []
+    for tile in range(SMALL_ROWS // 16):
+        row = tile * 16
+        at = chunk + row % chunk_s
+        tiles.append(gathered[slot_of(row // chunk_s, peers), at : at + 16, :] * inverse)
+    for tap in range(TAPS):
+        lanes = slice(tap * (mid + C1), tap * (mid + C1) + mid)
+        nheadm_ref[:, lanes] = tiles[tap]
+        lanes = slice(tap * (mid + C1) + mid, (tap + 1) * (mid + C1))
+        if tap < 5:
+            nheadm_ref[:, lanes] = tiles[9 + tap][:, :C1]
+        else:
+            nheadm_ref[:, lanes] = tiles[9 + tap - 5][:, C1:]
+    grad = nheadm_ref[...]
+    moment = MOMENTUM * headm_ref[...] + grad
+    nheadm_ref[...] = moment
+    turn = grad + MOMENTUM * moment
+    small[...] = jnp.zeros_like(small)
+    small[:16, :SMALL_LANES] = turn * lax.rsqrt(
+        jnp.sum(jnp.sum(turn * turn, axis=1, keepdims=True), axis=0, keepdims=True) + NORM_EPS
+    )
+    grad = jnp.concatenate([tiles[14][:, :C1], tiles[14][:, C1:]], axis=0)
+    moment = MOMENTUM * stemm_ref[...] + grad
+    nstemm_ref[...] = moment
+    turn = grad + MOMENTUM * moment
+    small[32:, SMALL_LANES:] = turn * lax.rsqrt(
+        jnp.sum(jnp.sum(turn * turn, axis=1, keepdims=True), axis=0, keepdims=True) + NORM_EPS
+    )
+    gram = lax.dot_general(
+        small[...],
+        small[...],
+        (((1,), (1,)), ((), ())),
+        preferred_element_type=F32,
+        precision=EXACT_PRECISION,
+    )
+    product = ns_chain(gram, identity(64))
+    turned = dot_nn(product, small[...], EXACT_PRECISION)
+    keep = 1.0 - LR_MUON * DECAY
+    nhead_ref[...] = head_ref[...] * keep - LR_MUON * turned[:16, :SMALL_LANES]
+    nstem_ref[...] = stem_ref[...] * keep - LR_MUON * turned[32:, SMALL_LANES:]
+
+    for copy in copies:
+        copy.wait_recv()
+    gram_all[own_part, :] = sum([gram_recv[k] for k in range(1, owners)], gram_recv[0])
+    copies = [
+        send(gram_all.at[own_part, :], gram_all.at[own_part, :], semh, k - 1, along(k))
+        for k in range(1, owners)
+    ]
+    for copy in copies:
+        copy.wait_recv()
+    gram = gram_all[...]
+    eye = identity(mid)
+    trace = jnp.sum(jnp.sum(gram * eye, axis=1, keepdims=True), axis=0, keepdims=True)
+    scale = lax.rsqrt(trace + NORM_EPS)
+    product = ns_chain(gram * (scale * scale), eye) * scale
+    turned = dot_nn(mine_u[...], product, EXACT_PRECISION)
+
+    place = lax.rem(chip, 4)
+    base = chip - place
+
+    def in_group(k):
+        return {"batch": (base + lax.rem(place + k, 4)) * 2 + core}
+
+    for task_core, buffer in ((0, x_zero), (1, x_one)):
+
+        @pl.when(core == task_core)
+        def _(buffer=buffer, other_buffer=(x_one, x_zero)[task_core]):
+            size = buffer.shape[1]
+            buffer[place] = turned[:size].astype(LOWTYPE)
+            here = buffer.at[place]
+            plane = [send(here, here, semx, k - 1, in_group(k), False) for k in range(1, 4)]
+            cross = [send(here, here, semy, 0, partner, False)]
+            for k in range(1, 4):
+                plane[k - 1].wait_recv()
+                other = buffer.at[lax.rem(place + 4 - k, 4)]
+                cross.append(send(other, other, semy, k, partner, False))
+            for k in range(4):
+                there = other_buffer.at[lax.rem(place + 4 - k, 4)]
+                pltpu.make_async_remote_copy(
+                    src_ref=there,
+                    dst_ref=there,
+                    send_sem=semy.at[0, k],
+                    recv_sem=semy.at[1, k],
+                    device_id=partner,
+                    device_id_type=MESH,
+                ).wait_recv()
+            for copy in plane + cross:
+                copy.wait_send()
+
+    for (task_chip, task_core), share, start in zip(TASKS, shares, starts):
+        buffer = (x_zero, x_one)[task_core]
+        rows = slice(start, start + share)
+        fresh = weight_ref[rows, :] * keep - LR_MUON * buffer[task_chip, :share, :].astype(F32)
+        new_ref[rows, :] = fresh
+        copy_ref[rows, :] = fresh.astype(LOWTYPE)
+    for copy in started:
+        copy.wait_send()
+
+
+def muon_call(owners, peers, operands):
+    mid = CHANNELS_MID
+    chips = peers // 2
+    chunk, small_chunk = chunk_rows(owners, peers)
+    block = block_rows(owners, peers)
+    rows = operands[2].shape[0]
+    part = mid // owners
+    shares = [seg_rows // owners for seg_rows in segment_rows()]
+    most = [max(s for s, t in zip(shares, TASKS) if t[1] == core) for core in (0, 1)]
+    out_shapes = [
+        ((rows, mid), F32),
+        ((rows, mid), F32),
+        ((rows, mid), LOWTYPE),
+        (operands[4].shape, F32),
+        (operands[4].shape, F32),
+        (operands[6].shape, F32),
+        (operands[6].shape, F32),
+        (operands[8].shape, F32),
+        (operands[8].shape, F32),
+        (operands[8].shape, F32),
+        ((8, C1), F32),
+    ]
+    scratch = [
+        ((chips, block, mid), F32),
+        ((block, mid), F32),
+        ((chips - 1, block, mid), F32),
+        ((chips - 1, block, mid), F32),
+        ((owners - 1, chunk, mid), F32),
+        ((owners - 1, chunk, mid), F32),
+        ((owners, small_chunk, mid), F32),
+        ((peers, chunk + small_chunk, mid), F32),
+        (operands[1].shape, F32),
+        ((chips,) + operands[1].shape, F32),
+        ((owners,) + operands[1].shape, F32),
+        ((rows, mid), F32),
+        ((max(most), mid), F32),
+        ((mid, mid), F32),
+        ((owners, part, mid), F32),
+        ((mid, mid), F32),
+        ((64, SMALL_LANES + C1), F32),
+        ((4, most[0], mid), LOWTYPE),
+        ((4, most[1], mid), LOWTYPE),
+    ]
+    sems = [
+        chips,
+        chips - 1,
+        owners - 1,
+        owners - 1,
+        chips - 1,
+        chips,
+        owners - 1,
+        owners - 1,
+        3,
+        4,
+        1,
+        chips - 1,
+        owners - 1,
+    ]
+    vmem = pl.BlockSpec(memory_space=pltpu.VMEM)
+    return pl.pallas_call(
+        functools.partial(muon_body, owners, peers),
+        out_shape=[jax.ShapeDtypeStruct(shape, kind) for shape, kind in out_shapes],
+        in_specs=[vmem] * len(operands),
+        out_specs=[vmem] * len(out_shapes),
+        scratch_shapes=[pltpu.VMEM(shape, kind) for shape, kind in scratch]
+        + [pltpu.SemaphoreType.DMA((2, count)) for count in sems],
+        compiler_params=pltpu.CompilerParams(
+            vmem_limit_bytes=VMEM_BYTES, collective_id=0, has_side_effects=True
+        ),
     )(*operands)
 
 
@@ -562,10 +1075,10 @@
                 tap = 2 * (block - 1) + inner - sub + 1
                 if 0 <= tap <= 2:
                     counts[block, inner, tap] += 1
-    full = np.zeros((3, 3, 4, 4, 3, 3, 3))
+    full = np.zeros((3, 3, ROWS12, 3, 3, 3))
+    both = (np.einsum("ayt,bxu->abyxtu", counts, counts) * 0.25).reshape(3, 3, 4, 3, 3)
     for c in range(3):
-        both = np.einsum("ayt,bxu->abyxtu", counts, counts) * 0.25
-        full[:, :, c, :, :, :, c] = both.reshape(3, 3, 4, 3, 3)
+        full[:, :, c:12:3, :, :, c] = both
     return jnp.asarray(full.reshape(TAPS * ROWS12, 27), F32)
 
 
@@ -580,6 +1093,11 @@
     return jnp.pad(values, [(0, 0)] * (values.ndim - 2) + [(0, rows - values.shape[-2]), (0, 0)])
 
 
+def lanes_of(vector):
+    rows = -(-vector.shape[0] // (8 * C1)) * 8
+    return jnp.pad(vector, (0, rows * C1 - vector.shape[0]), constant_values=1.0).reshape(rows, C1)
+
+
 def by_column(weights, chans):
     return weights.reshape(3, 3 * chans, CHANNELS_MID).transpose(1, 0, 2).reshape(3 * chans, -1)
 
@@ -588,35 +1106,6 @@
     group = np.arange(chans) // (chans // GROUPS)
     same = (group[:, None] == group[None, :]) / (PLACES * (chans // GROUPS))
     return jnp.asarray(same, F32)
-
-
-def ns_update(iterate, gram):
-    inner = NS_B * gram + NS_C * jnp.dot(gram, gram, precision=EXACT_PRECISION)
-    return NS_A * iterate + jnp.dot(iterate, inner, precision=EXACT_PRECISION)
-
-
-def local_muon(weight_m, moment, gradient):
-    moment_new = MOMENTUM * moment + gradient
-    direction = gradient + MOMENTUM * moment_new
-    iterate = direction * lax.rsqrt(jnp.sum(direction * direction) + NORM_EPS)
-    for step in range(NS_STEPS):
-        iterate = ns_update(iterate, jnp.dot(iterate.T, iterate, precision=EXACT_PRECISION))
-    return (weight_m * (1.0 - LR_MUON * DECAY) - LR_MUON * iterate, moment_new)
-
-
-def ns_product(gram):
-    eye = jnp.eye(gram.shape[0], dtype=jnp.float32)
-    product = None
-    for step in range(NS_STEPS):
-        square = jnp.dot(gram, gram, precision=EXACT_PRECISION)
-        factor = NS_A * eye + NS_B * gram + NS_C * square
-        product = (
-            factor if product is None else jnp.dot(product, factor, precision=EXACT_PRECISION)
-        )
-        if step < NS_STEPS - 1:
-            half = jnp.dot(gram, factor, precision=EXACT_PRECISION)
-            gram = jnp.dot(factor, half, precision=EXACT_PRECISION)
-    return product
 
 
 def shards(
@@ -634,13 +1123,11 @@
     vector_firsts,
     vector_seconds,
 ):
-    owners = lax.axis_size("bucket")
+    owners, peers = lax.axis_size("bucket"), lax.axis_size("batch")
     gathered = lax.all_gather(matrices.astype(LOWTYPE), "bucket", axis=0, tiled=True)
     conv_one, conv_two, skip_w, temb_w, query_w, key_w, value_w, out_w = unpack(gathered, owners)
     samples = images.shape[0]
     level, weight = plan(timesteps)
-    counts = jnp.sum(pixel_mask.astype(jnp.float32), axis=1)
-    weight_local = jnp.sum(3.0 * weight * counts)
     noisy = (
         jnp.sqrt(level)[:, None, None] * images + jnp.sqrt(1.0 - level)[:, None, None] * noise_field
     )
@@ -656,10 +1143,12 @@
     order = (phase_order()[:, None] == jnp.arange(S * S, dtype=jnp.int32)[None, :]).astype(F32)
     phased = jnp.dot(rows, order, precision=EXACT_PRECISION)
     planes = 3 * samples
-    noisy_low = pad_rows(phased[:planes].reshape(samples, 12, PLACES), ROWS12).astype(LOWTYPE)
-    noise_planes = pad_rows(phased[planes : 2 * planes].reshape(samples, 12, PLACES), ROWS12)
+    pictures = phased[: 2 * planes].reshape(2, samples, 3, 4, PLACES).transpose(0, 1, 3, 2, 4)
+    pictures = pad_rows(pictures.reshape(2, samples, 12, PLACES), ROWS12)
+    noisy_low = pictures[0].astype(LOWTYPE)
+    noise_planes = pictures[1]
     mask_planes = jnp.broadcast_to(
-        phased[2 * planes :].reshape(samples, 1, 4, PLACES), (samples, 3, 4, PLACES)
+        phased[2 * planes :].reshape(samples, 4, 1, PLACES), (samples, 4, 3, PLACES)
     ).reshape(samples, 12, PLACES)
     mask_planes = pad_rows(mask_planes, ROWS12)
     time_in = pad_rows(swish(embed(timesteps)).astype(LOWTYPE), -(-samples // 16) * 16)
@@ -667,22 +1156,15 @@
     stem_blocks = split_three(
         jnp.dot(spread, lax.reduce_precision(stem_weight, 8, 7), precision=EXACT_PRECISION)
     )
-    head_rows = head_weight.astype(LOWTYPE).reshape(TAPS, CHANNELS_MID + C1, 4, 3)
-    head_rows = pad_rows(
-        head_rows.transpose(0, 3, 2, 1).reshape(TAPS, 12, CHANNELS_MID + C1), ROWS12
-    ).reshape(TAPS * ROWS12, -1)
-    vec_rows = jnp.concatenate(
-        [
-            jnp.pad(vectors[: 3 * C1].reshape(3, C1), ((0, 0), (0, CHANNELS_MID - C1))),
-            vectors[3 * C1 : -12].reshape(10, CHANNELS_MID),
-        ],
-        axis=0,
-    )
-    head_bias = jnp.broadcast_to(
-        pad_rows(vectors[-12:].reshape(4, 3).T.reshape(12, 1), ROWS12), (ROWS12, C1)
-    )
-    acc, gstem_rows, ghead_rows, gvec, ghead_bias, loss_rows = unet_call(
+    head_turned = head_weight.T
+    head_rows = head_turned.astype(LOWTYPE).reshape(12, TAPS, CHANNELS_MID + C1)
+    head_rows = pad_rows(head_rows.transpose(1, 0, 2), ROWS12).reshape(TAPS * ROWS12, -1)
+    vec_rows = lanes_of(vectors)
+    head_bias = jnp.broadcast_to(pad_rows(vectors[-12:].reshape(12, 1), ROWS12), (ROWS12, C1))
+    rows_out, misc = unet_call(
         samples,
+        owners,
+        peers,
         [
             noisy_low,
             noise_planes,
@@ -698,84 +1180,55 @@
             temb_w,
             jnp.concatenate([query_w, key_w, value_w], axis=1),
             out_w,
-            pad_rows(vec_rows, ROWS12),
+            vec_rows,
             head_bias,
             same_group(C1),
             same_group(CHANNELS_MID),
+            jnp.pad(spread, ((0, 0), (0, 5))),
         ],
     )
-    loss_local = jnp.sum(loss_rows)
-    g_stem = jnp.dot(spread.T, gstem_rows, precision=EXACT_PRECISION)
-    g_head = (
-        ghead_rows.reshape(TAPS, ROWS12, -1)[:, :12]
-        .reshape(TAPS, 3, 4, CHANNELS_MID + C1)
-        .transpose(0, 3, 2, 1)
-        .reshape(-1, 12)
-    )
-    grad_vec = jnp.concatenate(
+    (
+        new_matrices,
+        new_matrix_moms,
+        matrix_copies,
+        new_stem,
+        new_stem_moms,
+        new_head,
+        new_head_moms,
+        new_vec,
+        new_first,
+        new_second,
+        sums,
+    ) = muon_call(
+        owners,
+        peers,
         [
-            gvec[:3, :C1].reshape(-1),
-            gvec[3:13].reshape(-1),
-            jnp.sum(ghead_bias[:12], axis=1).reshape(3, 4).T.reshape(-1),
-        ]
-    )
-    natural = acc.T
-    grad_pack = pack([natural[a:b] for a, b in zip(SEG_OFF[:-1], SEG_OFF[1:])], owners)
-    rows_dev = matrices.shape[0]
-    summed, grad_stem, grad_headw, grad_vec, loss_sum, weight_sum = lax.psum(
-        (grad_pack, g_stem, g_head, grad_vec, loss_local, weight_local), ("bucket", "batch")
-    )
-    inverse = 1.0 / weight_sum
-    summed = summed * inverse
-    grad_stem = grad_stem * inverse
-    grad_headw = grad_headw * inverse
-    grad_vec = grad_vec * inverse
-    grad_mine = lax.dynamic_slice_in_dim(summed, lax.axis_index("bucket") * rows_dev, rows_dev, 0)
-    shares = [seg_rows // owners for seg_rows in segment_rows()]
-    weight_parts, moment_parts, grad_parts = ([], [], [])
-    start = 0
-    for share in shares:
-        weight_parts.append(matrices[start : start + share])
-        moment_parts.append(matrix_moms[start : start + share])
-        grad_parts.append(grad_mine[start : start + share])
-        start += share
-    moments_new = [
-        MOMENTUM * moment + gradient for moment, gradient in zip(moment_parts, grad_parts)
-    ]
-    directions = [gradient + MOMENTUM * moment for gradient, moment in zip(grad_parts, moments_new)]
-    gram_sums = lax.psum(
-        tuple(jnp.dot(d.T, d, precision=EXACT_PRECISION) for d in directions), "bucket"
-    )
-    iterates = []
-    for direction, gram in zip(directions, gram_sums):
-        scale = lax.rsqrt(jnp.trace(gram) + NORM_EPS)
-        iterates.append(
-            jnp.dot(direction * scale, ns_product(gram * (scale * scale)), precision=EXACT_PRECISION)
-        )
-    new_matrices = jnp.concatenate(
-        [
-            weight_m * (1.0 - LR_MUON * DECAY) - LR_MUON * iterate
-            for weight_m, iterate in zip(weight_parts, iterates)
+            rows_out,
+            misc,
+            matrices,
+            matrix_moms,
+            pad_rows(stem_weight, 32),
+            pad_rows(stem_moms, 32),
+            pad_rows(head_turned, ROWS12),
+            pad_rows(head_moms.T, ROWS12),
+            vec_rows,
+            lanes_of(vector_firsts),
+            lanes_of(vector_seconds),
         ],
-        axis=0,
-    )
-    new_matrix_moms = jnp.concatenate(moments_new, axis=0)
-    new_stem, new_stem_moms = local_muon(stem_weight, stem_moms, grad_stem)
-    new_head, new_head_moms = local_muon(head_weight, head_moms, grad_headw)
-    new_firsts = BETA_ONE * vector_firsts + (1.0 - BETA_ONE) * grad_vec
-    new_seconds = BETA_TWO * vector_seconds + (1.0 - BETA_TWO) * grad_vec * grad_vec
-    step_dir = (
-        new_firsts
-        / (1.0 - BETA_ONE**STEP)
-        / (jnp.sqrt(new_seconds / (1.0 - BETA_TWO**STEP)) + ADAM_EPS)
-    )
-    new_vectors = vectors - LR_ADAM * step_dir
+    )
+    count = vectors.shape[0]
+    new_stem, new_stem_moms = new_stem[:27], new_stem_moms[:27]
+    new_head, new_head_moms = new_head[:12].T, new_head_moms[:12].T
+    new_vectors = new_vec.reshape(-1)[:count]
+    new_firsts = new_first.reshape(-1)[:count]
+    new_seconds = new_second.reshape(-1)[:count]
+    loss_sum, weight_sum = sums[0, 0], sums[0, 1]
     return (
         loss_sum,
         weight_sum,
         new_matrices,
         new_matrix_moms,
-        new_matrices.astype(LOWTYPE),
+        matrix_copies,
         new_stem,
         new_stem_moms,
         new_stem.astype(LOWTYPE),

time: 660 us -> 340 us (0.52)
  waiting for transfers between devices: 276 us -> 44.3 us
  Pallas kernels: 133 us -> 239 us
  matrix products: 96.9 us -> 1.95 us
  blocking collectives: 40 us -> 0 us
  local copies, waits for them, and re-layouts: 58.6 us -> 30.9 us
  other arithmetic: 24.6 us -> 8.67 us
  between operations: 23.9 us -> 14.4 us
    psum x2 -> x0, waiting for transfers between devices: 228 us -> none  [the longest x1 145 us: shards(): lax.psum((grad_pack, g_stem, g_head, grad_vec, loss_local, weight_local),...]
    pallas_call x1 -> x2, Pallas kernels: 133 us -> 239 us  [the longest x1 134 us: unet_call(): pl.pallas_call(functools.partial(unet_body, group, steps, owners, peers),...]
    dot_general x183 -> x0, matrix products: 95 us -> none  [the longest x32 20.5 us: ns_product(): half = jnp.dot(gram, factor, precision=EXACT_PRECISION)]
    psum x1 -> x0, blocking collectives: 40 us -> none  [shards(): lax.psum((grad_pack, g_stem, g_head, grad_vec, loss_local, weight_local),...]
    slice x18 -> x3, local copies, waits for them, and re-layouts: 20.7 us -> 1.38 us  [the longest x1 1.34 us: shards(): loss_sum, weight_sum = (sums[0, 0], sums[0, 1])]
    reduce_sum x10 -> x0, other arithmetic: 10.5 us -> none  [the longest x4 3.73 us: shards(): scale = lax.rsqrt(jnp.trace(gram) + NORM_EPS)]
  transfers between devices with their start and end apart: 3 -> 1, of which waited for: 3 -> 1; matrix products, arithmetic and copies ran while one was open for 3% -> 4% of each run, Pallas kernels for 0% -> 0%
where the time goes in v3:
time: 340 us
  Pallas kernels  239 us (70%)
  waiting for transfers between devices  44.3 us (13%)
  local copies, waits for them, and re-layouts  30.9 us (9%)
  between operations  14.4 us (4%)
  other arithmetic  8.67 us (3%)
    pallas_call x1, Pallas kernels, unet_call(): pl.pallas_call(functools.partial(unet_body, group, steps, owners, peers),...  134 us
    pallas_call x1, Pallas kernels, muon_call(): pl.pallas_call(functools.partial(muon_body, owners, peers), out_shape=[ja...  105 us
    all_gather x1, waiting for transfers between devices, shards(): lax.all_gather(matrices.astype(LOWTYPE), 'bucket', axis=0, tiled=True)  44.3 us
    unnamed x48, local copies, waits for them, and re-layouts  7.99 us
    slice x5, local copies, waits for them, and re-layouts, unpack(): blocks[:, start:start + share, :].reshape(seg_rows, packed.shape[1])  7.97 us
  transfers between devices with their start and end apart: 1, of which 1 were waited for; matrix products, arithmetic and copies ran while one was open for 4% of the time, Pallas kernels for 0%

profile of v3, /device:TPU:0, one launch (start us, length us, event | category | flops | bytes accessed | tf_op | source)
XLA Modules:
  0.0 339.5 jit_solution(15588943627874565829)
XLA Ops:
  7.3 2.3 convert_element_type.53
  10.8 1.7 fusion
  13.5 0.7 copy-done.4
  14.6 0.6 pad.50.time_ref
  15.2 0.7 pad.51.clone
  15.9 0.8 pad.49.maskw_ref
  16.7 0.7 pad.57.head_ref
  17.4 0.7 pad.58.headm_ref
  18.1 0.6 pad.55.stem_ref
  21.4 0.7 pad_maximum_fusion.1.stemw_ref
  22.0 0.7 fusion.8.noisy_ref
  22.7 0.8 fusion.7.noise_ref
  23.5 44.3 %all-gather.2.cloned.1.call-done = bf16[5120,256]{1,0:T(8,128)(2,1)} async-done(((bf16[1280,256]{1,0:T(8,128)(2,1)}), bf16[5120,256]{1,0:T(8,128)(2,1)}) %all-gather.2.cloned.1.call-update) | async-done | bytes 2621456 | tf_op jit(solution)/shard_map/all_gather | solution.py:1127
  67.7 1.8 fusion.18
  69.5 1.3 slice.92
  70.9 1.5 slice.91
  72.4 1.9 slice.94
  74.3 1.5 slice.93
  75.7 0.7 copy.53
  76.5 1.5 copy.55.conv2b_ref
  78.2 1.1 copy.54.conv1b_ref
  79.3 0.8 pad_maximum_fusion.qkv_ref
  80.1 0.7 broadcast_in_dim.11.headb_ref
  80.8 134.0 %shard_map.280 = (f32[5376,256]{1,0:T(8,128)}, f32[16,384]{1,0:T(8,128)}) custom-call(bf16[20,16,256]{2,1,0:T(8,128)(2,1)} %fusion.8.noisy_ref, f32[20,16,256]{2,1,0:T(8,128)} %fusion.7.noise_ref, f32[20,16,256]{2,1,0:T(8,128)} %pad.49.maskw_ref, bf16[32,512]{1,0:T(8,128)(2,1)} %pad.50.time_ref, bf16[144,384]{1,0:T(8,128)(2,1)} %pad_maximum_fusion.1.stemw_ref, ...), custom_call_target="tpu_custom_call" | custom-call | tf_op jit(solution)/shard_map/pallas_call | solution.py:623
  214.8 105.3 %shard_map.281 = (f32[1280,256]{1,0:T(8,128)}, f32[1280,256]{1,0:T(8,128)}, bf16[1280,256]{1,0:T(8,128)(2,1)}, f32[32,128]{1,0:T(8,128)}, f32[32,128]{1,0:T(8,12...) custom-call(f32[5376,256]{1,0:T(8,128)} %get-tuple-element.28.rows_r, ...), custom_call_target="tpu_custom_call" | custom-call | tf_op jit(solution)/shard_map/pallas_call | solution.py:1050
  320.1 1.3 fusion.16
  321.4 1.3 fusion.14
  322.7 1.3 fusion.19
  324.0 1.9 fusion.15
  325.9 2.6 copy.63
  328.5 1.1 copy.64
  330.0 0.8 copy.65
  (76 shorter events, 7.7 us)
Async XLA Ops:
  7.2 2.4 copy-start.3
  7.2 2.6 copy-start.18
  7.2 2.6 copy-start.6
  7.2 60.5 %all-gather.2.cloned.1.call-start = ((), (), s32[]{:S(2)}) async-start(), calls=%async_computation | async-start | bytes 3276800 | tf_op jit(solution)/shard_map/all_gather | solution.py:1127
  9.8 0.9 copy-start.8
  9.8 1.0 copy-start.19
  13.3 0.9 copy-start.4
  14.2 3.2 copy-start.7
  14.2 3.9 %copy-start.10 = (f32[27,128]{1,0:T(8,128)S(1)}, f32[27,128]{1,0:T(8,128)}, u32[]{:S(2)}) copy-start(f32[27,128]{1,0:T(8,128)} %param.23) | copy-start | bytes 41476
  14.2 4.5 %copy-start.11 = (f32[27,128]{1,0:T(8,128)S(1)}, f32[27,128]{1,0:T(8,128)}, u32[]{:S(2)}) copy-start(f32[27,128]{1,0:T(8,128)} %param.24) | copy-start | bytes 41476
  14.2 5.1 %copy-start.13 = (f32[2956]{0:T(1024)S(1)}, f32[2956]{0:T(1024)}, u32[]{:S(2)}) copy-start(f32[2956]{0:T(1024)} %param.27) | copy-start | bytes 35476
  14.3 5.7 %copy-start.14 = (f32[2956]{0:T(1024)S(1)}, f32[2956]{0:T(1024)}, u32[]{:S(2)}) copy-start(f32[2956]{0:T(1024)} %param.29) | copy-start | bytes 35476
  14.3 6.3 %copy-start.15 = (f32[2956]{0:T(1024)S(1)}, f32[2956]{0:T(1024)}, u32[]{:S(2)}) copy-start(f32[2956]{0:T(1024)} %param.28) | copy-start | bytes 35476
  14.3 6.9 %copy-start.9 = (f32[144,27]{1,0:T(8,128)S(1)}, f32[144,27]{1,0:T(8,128)}, u32[]{:S(2)}) copy-start(f32[144,27]{1,0:T(8,128)} %constant.35.clone) | copy-start | bytes 46660
  70.9 5.6 %copy-start = (bf16[4,576,256]{2,1,0:T(8,128)(2,1)}, bf16[4,576,256]{2,1,0:T(8,128)(2,1)S(1)}, u32[]{:S(2)}) copy-start(bf16[4,576,256]{2,1,0:T(8,128)(2,1)S(1)} %slice.92) | copy-start | bytes 3538948
  72.4 5.5 %copy-start.1 = (bf16[4,288,256]{2,1,0:T(8,128)(2,1)}, bf16[4,288,256]{2,1,0:T(8,128)(2,1)S(1)}, u32[]{:S(2)}) copy-start(bf16[4,288,256]{2,1,0:T(8,128)(2,1)S(1)} %slice.91) | copy-start | bytes 1769476
  325.9 2.6 copy-start.2
  328.5 1.5 copy-start.5
  330.0 0.8 copy-start.12
  330.0 1.5 copy-start.17
  330.0 2.1 copy-start.16
Sparse Core Ops, SparseCore 0:
  10.2 57.4 all-gather.1

commit v4 on v3

--- a/solution.py
+++ b/solution.py
@@ -169,6 +169,7 @@
     qkv,
     plow,
     attl,
+    low0,
     joined,
     patch,
     pad1,
@@ -180,6 +181,10 @@
     dpool,
     tproj,
     gtime,
+    dtap,
+    datt,
+    dscore,
+    dpool_low,
 ):
     step = pl.program_id(0)
     mid = CHANNELS_MID
@@ -217,7 +222,11 @@
 
     def grouped(stats, chans):
         same = same128_ref if chans == C1 else same256_ref
-        return dot_nn(stats, same[...], precision=EXACT_PRECISION)
+        first = stats.astype(LOWTYPE).astype(F32)
+        second = (stats - first).astype(LOWTYPE).astype(F32)
+        third = stats - first - second
+        sums = dot_nn(jnp.concatenate([first, second, third], axis=0).astype(LOWTYPE), same[...])
+        return sums[:group] + sums[group : 2 * group] + sums[2 * group :]
 
     def gn_stats(ref, sums, chans):
         mean = grouped(sums, chans)
@@ -234,21 +243,18 @@
         col = lax.broadcasted_iota(jnp.int32, (CHUNK, chans), 0) % SIDE
         return (col > 0) if left else (col < SIDE - 1)
 
-    def act_shift(ref, mean, rstd, gain, shift, dest, chans):
-        for g in images:
-            for r in chunks:
-                y = (ref[g, r : r + CHUNK, :] - mean[g : g + 1]) * rstd[g : g + 1] * gain + shift
-                a = y * sigmoid(y)
-                shiftf[g, 8 + r : 8 + r + CHUNK, :chans] = a
-                dest[g, SIDE + r : SIDE + r + CHUNK, chans : 2 * chans] = a.astype(LOWTYPE)
-            for r in chunks:
-                before = shiftf[g, 7 + r : 7 + r + CHUNK, :chans]
-                after = shiftf[g, 9 + r : 9 + r + CHUNK, :chans]
-                rows = slice(SIDE + r, SIDE + r + CHUNK)
-                dest[g, rows, :chans] = jnp.where(edge(chans, True), before, 0.0).astype(LOWTYPE)
-                dest[g, rows, 2 * chans :] = jnp.where(edge(chans, False), after, 0.0).astype(
-                    LOWTYPE
-                )
+    def act_shift(ref, g, mean, rstd, gain, shift, dest, chans):
+        for r in chunks:
+            y = (ref[g, r : r + CHUNK, :] - mean[g : g + 1]) * rstd[g : g + 1] * gain + shift
+            a = y * sigmoid(y)
+            shiftf[g, 8 + r : 8 + r + CHUNK, :chans] = a
+            dest[g, SIDE + r : SIDE + r + CHUNK, chans : 2 * chans] = a.astype(LOWTYPE)
+        for r in chunks:
+            before = shiftf[g, 7 + r : 7 + r + CHUNK, :chans]
+            after = shiftf[g, 9 + r : 9 + r + CHUNK, :chans]
+            rows = slice(SIDE + r, SIDE + r + CHUNK)
+            dest[g, rows, :chans] = jnp.where(edge(chans, True), before, 0.0).astype(LOWTYPE)
+            dest[g, rows, 2 * chans :] = jnp.where(edge(chans, False), after, 0.0).astype(LOWTYPE)
 
     def dy_cat(ref, g, order):
         return jnp.concatenate(
@@ -258,101 +264,138 @@
     def stack(parts):
         return jnp.concatenate(parts, axis=0) if len(parts) > 1 else parts[0]
 
-    for g in images:
+    def staged(stages, fillers=()):
+        fillers = list(fillers)
+        for stage in stages:
+            for g in images:
+                stage(g)
+            if fillers:
+                fillers.pop(0)()
+        for filler in fillers:
+            filler()
+
+    def rows_of(g):
+        return slice(g * PLACES, (g + 1) * PLACES)
+
+    sums1 = [None] * group
+
+    def stem_patch(g):
         noisy = noisy_ref[g].astype(F32)
         for tap, (di, dj) in enumerate(tap_offsets()):
             patch[g, tap * ROWS12 : (tap + 1) * ROWS12, :] = shift_lanes(noisy, di, dj).astype(
                 LOWTYPE
             )
-    sums = []
-    for g in images:
+
+    def stem_pool(g):
         wide = dot_tn(patch[g], stemw_ref[...])
         acc = jnp.zeros((8, C1), F32)
         for r in chunks:
             w = wide[r : r + CHUNK]
             v = (w[:, :C1] + w[:, C1 : 2 * C1]) + w[:, 2 * C1 :] + vec(0, C1)
             x0[g, r : r + CHUNK, :] = v
+            low0[g * PLACES + r : g * PLACES + r + CHUNK, :] = v.astype(LOWTYPE)
             acc += fold8(v)
-        sums.append(acc)
-    mean1, rstd1 = gn_stats(x0, total(sums), C1)
+        sums1[g] = acc
+
+    staged([stem_patch, stem_pool])
+    mean1, rstd1 = gn_stats(x0, total(sums1), C1)
     gain1, shift1 = vec(1, C1), vec(2, C1)
-    act_shift(x0, mean1, rstd1, gain1, shift1, a1, C1)
-
-    wide = dot_nn(stack([dy_cat(a1, g, (0, 1, 2)) for g in images]), conv1_ref[...])
-    sums = []
-    for g in images:
+
+    sums2 = [None] * group
+
+    def act_one(g):
+        act_shift(x0, g, mean1, rstd1, gain1, shift1, a1, C1)
+
+    def conv_one(g):
+        wide = dot_nn(dy_cat(a1, g, (0, 1, 2)), conv1_ref[...])
         bias = vec(3) + vec(4) + tproj[pl.ds(step * group + g, 1), :]
         acc = jnp.zeros((8, mid), F32)
         for r in chunks:
-            v = wide[g * PLACES + r : g * PLACES + r + CHUNK] + bias
+            v = wide[r : r + CHUNK] + bias
             hid[g, r : r + CHUNK, :] = v
             acc += fold8(v)
-        sums.append(acc)
-    mean2, rstd2 = gn_stats(hid, total(sums), mid)
+        sums2[g] = acc
+
+    staged([act_one, conv_one])
+    mean2, rstd2 = gn_stats(hid, total(sums2), mid)
     gain2, shift2 = vec(5), vec(6)
-    act_shift(hid, mean2, rstd2, gain2, shift2, a2, mid)
-
-    wide = dot_nn(stack([dy_cat(a2, g, (0, 1, 2)) for g in images]), conv2_ref[...])
-    low0 = stack([x0[g].astype(LOWTYPE) for g in images])
-    wide = wide + dot_nn(low0, skip_ref[...])
-    sums = []
-    for g in images:
+
+    sums3 = [None] * group
+
+    def act_two(g):
+        act_shift(hid, g, mean2, rstd2, gain2, shift2, a2, mid)
+
+    def conv_two(g):
+        wide = dot_nn(dy_cat(a2, g, (0, 1, 2)), conv2_ref[...])
+        wide = wide + dot_nn(low0[rows_of(g), :], skip_ref[...])
         acc = jnp.zeros((8, mid), F32)
         for r in chunks:
-            v = wide[g * PLACES + r : g * PLACES + r + CHUNK] + vec(7)
+            v = wide[r : r + CHUNK] + vec(7)
             res[g, r : r + CHUNK, :] = v
             acc += fold8(v)
-        sums.append(acc)
-    mean3, rstd3 = gn_stats(res, total(sums), mid)
+        sums3[g] = acc
+
+    staged([act_two, conv_two])
+    mean3, rstd3 = gn_stats(res, total(sums3), mid)
     gain3, shift3 = vec(8), vec(9)
-    for g in images:
+    scale = mid ** (-0.5)
+    ones3, twos3 = [None] * group, [None] * group
+
+    def norm_three(g):
         for r in chunks:
-            y = (res[g, r : r + CHUNK, :] - mean3[g : g + 1]) * rstd3[g : g + 1] * gain3 + shift3
+            xh = (res[g, r : r + CHUNK, :] - mean3[g : g + 1]) * rstd3[g : g + 1]
+            y = xh * gain3 + shift3
             normed[g * PLACES + r : g * PLACES + r + CHUNK, :] = y.astype(LOWTYPE)
 
-    wide = dot_nn(normed[...], qkv_ref[...])
-    qkv[:, :mid] = (wide[:, :mid] + vec(10)).astype(LOWTYPE)
-    qkv[:, mid : 2 * mid] = wide[:, mid : 2 * mid].astype(LOWTYPE)
-    qkv[:, 2 * mid :] = (wide[:, 2 * mid :] + vec(11)).astype(LOWTYPE)
-    scale = mid ** (-0.5)
-    for g in images:
-        rows = slice(g * PLACES, (g + 1) * PLACES)
+    def project(g):
+        rows = rows_of(g)
+        wide = dot_nn(normed[rows, :], qkv_ref[...])
+        qkv[rows, :mid] = (wide[:, :mid] + vec(10)).astype(LOWTYPE)
+        qkv[rows, mid : 2 * mid] = wide[:, mid : 2 * mid].astype(LOWTYPE)
+        qkv[rows, 2 * mid :] = (wide[:, 2 * mid :] + vec(11)).astype(LOWTYPE)
+
+    def weigh(g):
+        rows = rows_of(g)
         logits = dot_nt(qkv[rows, :mid], qkv[rows, mid : 2 * mid])
         for r in chunks:
             s = logits[r : r + CHUNK] * scale
             e = jnp.exp(s - jnp.max(s, axis=1, keepdims=True))
-            p = e / jnp.sum(e, axis=1, keepdims=True)
+            p = e * (1.0 / jnp.sum(e, axis=1, keepdims=True))
             attn[g, r : r + CHUNK, :] = p
             plow[g, r : r + CHUNK, :] = p.astype(LOWTYPE)
-        attl[rows, :] = dot_nn(plow[g], qkv[rows, 2 * mid :]).astype(LOWTYPE)
-    wide = dot_nn(attl[...], outw_ref[...])
-    for g in images:
+
+    def attend(g):
+        attl[rows_of(g), :] = dot_nn(plow[g], qkv[rows_of(g), 2 * mid :]).astype(LOWTYPE)
+
+    def join(g):
+        wide = dot_nn(attl[rows_of(g), :], outw_ref[...])
         for r in chunks:
             rows = slice(g * PLACES + r, g * PLACES + r + CHUNK)
-            o = res[g, r : r + CHUNK, :] + wide[rows] + vec(12)
+            o = res[g, r : r + CHUNK, :] + wide[r : r + CHUNK] + vec(12)
             outp[g, r : r + CHUNK, :] = o
             joined[rows, :mid] = (o * sigmoid(o)).astype(LOWTYPE)
             x = x0[g, r : r + CHUNK, :]
             joined[rows, mid:] = (x * sigmoid(x)).astype(LOWTYPE)
 
-    for g in images:
-        rows = slice(g * PLACES, (g + 1) * PLACES)
-        taps = dot_nt(headw_ref[...], joined[rows, :])
-        head = headb_ref[:, :1] + jnp.zeros((ROWS12, PLACES), F32)
+    def head(g):
+        taps = dot_nt(headw_ref[...], joined[rows_of(g), :])
+        value = headb_ref[:, :1] + jnp.zeros((ROWS12, PLACES), F32)
         for tap, (di, dj) in enumerate(tap_offsets()):
-            head = head + shift_lanes(taps[tap * ROWS12 : (tap + 1) * ROWS12, :], di, dj)
-        error = head - noise_ref[g]
+            value = value + shift_lanes(taps[tap * ROWS12 : (tap + 1) * ROWS12, :], di, dj)
+        error = value - noise_ref[g]
         masked = maskw_ref[g] * error
         loss_ref[...] += masked * error
         wsum_ref[...] += maskw_ref[g]
         grad = 2.0 * masked
         ghb_ref[...] += grad
         gradl = grad.astype(LOWTYPE).astype(F32)
-        dtap = jnp.concatenate(
-            [shift_lanes(gradl, -di, -dj).astype(LOWTYPE) for di, dj in tap_offsets()], axis=0
-        )
-        ghead_ref[...] += dot_nn(dtap, joined[rows, :])
-        wide = dot_tn(dtap, headw_ref[...])
+        for tap, (di, dj) in enumerate(tap_offsets()):
+            dtap[g, tap * ROWS12 : (tap + 1) * ROWS12, :] = shift_lanes(gradl, -di, -dj).astype(
+                LOWTYPE
+            )
+
+    def head_back(g):
+        wide = dot_tn(dtap[g], headw_ref[...])
         acc = jnp.zeros((8, mid), F32)
         for r in chunks:
             o = outp[g, r : r + CHUNK, :]
@@ -366,67 +409,86 @@
             dpool[g, r : r + CHUNK, :] = wide[r : r + CHUNK, mid:] * (s * (1.0 + x * (1.0 - s)))
         add_vec(12, jnp.sum(acc, axis=0, keepdims=True))
 
-    lowt = dout[...].T
-    acc_ref[:, SEG_OFF[7] : SEG_OFF[8]] += dot_nn(lowt, attl[...])
-    datt = dot_nt(dout[...], outw_ref[...]).astype(LOWTYPE)
-    for g in images:
-        rows = slice(g * PLACES, (g + 1) * PLACES)
-        datt_g = datt[rows]
-        gweights = dot_nt(datt_g, qkv[rows, 2 * mid :])
-        dval = dot_tn(plow[g], datt_g)
+    def attend_back(g):
+        datt[rows_of(g), :] = dot_nt(dout[rows_of(g), :], outw_ref[...]).astype(LOWTYPE)
+
+    def weigh_back(g):
+        rows = rows_of(g)
+        gweights = dot_nt(datt[rows, :], qkv[rows, 2 * mid :])
+        dval = dot_tn(plow[g], datt[rows, :])
+        add_vec(11, jnp.sum(fold8(dval), axis=0, keepdims=True))
+        dq3[rows, 2 * mid :] = dval.astype(LOWTYPE)
         for r in chunks:
             p = attn[g, r : r + CHUNK, :]
             gw = gweights[r : r + CHUNK]
             ds = p * (gw - jnp.sum(gw * p, axis=1, keepdims=True))
-            plow[g, r : r + CHUNK, :] = (ds * scale).astype(LOWTYPE)
-        dqry = dot_nn(plow[g], qkv[rows, mid : 2 * mid])
-        dkey = dot_tn(plow[g], qkv[rows, :mid])
+            dscore[g, r : r + CHUNK, :] = (ds * scale).astype(LOWTYPE)
+
+    def query_back(g):
+        rows = rows_of(g)
+        dqry = dot_nn(dscore[g], qkv[rows, mid : 2 * mid])
+        dkey = dot_tn(dscore[g], qkv[rows, :mid])
         add_vec(10, jnp.sum(fold8(dqry), axis=0, keepdims=True))
-        add_vec(11, jnp.sum(fold8(dval), axis=0, keepdims=True))
         dq3[rows, :mid] = dqry.astype(LOWTYPE)
         dq3[rows, mid : 2 * mid] = dkey.astype(LOWTYPE)
-        dq3[rows, 2 * mid :] = dval.astype(LOWTYPE)
-    for k in range(3):
-        lowt = dq3[:, k * mid : (k + 1) * mid].T
-        acc_ref[:, SEG_OFF[4 + k] : SEG_OFF[5 + k]] += dot_nn(lowt, normed[...])
-    wide = dot_nt(dq3[...], qkv_ref[...])
-
-    ones, twos = [], []
-    for g in images:
+
+    def project_back(g):
         one, two = jnp.zeros((8, mid), F32), jnp.zeros((8, mid), F32)
+        wide = dot_nt(dq3[rows_of(g), :], qkv_ref[...])
         for r in chunks:
             xh = (res[g, r : r + CHUNK, :] - mean3[g : g + 1]) * rstd3[g : g + 1]
-            d = wide[g * PLACES + r : g * PLACES + r + CHUNK]
+            d = wide[r : r + CHUNK]
             res[g, r : r + CHUNK, :] = xh
             dyf[g, r : r + CHUNK, :] = d
             one += fold8(d)
             two += fold8(d * xh)
-        ones.append(one)
-        twos.append(two)
-    ones, twos = total(ones), total(twos)
+        ones3[g], twos3[g] = one, two
+
+    staged(
+        [
+            norm_three,
+            project,
+            weigh,
+            attend,
+            join,
+            head,
+            head_back,
+            attend_back,
+            weigh_back,
+            query_back,
+            project_back,
+        ]
+    )
+
+    ones, twos = total(ones3), total(twos3)
     add_vec(9, jnp.sum(ones, axis=0, keepdims=True))
     add_vec(8, jnp.sum(twos, axis=0, keepdims=True))
-    m1, m2 = grouped(ones * gain3, mid), grouped(twos * gain3, mid)
-    for g in images:
-        r1 = rstd3[g : g + 1]
-        acc = jnp.zeros((8, mid), F32)
+
+    def finish(ref, dest, rstd, gain, m1, m2, chans, extra, g, row):
+        r1 = rstd[g : g + 1]
+        acc = jnp.zeros((8, chans), F32)
         for r in chunks:
-            d = dyf[g, r : r + CHUNK, :] * (gain3 * r1)
-            d = d - m1[g : g + 1] * r1 - res[g, r : r + CHUNK, :] * (m2[g : g + 1] * r1)
-            d = d + outp[g, r : r + CHUNK, :]
+            d = dyf[g, r : r + CHUNK, :chans] * (gain * r1)
+            d = d - m1[g : g + 1] * r1 - ref[g, r : r + CHUNK, :] * (m2[g : g + 1] * r1)
+            if extra is not None:
+                d = d + extra[g, r : r + CHUNK, :]
             acc += fold8(d)
-            pad2[g, SIDE + r : SIDE + r + CHUNK, :] = d.astype(LOWTYPE)
-        add_vec(7, jnp.sum(acc, axis=0, keepdims=True))
-
-    low = stack([pad2[g, SIDE : SIDE + PLACES, :] for g in images])
-    lowt = low.T
-    acc_ref[:, SEG_OFF[2] : SEG_OFF[3]] += dot_nn(lowt, low0)
-    acc_ref[:, SEG_OFF[1] : SEG_OFF[2]] += dot_nn(
-        lowt, stack([dy_cat(a2, g, (0, 1, 2)) for g in images])
-    )
-    dskip = dot_nt(low, skip_ref[...])
-    for g in images:
-        dpool[g] += dskip[g * PLACES : (g + 1) * PLACES]
+            dest(g, r, d.astype(LOWTYPE))
+        acc = jnp.sum(acc, axis=0, keepdims=True)
+        add_vec(row, acc)
+        return acc
+
+    def to_pad(pad):
+        def put(g, r, low):
+            pad[g, SIDE + r : SIDE + r + CHUNK, :] = low
+
+        return put
+
+    def turned(parts):
+        return stack(parts).T
+
+    def pad_turned(pad):
+        return turned([pad[g, SIDE : SIDE + PLACES, :] for g in images])
 
     def conv_back(pad, weights, g, chans, apply):
         wide = dot_nt(dy_cat(pad, g, (2, 1, 0)), weights)
@@ -440,63 +502,106 @@
             before = shiftf[g, 7 + r : 7 + r + CHUNK, :chans]
             apply(r, dyf[g, r : r + CHUNK, :chans] + jnp.where(edge(chans, True), before, 0.0))
 
-    def norm_back(pad, weights, ref, mean, rstd, gain, shift, chans):
-        ones, twos = [], []
+    def norm_back(pad, weights, ref, mean, rstd, gain, shift, chans, ones, twos, g):
+        sums = [jnp.zeros((8, chans), F32), jnp.zeros((8, chans), F32)]
+
+        def apply(r, da):
+            xh = (ref[g, r : r + CHUNK, :] - mean[g : g + 1]) * rstd[g : g + 1]
+            y = xh * gain + shift
+            s = sigmoid(y)
+            d = da * (s * (1.0 + y * (1.0 - s)))
+            ref[g, r : r + CHUNK, :] = xh
+            dyf[g, r : r + CHUNK, :chans] = d
+            sums[0] += fold8(d)
+            sums[1] += fold8(d * xh)
+
+        conv_back(pad, weights[...], g, chans, apply)
+        ones[g], twos[g] = sums
+
+    def add_product(first, last, left, right):
+        acc_ref[:, first:last] += dot_nn(left(), right())
+
+    m1, m2 = grouped(ones * gain3, mid), grouped(twos * gain3, mid)
+    ones2, twos2 = [None] * group, [None] * group
+
+    def grad_out():
+        add_product(SEG_OFF[7], SEG_OFF[8], lambda: dout[...].T, lambda: attl[...])
+
+    def grad_project(k):
+        add_product(
+            SEG_OFF[4 + k],
+            SEG_OFF[5 + k],
+            lambda: dq3[:, k * mid : (k + 1) * mid].T,
+            lambda: normed[...],
+        )
+
+    def grad_head():
         for g in images:
-            sums = [jnp.zeros((8, chans), F32), jnp.zeros((8, chans), F32)]
-
-            def apply(r, da, g=g, sums=sums):
-                xh = (ref[g, r : r + CHUNK, :] - mean[g : g + 1]) * rstd[g : g + 1]
-                y = xh * gain + shift
-                s = sigmoid(y)
-                d = da * (s * (1.0 + y * (1.0 - s)))
-                ref[g, r : r + CHUNK, :] = xh
-                dyf[g, r : r + CHUNK, :chans] = d
-                sums[0] += fold8(d)
-                sums[1] += fold8(d * xh)
-
-            conv_back(pad, weights, g, chans, apply)
-            ones.append(sums[0])
-            twos.append(sums[1])
-        ones, twos = total(ones), total(twos)
-        m1, m2 = grouped(ones * gain, chans), grouped(twos * gain, chans)
-        return jnp.sum(ones, axis=0, keepdims=True), jnp.sum(twos, axis=0, keepdims=True), m1, m2
-
-    one, two, m1, m2 = norm_back(pad2, conv2b_ref[...], hid, mean2, rstd2, gain2, shift2, mid)
-    add_vec(6, one)
-    add_vec(5, two)
-    for g in images:
-        r1 = rstd2[g : g + 1]
-        acc = jnp.zeros((8, mid), F32)
-        for r in chunks:
-            d = dyf[g, r : r + CHUNK, :] * (gain2 * r1)
-            d = d - m1[g : g + 1] * r1 - hid[g, r : r + CHUNK, :] * (m2[g : g + 1] * r1)
-            acc += fold8(d)
-            pad1[g, SIDE + r : SIDE + r + CHUNK, :] = d.astype(LOWTYPE)
-        acc = jnp.sum(acc, axis=0, keepdims=True)
-        add_vec(3, acc)
+            ghead_ref[...] += dot_nn(dtap[g], joined[rows_of(g), :])
+
+    staged(
+        [
+            lambda g: finish(res, to_pad(pad2), rstd3, gain3, m1, m2, mid, outp, g, 7),
+            lambda g: norm_back(
+                pad2, conv2b_ref, hid, mean2, rstd2, gain2, shift2, mid, ones2, twos2, g
+            ),
+        ],
+        [grad_out, grad_head] + [functools.partial(grad_project, k) for k in range(3)],
+    )
+    ones, twos = total(ones2), total(twos2)
+    add_vec(6, jnp.sum(ones, axis=0, keepdims=True))
+    add_vec(5, jnp.sum(twos, axis=0, keepdims=True))
+
+    n1, n2 = grouped(ones * gain2, mid), grouped(twos * gain2, mid)
+    ones1, twos1 = [None] * group, [None] * group
+    lowt2 = pad_turned(pad2)
+
+    def finish_two(g):
+        acc = finish(hid, to_pad(pad1), rstd2, gain2, n1, n2, mid, None, g, 3)
         add_vec(4, acc)
         gtime[pl.ds(step * group + g, 1), :] = acc
 
-    lowt = stack([pad1[g, SIDE : SIDE + PLACES, :] for g in images]).T
-    acc_ref[:, SEG_OFF[0] : SEG_OFF[1]] += dot_nn(
-        lowt, stack([dy_cat(a1, g, (0, 1, 2)) for g in images])
-    )
-    one, two, m1, m2 = norm_back(pad1, conv1b_ref[...], x0, mean1, rstd1, gain1, shift1, C1)
-    add_vec(2, one)
-    add_vec(1, two)
-    for g in images:
-        r1 = rstd1[g : g + 1]
-        acc = jnp.zeros((8, C1), F32)
-        lows = []
-        for r in chunks:
-            d = dyf[g, r : r + CHUNK, :C1] * (gain1 * r1)
-            d = d - m1[g : g + 1] * r1 - x0[g, r : r + CHUNK, :] * (m2[g : g + 1] * r1)
-            d = d + dpool[g, r : r + CHUNK, :]
-            acc += fold8(d)
-            lows.append(d.astype(LOWTYPE))
-        add_vec(0, jnp.sum(acc, axis=0, keepdims=True))
-        gstem_ref[...] += dot_nn(patch[g], stack(lows))
+    def grad_conv(lowt, act, offset, k):
+        width = act.shape[2]
+        first = offset + k * width
+        add_product(
+            first,
+            first + width,
+            lambda: lowt,
+            lambda: stack([act[g, SIDE * k : SIDE * k + PLACES, :] for g in images]),
+        )
+
+    def grad_skip():
+        add_product(SEG_OFF[2], SEG_OFF[3], lambda: lowt2, lambda: low0[...])
+        for g in images:
+            dpool[g] += dot_nt(pad2[g, SIDE : SIDE + PLACES, :], skip_ref[...])
+
+    staged(
+        [
+            finish_two,
+            lambda g: norm_back(
+                pad1, conv1b_ref, x0, mean1, rstd1, gain1, shift1, C1, ones1, twos1, g
+            ),
+        ],
+        [functools.partial(grad_conv, lowt2, a2, SEG_OFF[1], k) for k in range(3)] + [grad_skip],
+    )
+    ones, twos = total(ones1), total(twos1)
+    add_vec(2, jnp.sum(ones, axis=0, keepdims=True))
+    add_vec(1, jnp.sum(twos, axis=0, keepdims=True))
+
+    p1, p2 = grouped(ones * gain1, C1), grouped(twos * gain1, C1)
+    lowt1 = pad_turned(pad1)
+
+    def to_pool(g, r, low):
+        dpool_low[g, r : r + CHUNK, :] = low
+
+    def grad_stem(g):
+        gstem_ref[...] += dot_nn(patch[g], dpool_low[g])
+
+    staged(
+        [lambda g: finish(x0, to_pool, rstd1, gain1, p1, p2, C1, dpool, g, 0), grad_stem],
+        [functools.partial(grad_conv, lowt1, a1, SEG_OFF[0], k) for k in range(3)],
+    )
 
     @pl.when(step == steps - 1)
     def _():
@@ -576,7 +681,7 @@
 
 
 def unet_call(samples, owners, peers, operands):
-    group = 2 if samples % 2 == 0 else 1
+    group = max(k for k in (1, 2, 4) if samples % k == 0)
     steps = samples // group
     time_rows = operands[3].shape[0]
     mid = CHANNELS_MID
@@ -608,6 +713,7 @@
         ((places, 3 * mid), LOWTYPE),
         ((group, PLACES, mid), LOWTYPE),
         ((places, mid), LOWTYPE),
+        ((places, C1), LOWTYPE),
         ((places, mid + C1), LOWTYPE),
         ((group, TAPS * ROWS12, PLACES), LOWTYPE),
         ((group, HALO, mid), LOWTYPE),
@@ -619,6 +725,10 @@
         ((group, PLACES, C1), F32),
         ((time_rows, mid), F32),
         ((time_rows, mid), F32),
+        ((group, TAPS * ROWS12, PLACES), LOWTYPE),
+        ((places, mid), LOWTYPE),
+        ((group, PLACES, mid), LOWTYPE),
+        ((group, PLACES, C1), LOWTYPE),
     ]
     return pl.pallas_call(
         functools.partial(unet_body, group, steps, owners, peers),
@@ -1105,7 +1215,7 @@
 def same_group(chans):
     group = np.arange(chans) // (chans // GROUPS)
     same = (group[:, None] == group[None, :]) / (PLACES * (chans // GROUPS))
-    return jnp.asarray(same, F32)
+    return jnp.asarray(same, LOWTYPE)
 
 
 def shards(

time: 340 us -> 287 us (0.84)
  Pallas kernels: 239 us -> 186 us
    pallas_call x1, Pallas kernels: 134 us -> 80.8 us  [unet_call(): pl.pallas_call(functools.partial(unet_body, group, steps, owners, peers),...]
where the time goes in v4:
time: 287 us; the launch traced here: 286 us
  Pallas kernels  186 us (65%)
  waiting for transfers between devices  44.3 us (15%)
  local copies, waits for them, and re-layouts  30.9 us (11%)
  between operations  14.4 us (5%)
  other arithmetic  8.67 us (3%)
    pallas_call x1, Pallas kernels, muon_call(): pl.pallas_call(functools.partial(muon_body, owners, peers), out_shape=[ja...  105 us
    pallas_call x1, Pallas kernels, unet_call(): pl.pallas_call(functools.partial(unet_body, group, steps, owners, peers),...  80.8 us
    all_gather x1, waiting for transfers between devices, shards(): lax.all_gather(matrices.astype(LOWTYPE), 'bucket', axis=0, tiled=True)  44.3 us
    unnamed x48, local copies, waits for them, and re-layouts  7.99 us
    slice x5, local copies, waits for them, and re-layouts, unpack(): blocks[:, start:start + share, :].reshape(seg_rows, packed.shape[1])  7.97 us
  transfers between devices with their start and end apart: 1, of which 1 were waited for; matrix products, arithmetic and copies ran while one was open for 4% of the time, Pallas kernels for 0%

profile of v4, /device:TPU:0, one launch (start us, length us, event | category | flops | bytes accessed | tf_op | source)
XLA Modules:
  0.0 286.3 jit_solution(12107131767566682034)
XLA Ops:
  7.3 2.3 convert_element_type.53
  10.8 1.7 fusion
  13.5 0.7 copy-done.4
  14.6 0.6 pad.50.time_ref
  15.2 0.7 pad.51.clone
  15.9 0.8 pad.49.maskw_ref
  16.7 0.7 pad.57.head_ref
  17.4 0.7 pad.58.headm_ref
  18.1 0.6 pad.55.stem_ref
  21.4 0.7 pad_maximum_fusion.1.stemw_ref
  22.0 0.7 fusion.8.noisy_ref
  22.7 0.8 fusion.7.noise_ref
  23.5 44.3 %all-gather.2.cloned.1.call-done = bf16[5120,256]{1,0:T(8,128)(2,1)} async-done(((bf16[1280,256]{1,0:T(8,128)(2,1)}), bf16[5120,256]{1,0:T(8,128)(2,1)}) %all-gather.2.cloned.1.call-update) | async-done | bytes 2621456 | tf_op jit(solution)/shard_map/all_gather | solution.py:1237
  67.7 1.8 fusion.18
  69.5 1.3 slice.92
  70.9 1.5 slice.91
  72.4 1.9 slice.94
  74.3 1.5 slice.93
  75.7 0.7 copy.53
  76.5 1.5 copy.55.conv2b_ref
  78.2 1.1 copy.54.conv1b_ref
  79.3 0.8 pad_maximum_fusion.qkv_ref
  80.1 0.7 broadcast_in_dim.11.headb_ref
  80.8 80.8 %shard_map.280 = (f32[5376,256]{1,0:T(8,128)}, f32[16,384]{1,0:T(8,128)}) custom-call(bf16[20,16,256]{2,1,0:T(8,128)(2,1)} %fusion.8.noisy_ref, f32[20,16,256]{2,1,0:T(8,128)} %fusion.7.noise_ref, f32[20,16,256]{2,1,0:T(8,128)} %pad.49.maskw_ref, bf16[32,512]{1,0:T(8,128)(2,1)} %pad.50.time_ref, bf16[144,384]{1,0:T(8,128)(2,1)} %pad_maximum_fusion.1.stemw_ref, ...), custom_call_target="tpu_custom_call" | custom-call | tf_op jit(solution)/shard_map/pallas_call | solution.py:733
  161.5 105.3 %shard_map.281 = (f32[1280,256]{1,0:T(8,128)}, f32[1280,256]{1,0:T(8,128)}, bf16[1280,256]{1,0:T(8,128)(2,1)}, f32[32,128]{1,0:T(8,128)}, f32[32,128]{1,0:T(8,12...) custom-call(f32[5376,256]{1,0:T(8,128)} %get-tuple-element.28.rows_r, ...), custom_call_target="tpu_custom_call" | custom-call | tf_op jit(solution)/shard_map/pallas_call | solution.py:1160
  266.9 1.3 fusion.16
  268.2 1.3 fusion.14
  269.5 1.3 fusion.19
  270.8 1.9 fusion.15
  272.7 2.6 copy.63
  275.3 1.1 copy.64
  276.8 0.8 copy.65
  (76 shorter events, 7.7 us)
Async XLA Ops:
  7.2 2.4 copy-start.3
  7.2 2.6 copy-start.18
  7.2 2.6 copy-start.6
  7.2 60.5 %all-gather.2.cloned.1.call-start = ((), (), s32[]{:S(2)}) async-start(), calls=%async_computation | async-start | bytes 3276800 | tf_op jit(solution)/shard_map/all_gather | solution.py:1237
  9.8 0.9 copy-start.8
  9.8 1.0 copy-start.19
  13.3 0.9 copy-start.4
  14.2 3.2 %copy-start.7 = (f32[3456,12]{0,1:T(8,128)S(1)}, f32[3456,12]{0,1:T(8,128)}, u32[]{:S(2)}) copy-start(f32[3456,12]{0,1:T(8,128)} %param.26) | copy-start | bytes 497668
  14.2 3.9 %copy-start.10 = (f32[27,128]{1,0:T(8,128)S(1)}, f32[27,128]{1,0:T(8,128)}, u32[]{:S(2)}) copy-start(f32[27,128]{1,0:T(8,128)} %param.23) | copy-start | bytes 41476
  14.2 4.5 %copy-start.11 = (f32[27,128]{1,0:T(8,128)S(1)}, f32[27,128]{1,0:T(8,128)}, u32[]{:S(2)}) copy-start(f32[27,128]{1,0:T(8,128)} %param.24) | copy-start | bytes 41476
  14.2 5.1 %copy-start.13 = (f32[2956]{0:T(1024)S(1)}, f32[2956]{0:T(1024)}, u32[]{:S(2)}) copy-start(f32[2956]{0:T(1024)} %param.27) | copy-start | bytes 35476
  14.3 5.7 %copy-start.14 = (f32[2956]{0:T(1024)S(1)}, f32[2956]{0:T(1024)}, u32[]{:S(2)}) copy-start(f32[2956]{0:T(1024)} %param.29) | copy-start | bytes 35476
  14.3 6.3 %copy-start.15 = (f32[2956]{0:T(1024)S(1)}, f32[2956]{0:T(1024)}, u32[]{:S(2)}) copy-start(f32[2956]{0:T(1024)} %param.28) | copy-start | bytes 35476
  14.3 6.9 %copy-start.9 = (f32[144,27]{1,0:T(8,128)S(1)}, f32[144,27]{1,0:T(8,128)}, u32[]{:S(2)}) copy-start(f32[144,27]{1,0:T(8,128)} %constant.35.clone) | copy-start | bytes 46660
  70.9 5.6 %copy-start = (bf16[4,576,256]{2,1,0:T(8,128)(2,1)}, bf16[4,576,256]{2,1,0:T(8,128)(2,1)S(1)}, u32[]{:S(2)}) copy-start(bf16[4,576,256]{2,1,0:T(8,128)(2,1)S(1)} %slice.92) | copy-start | bytes 3538948
  72.4 5.5 %copy-start.1 = (bf16[4,288,256]{2,1,0:T(8,128)(2,1)}, bf16[4,288,256]{2,1,0:T(8,128)(2,1)S(1)}, u32[]{:S(2)}) copy-start(bf16[4,288,256]{2,1,0:T(8,128)(2,1)S(1)} %slice.91) | copy-start | bytes 1769476
  272.7 2.6 copy-start.2
  275.3 1.5 copy-start.5
  276.8 0.8 copy-start.12
  276.8 1.5 copy-start.17
  276.8 2.1 copy-start.16
Sparse Core Ops, SparseCore 0:
  10.2 57.4 all-gather.1

commit v5 on v4

--- a/solution.py
+++ b/solution.py
@@ -46,17 +46,6 @@
         CHANNELS_MID,
         CHANNELS_MID,
     ]
-
-
-def unpack(packed, owners):
-    blocks = packed.reshape(owners, -1, packed.shape[1])
-    pieces = []
-    start = 0
-    for seg_rows in segment_rows():
-        share = seg_rows // owners
-        pieces.append(blocks[:, start : start + share, :].reshape(seg_rows, packed.shape[1]))
-        start += share
-    return pieces
 
 
 def plan(timesteps):
@@ -280,7 +269,7 @@
     sums1 = [None] * group
 
     def stem_patch(g):
-        noisy = noisy_ref[g].astype(F32)
+        noisy = noisy_ref[g]
         for tap, (di, dj) in enumerate(tap_offsets()):
             patch[g, tap * ROWS12 : (tap + 1) * ROWS12, :] = shift_lanes(noisy, di, dj).astype(
                 LOWTYPE
@@ -1170,11 +1159,217 @@
     )(*operands)
 
 
-def phase_order():
-    pixel = np.arange(S * S)
-    row, col = pixel // S, pixel % S
-    lane = (row % 2 * 2 + col % 2) * PLACES + row // 2 * SIDE + col // 2
-    return jnp.asarray(lane, jnp.int32)
+def open_body(
+    owners,
+    peers,
+    weight_ref,
+    images_ref,
+    noise_ref,
+    mask_ref,
+    image_ref,
+    conv1_ref,
+    conv1b_ref,
+    conv2_ref,
+    conv2b_ref,
+    skip_ref,
+    temb_ref,
+    qkv_ref,
+    outw_ref,
+    noisy_ref,
+    planes_ref,
+    maskw_ref,
+    held,
+    left,
+    sema,
+    semb,
+    semc,
+):
+    mid = CHANNELS_MID
+    chips = peers // 2
+    chunk, _ = chunk_rows(owners, peers)
+    own_rows = weight_ref.shape[0]
+    z = lax.axis_index("bucket")
+    peer = lax.axis_index("batch")
+    chip, core = peer // 2, peer % 2
+    partner = {"batch": chip * 2 + 1 - core}
+    slot = core * chips + chip
+    started = []
+
+    def same_core(k):
+        return {"batch": lax.rem(chip + k, chips) * 2 + core}
+
+    def along(k):
+        return {"bucket": lax.rem(z + k, owners)}
+
+    def send(source, target, sems, index, device):
+        copy = pltpu.make_async_remote_copy(
+            src_ref=source,
+            dst_ref=target,
+            send_sem=sems.at[0, index],
+            recv_sem=sems.at[1, index],
+            device_id=device,
+            device_id_type=MESH,
+        )
+        copy.start()
+        started.append(copy)
+        return copy
+
+    barrier = pltpu.get_barrier_semaphore()
+    friends = [partner] + [same_core(k) for k in range(1, chips)]
+    friends += [along(k) for k in range(1, owners)]
+    for friend in friends:
+        pl.semaphore_signal(barrier, inc=1, device_id=friend, device_id_type=MESH)
+
+    for other in range(peers):
+        start = other * chunk
+        size = min(chunk, own_rows - start)
+        if size > 0:
+            held[z, slot_of(other, peers), :size, :] = weight_ref[start : start + size, :].astype(
+                LOWTYPE
+            )
+        if size < chunk:
+            held[z, slot_of(other, peers), max(size, 0) :, :] = jnp.zeros(
+                (chunk - max(size, 0), mid), LOWTYPE
+            )
+    pl.semaphore_wait(barrier, len(friends))
+
+    here = held.at[z, slot]
+    first = [send(here, here, sema, k - 1, along(k)) for k in range(1, owners)]
+
+    samples = mask_ref.shape[0]
+    left[...] = jnp.zeros_like(left)
+    for c in range(3):
+        noise = noise_ref[c]
+        noisy = image_ref[:, 0:1] * images_ref[c] + image_ref[:, 1:2] * noise
+        left[c, :samples, :] = noisy.astype(LOWTYPE)
+        one = noise.astype(LOWTYPE)
+        rest = noise - one.astype(F32)
+        two = rest.astype(LOWTYPE)
+        left[3 + c, :samples, :] = one
+        left[6 + c, :samples, :] = two
+        left[9 + c, :samples, :] = (rest - two.astype(F32)).astype(LOWTYPE)
+    left[12, :samples, :] = mask_ref[...].astype(F32).astype(LOWTYPE)
+    for ref in (noisy_ref, planes_ref, maskw_ref):
+        ref[:, 12:, :] = jnp.zeros((samples, ROWS12 - 12, PLACES), F32)
+
+    def picture(quarter):
+        pixel = lax.broadcasted_iota(jnp.int32, (S * S, PLACES), 0)
+        lane = lax.broadcasted_iota(jnp.int32, (S * S, PLACES), 1)
+        wanted = (
+            (lane // SIDE * 2 + quarter // 2) * S + lane % SIDE * 2 + quarter % 2
+        )
+        pick = jnp.where(pixel == wanted, 1.0, 0.0).astype(LOWTYPE)
+        rows = left.shape[1]
+        moved = dot_nn(left[...].reshape(13 * rows, S * S), pick)
+        maskw = moved[12 * rows : 12 * rows + samples] * image_ref[:, 2:3]
+        for c in range(3):
+            k = quarter * 3 + c
+            noisy_ref[:, k, :] = moved[c * rows : c * rows + samples]
+            planes_ref[:, k, :] = sum(
+                [moved[(p + c) * rows : (p + c) * rows + samples] for p in (6, 9)],
+                moved[(3 + c) * rows : (3 + c) * rows + samples],
+            )
+            maskw_ref[:, k, :] = maskw
+
+    picture(0)
+    second = []
+    for k, copy in zip(range(1, owners), first):
+        copy.wait_recv()
+        there = held.at[lax.rem(z + owners - k, owners), slot]
+        second.append(
+            [
+                send(there, there, semb, (k - 1) * (chips - 1) + j - 1, same_core(j))
+                for j in range(1, chips)
+            ]
+        )
+        if k < 4:
+            picture(k)
+    for k in range(owners, 4):
+        picture(k)
+    third = []
+    for k, copies in zip(range(1, owners), second):
+        for copy in copies:
+            copy.wait_recv()
+        mine = held.at[lax.rem(z + owners - k, owners), pl.ds(core * chips, chips)]
+        third.append(send(mine, mine, semc, k - 1, partner))
+    for copy in third:
+        copy.wait_recv()
+
+    def place(seg, row, values):
+        size = values.shape[0]
+        if seg < 2:
+            whole, side = ((conv1_ref, conv1b_ref), (conv2_ref, conv2b_ref))[seg]
+            whole[row : row + size, :] = values
+            height = side.shape[0]
+            done = 0
+            while done < size:
+                offset, inner = (row + done) // height, (row + done) % height
+                part = min(size - done, height - inner)
+                side[inner : inner + part, offset * mid : (offset + 1) * mid] = values[
+                    done : done + part
+                ]
+                done += part
+        elif seg in (4, 5, 6):
+            qkv_ref[row : row + size, (seg - 4) * mid : (seg - 3) * mid] = values
+        else:
+            {2: skip_ref, 3: temb_ref, 7: outw_ref}[seg][row : row + size, :] = values
+
+    for owner in range(owners):
+        packed = 0
+        for seg, seg_rows in enumerate(segment_rows()):
+            share = seg_rows // owners
+            done = 0
+            while done < share:
+                row = packed + done
+                size = min(share - done, chunk - row % chunk)
+                inner = row % chunk
+                place(
+                    seg,
+                    owner * share + done,
+                    held[owner, slot_of(row // chunk, peers), inner : inner + size, :],
+                )
+                done += size
+            packed += share
+    for copy in started:
+        copy.wait_send()
+
+
+def open_call(owners, peers, operands):
+    mid = CHANNELS_MID
+    chips = peers // 2
+    chunk, _ = chunk_rows(owners, peers)
+    samples = operands[3].shape[0]
+    rows = -(-samples // 16) * 16
+    out_shapes = [
+        ((9 * C1, mid), LOWTYPE),
+        ((3 * C1, 3 * mid), LOWTYPE),
+        ((9 * mid, mid), LOWTYPE),
+        ((3 * mid, 3 * mid), LOWTYPE),
+        ((C1, mid), LOWTYPE),
+        ((TEMB, mid), LOWTYPE),
+        ((mid, 3 * mid), LOWTYPE),
+        ((mid, mid), LOWTYPE),
+        ((samples, ROWS12, PLACES), F32),
+        ((samples, ROWS12, PLACES), F32),
+        ((samples, ROWS12, PLACES), F32),
+    ]
+    vmem = pl.BlockSpec(memory_space=pltpu.VMEM)
+    return pl.pallas_call(
+        functools.partial(open_body, owners, peers),
+        out_shape=[jax.ShapeDtypeStruct(shape, kind) for shape, kind in out_shapes],
+        in_specs=[vmem] * len(operands),
+        out_specs=[vmem] * len(out_shapes),
+        scratch_shapes=[
+            pltpu.VMEM((owners, peers, chunk, mid), LOWTYPE),
+            pltpu.VMEM((13, rows, S * S), LOWTYPE),
+            pltpu.SemaphoreType.DMA((2, owners - 1)),
+            pltpu.SemaphoreType.DMA((2, (owners - 1) * (chips - 1))),
+            pltpu.SemaphoreType.DMA((2, owners - 1)),
+        ],
+        compiler_params=pltpu.CompilerParams(
+            vmem_limit_bytes=VMEM_BYTES, collective_id=1, has_side_effects=True
+        ),
+    )(*operands)
 
 
 def stem_spread():
@@ -1206,10 +1401,6 @@
 def lanes_of(vector):
     rows = -(-vector.shape[0] // (8 * C1)) * 8
     return jnp.pad(vector, (0, rows * C1 - vector.shape[0]), constant_values=1.0).reshape(rows, C1)
-
-
-def by_column(weights, chans):
-    return weights.reshape(3, 3 * chans, CHANNELS_MID).transpose(1, 0, 2).reshape(3 * chans, -1)
 
 
 def same_group(chans):
@@ -1234,33 +1425,20 @@
     vector_seconds,
 ):
     owners, peers = lax.axis_size("bucket"), lax.axis_size("batch")
-    gathered = lax.all_gather(matrices.astype(LOWTYPE), "bucket", axis=0, tiled=True)
-    conv_one, conv_two, skip_w, temb_w, query_w, key_w, value_w, out_w = unpack(gathered, owners)
     samples = images.shape[0]
     level, weight = plan(timesteps)
-    noisy = (
-        jnp.sqrt(level)[:, None, None] * images + jnp.sqrt(1.0 - level)[:, None, None] * noise_field
+    per_image = jnp.stack([jnp.sqrt(level), jnp.sqrt(1.0 - level), weight], axis=1)
+    conv1, conv1b, conv2, conv2b, skip, temb, qkv, outw, noisy, noise, mask_weight = open_call(
+        owners,
+        peers,
+        [
+            matrices,
+            images.transpose(1, 0, 2),
+            noise_field.transpose(1, 0, 2),
+            pixel_mask,
+            per_image,
+        ],
     )
-    mask_weight = pixel_mask.astype(jnp.float32) * weight[:, None]
-    rows = jnp.concatenate(
-        [
-            lax.reduce_precision(noisy, 8, 7).reshape(-1, S * S),
-            noise_field.reshape(-1, S * S),
-            mask_weight,
-        ],
-        axis=0,
-    )
-    order = (phase_order()[:, None] == jnp.arange(S * S, dtype=jnp.int32)[None, :]).astype(F32)
-    phased = jnp.dot(rows, order, precision=EXACT_PRECISION)
-    planes = 3 * samples
-    pictures = phased[: 2 * planes].reshape(2, samples, 3, 4, PLACES).transpose(0, 1, 3, 2, 4)
-    pictures = pad_rows(pictures.reshape(2, samples, 12, PLACES), ROWS12)
-    noisy_low = pictures[0].astype(LOWTYPE)
-    noise_planes = pictures[1]
-    mask_planes = jnp.broadcast_to(
-        phased[2 * planes :].reshape(samples, 4, 1, PLACES), (samples, 4, 3, PLACES)
-    ).reshape(samples, 12, PLACES)
-    mask_planes = pad_rows(mask_planes, ROWS12)
     time_in = pad_rows(swish(embed(timesteps)).astype(LOWTYPE), -(-samples // 16) * 16)
     spread = stem_spread()
     stem_blocks = split_three(
@@ -1276,20 +1454,20 @@
         owners,
         peers,
         [
-            noisy_low,
-            noise_planes,
-            mask_planes,
+            noisy,
+            noise,
+            mask_weight,
             time_in,
             stem_blocks,
             head_rows,
-            conv_one,
-            by_column(conv_one, C1),
-            conv_two,
-            by_column(conv_two, CHANNELS_MID),
-            skip_w,
-            temb_w,
-            jnp.concatenate([query_w, key_w, value_w], axis=1),
-            out_w,
+            conv1,
+            conv1b,
+            conv2,
+            conv2b,
+            skip,
+            temb,
+            qkv,
+            outw,
             vec_rows,
             head_bias,
             same_group(C1),

time: 287 us -> 236 us (0.82)
  waiting for transfers between devices: 44.3 us -> 0 us
  Pallas kernels: 186 us -> 213 us
  local copies, waits for them, and re-layouts: 30.9 us -> 15.3 us
  between operations: 14.4 us -> 0.79 us
    all_gather x1 -> x0, waiting for transfers between devices: 44.3 us -> none  [shards(): lax.all_gather(matrices.astype(LOWTYPE), 'bucket', axis=0, tiled=True)]
    pallas_call x0 -> x1, Pallas kernels: none -> 26.3 us  [open_call(): pl.pallas_call(functools.partial(open_body, owners, peers), out_shape=[ja...]
    slice x7 -> x0, local copies, waits for them, and re-layouts: 8.01 us -> none  [the longest x5 7.97 us: unpack(): blocks[:, start:start + share, :].reshape(seg_rows, packed.shape[1])]
    reshape x8 -> x0, local copies, waits for them, and re-layouts: 3.57 us -> none  [the longest x2 2.55 us: by_column(): weights.reshape(3, 3 * chans, CHANNELS_MID).transpose(1, 0, 2)]
    unnamed x48 -> x35, local copies, waits for them, and re-layouts: 7.99 us -> 6.81 us
  transfers between devices with their start and end apart: 1 -> 0, of which waited for: 1 -> 0; matrix products, arithmetic and copies ran while one was open for 4% -> 0% of each run, Pallas kernels for 0% -> 0%
where the time goes in v5:
time: 236 us; the launch traced here: 235 us
  Pallas kernels  213 us (90%)
  local copies, waits for them, and re-layouts  15.3 us (6%)
  other arithmetic  6.15 us (3%)
    pallas_call x1, Pallas kernels, muon_call(): pl.pallas_call(functools.partial(muon_body, owners, peers), out_shape=[ja...  106 us
    pallas_call x1, Pallas kernels, unet_call(): pl.pallas_call(functools.partial(unet_body, group, steps, owners, peers),...  80.8 us
    pallas_call x1, Pallas kernels, open_call(): pl.pallas_call(functools.partial(open_body, owners, peers), out_shape=[ja...  26.3 us
    unnamed x35, local copies, waits for them, and re-layouts  6.81 us

profile of v5, /device:TPU:0, one launch (start us, length us, event | category | flops | bytes accessed | tf_op | source)
XLA Modules:
  0.0 235.2 jit_solution(4085328154597281640)
XLA Ops:
  0.6 0.0 copy-start.4
  0.7 0.8 sqrt_bitcast_fusion.1
  1.5 0.7 copy.39.image_ref
  2.2 26.3 %shard_map.271 = (bf16[1152,256]{1,0:T(8,128)(2,1)}, bf16[384,768]{1,0:T(8,128)(2,1)}, bf16[2304,256]{1,0:T(8,128)(2,1)}, bf16[768,768]{1,0:T(8,128)(2,1)}, bf16...) custom-call(f32[1280,256]{1,0:T(8,128)} %weight_ref.3, ...), custom_call_target="tpu_custom_call" | custom-call | tf_op jit(solution)/shard_map/pallas_call | solution.py:1357
  28.5 0.0 copy-done.4
  28.5 0.2 reduce-precision_convert_fusion.1
  28.7 0.7 pad_maximum_fusion.stemw_ref
  29.4 0.2 multiply_sine_fusion
  29.6 0.6 pad.40.time_ref
  30.2 0.6 pad_bitcast_fusion.2.vec_ref
  30.8 0.1 reshape.63
  31.0 0.7 pad.41.clone
  31.6 0.7 broadcast_in_dim.10.headb_ref
  32.3 80.8 %shard_map.272 = (f32[5376,256]{1,0:T(8,128)}, f32[16,384]{1,0:T(8,128)}) custom-call(f32[20,16,256]{2,1,0:T(8,128)} %get-tuple-element.39.noisy_ref, f32[20,16,256]{2,1,0:T(8,128)} %get-tuple-element.40.noise_ref, f32[20,16,256]{2,1,0:T(8,128)} %get-tuple-element.41.maskw_ref, bf16[32,512]{1,0:T(8,128)(2,1)} %pad.40.time_ref, ...), custom_call_target="tpu_custom_call" | custom-call | tf_op jit(solution)/shard_map/pallas_call | solution.py:722
  113.1 0.7 pad.47.head_ref
  113.8 0.7 pad.48.headm_ref
  114.5 0.6 pad.45.stem_ref
  115.1 0.6 pad.46.stemm_ref
  115.7 0.6 pad_bitcast_fusion.second_ref
  116.3 0.6 pad_bitcast_fusion.1.first_ref
  116.9 105.7 %shard_map.273 = (f32[1280,256]{1,0:T(8,128)}, f32[1280,256]{1,0:T(8,128)}, bf16[1280,256]{1,0:T(8,128)(2,1)}, f32[32,128]{1,0:T(8,128)}, f32[32,128]{1,0:T(8,12...) custom-call(f32[5376,256]{1,0:T(8,128)} %get-tuple-element.50.rows_r, ...), custom_call_target="tpu_custom_call" | custom-call | tf_op jit(solution)/shard_map/pallas_call | solution.py:1149
  222.6 1.9 fusion.4
  224.5 1.3 fusion.5
  225.8 1.3 fusion.3
  227.1 1.3 fusion.6
  228.4 2.6 %copy.48 = f32[1280,256]{1,0:T(8,128)} copy(f32[1280,256]{1,0:T(8,128)} %get-tuple-element.98) | data formatting | bytes 2621440
  231.0 1.1 copy.49
  232.1 0.5 copy-done.2
  232.5 0.8 copy.50
  233.4 0.6 copy.51
  234.0 0.6 copy.52
  234.6 0.6 copy.53
  (34 shorter events, 0.1 us)
Async XLA Ops:
  0.6 27.8 %copy-start.4 = (f32[144,27]{1,0:T(8,128)S(1)}, f32[144,27]{1,0:T(8,128)}, u32[]{:S(2)}) copy-start(f32[144,27]{1,0:T(8,128)} %constant.32.clone) | copy-start | bytes 46660
  0.7 28.7 %copy-start.13 = (s32[20]{0:T(128)S(1)}, s32[20]{0:T(128)}, u32[]{:S(2)}) copy-start(s32[20]{0:T(128)} %param.18) | copy-start | bytes 244
  0.7 27.8 %copy-start.5 = (f32[27,128]{1,0:T(8,128)S(1)}, f32[27,128]{1,0:T(8,128)}, u32[]{:S(2)}) copy-start(f32[27,128]{1,0:T(8,128)} %param.22) | copy-start | bytes 41476
  2.2 28.1 %copy-start.8 = (f32[2956]{0:T(1024)S(1)}, f32[2956]{0:T(1024)}, u32[]{:S(2)}) copy-start(f32[2956]{0:T(1024)} %param.26) | copy-start | bytes 35476
  2.2 28.7 %copy-start.1 = (f32[3456,12]{0,1:T(8,128)S(1)}, f32[3456,12]{0,1:T(8,128)}, u32[]{:S(2)}) copy-start(f32[3456,12]{0,1:T(8,128)} %param.24) | copy-start | bytes 497668
  32.3 81.5 %copy-start.3 = (f32[3456,12]{0,1:T(8,128)S(1)}, f32[3456,12]{0,1:T(8,128)}, u32[]{:S(2)}) copy-start(f32[3456,12]{0,1:T(8,128)} %param.25) | copy-start | bytes 497668
  32.3 82.8 %copy-start.6 = (f32[27,128]{1,0:T(8,128)S(1)}, f32[27,128]{1,0:T(8,128)}, u32[]{:S(2)}) copy-start(f32[27,128]{1,0:T(8,128)} %param.23) | copy-start | bytes 41476
  32.3 83.4 %copy-start.9 = (f32[2956]{0:T(1024)S(1)}, f32[2956]{0:T(1024)}, u32[]{:S(2)}) copy-start(f32[2956]{0:T(1024)} %param.28) | copy-start | bytes 35476
  32.3 84.0 %copy-start.10 = (f32[2956]{0:T(1024)S(1)}, f32[2956]{0:T(1024)}, u32[]{:S(2)}) copy-start(f32[2956]{0:T(1024)} %param.27) | copy-start | bytes 35476
  228.4 2.6 %copy-start = (f32[1280,256]{1,0:T(8,128)S(1)}, f32[1280,256]{1,0:T(8,128)}, u32[]{:S(2)}) copy-start(f32[1280,256]{1,0:T(8,128)} %get-tuple-element.99) | copy-start | bytes 3932164
  231.0 1.5 copy-start.2
  232.5 0.8 copy-start.7
  232.5 1.5 copy-start.12
  232.5 2.1 copy-start.11

commit v6 on v5

--- a/solution.py
+++ b/solution.py
@@ -849,30 +849,53 @@
         pl.semaphore_signal(barrier, inc=1, device_id=friend, device_id_type=MESH)
     pl.semaphore_wait(barrier, len(friends))
 
+    parts = [None] + list(range(1, owners)) + [0]
+
+    def part_rows(part, base=0):
+        if part is None:
+            return pl.ds(pl.multiple_of(base + owners * chunk, 16), small_chunk)
+        start = base + lax.rem(z + part, owners) * chunk
+        return pl.ds(pl.multiple_of(start, 16), chunk)
+
+    def base_of(k, other_core):
+        owner_core = 1 - core if other_core else core
+        return (owner_core * chips + lax.rem(chip + k, chips)) * block
+
     misc_copy = send(misc_ref, misc1, semm1, 0, partner)
-    first = []
     order = list(range(1, chips)) + [0]
-    for k in order:
-        other = lax.rem(chip + k, chips)
-        start = pl.multiple_of(((1 - core) * chips + other) * block, 16)
-        first.append(send(rows_ref.at[pl.ds(start, block), :], recv1.at[k], sem1, k, partner))
+    first = {}
+    for number, part in enumerate(parts):
+        for k in order:
+            first[part, k] = send(
+                rows_ref.at[part_rows(part, base_of(k, True)), :],
+                recv1.at[k, part_rows(part), :],
+                sem1,
+                number * chips + k,
+                partner,
+            )
 
     misc_copy.wait_recv()
     misc2[chip] = misc_ref[...] + misc1[...]
     misc_copies = [
         send(misc2.at[chip], misc2.at[chip], semm2, k - 1, same_core(k)) for k in range(1, chips)
     ]
-    second = []
-    for k, copy in zip(order, first):
-        copy.wait_recv()
-        other = lax.rem(chip + k, chips)
-        start = pl.multiple_of((core * chips + other) * block, 16)
-        total = rows_ref[pl.ds(start, block), :] + recv1[k]
-        if k == 0:
-            own2[...] = total
-        else:
-            send2[k - 1] = total
-            second.append(send(send2.at[k - 1], recv2.at[k - 1], sem2, k - 1, same_core(k)))
+    second = {}
+    for number, part in enumerate(parts):
+        rows = part_rows(part)
+        for k in order:
+            first[part, k].wait_recv()
+            total = rows_ref[part_rows(part, base_of(k, False)), :] + recv1[k, rows, :]
+            if k == 0:
+                own2[rows, :] = total
+            else:
+                send2[k - 1, rows, :] = total
+                second[part, k] = send(
+                    send2.at[k - 1, rows, :],
+                    recv2.at[k - 1, rows, :],
+                    sem2,
+                    number * (chips - 1) + k - 1,
+                    same_core(k),
+                )
 
     for copy in misc_copies:
         copy.wait_recv()
@@ -880,28 +903,26 @@
     misc_copies = [
         send(misc3.at[z], misc3.at[z], semm3, k - 1, along(k)) for k in range(1, owners)
     ]
-    for copy in second:
-        copy.wait_recv()
     third = []
-    for k in list(range(1, owners)) + [0]:
-        start = pl.multiple_of(lax.rem(z + k, owners) * chunk, 16)
-        rows = pl.ds(start, chunk)
+    for part in parts:
+        for k in range(1, chips):
+            second[part, k].wait_recv()
+        rows = part_rows(part)
         total = own2[rows, :]
         for other in range(chips - 1):
             total = total + recv2[other, rows, :]
-        if k == 0:
+        if part is None:
+            recvs3[z] = total
+            third += [
+                send(recvs3.at[z], recvs3.at[z], sems3, k - 1, along(k)) for k in range(1, owners)
+            ]
+        elif part == 0:
             own2[rows, :] = total
         else:
-            send3[k - 1] = total
-            third.append(send(send3.at[k - 1], recv3.at[k - 1], sem3, k - 1, along(k)))
-    tail = slice(owners * chunk, block)
-    total = own2[tail, :]
-    for other in range(chips - 1):
-        total = total + recv2[other, tail, :]
-    recvs3[z] = total
-    third += [
-        send(recvs3.at[z], recvs3.at[z], sems3, k - 1, along(k)) for k in range(1, owners)
-    ]
+            send3[part - 1] = total
+            third.append(
+                send(send3.at[part - 1], recv3.at[part - 1], sem3, part - 1, along(part))
+            )
     for copy in third:
         copy.wait_recv()
     total = own2[pl.ds(pl.multiple_of(z * chunk, 16), chunk), :]
@@ -1131,8 +1152,8 @@
         ((4, most[1], mid), LOWTYPE),
     ]
     sems = [
-        chips,
-        chips - 1,
+        (owners + 1) * chips,
+        (owners + 1) * (chips - 1),
         owners - 1,
         owners - 1,
         chips - 1,

time: 236 us -> 217 us (0.919)
  Pallas kernels: 213 us -> 195 us
    pallas_call x1, Pallas kernels: 106 us -> 87.5 us  [muon_call(): pl.pallas_call(functools.partial(muon_body, owners, peers), out_shape=[ja...]
where the time goes in v6:
time: 217 us
  Pallas kernels  195 us (90%)
  local copies, waits for them, and re-layouts  15.3 us (7%)
  other arithmetic  6.15 us (3%)
    pallas_call x1, Pallas kernels, muon_call(): pl.pallas_call(functools.partial(muon_body, owners, peers), out_shape=[ja...  87.5 us
    pallas_call x1, Pallas kernels, unet_call(): pl.pallas_call(functools.partial(unet_body, group, steps, owners, peers),...  80.8 us
    pallas_call x1, Pallas kernels, open_call(): pl.pallas_call(functools.partial(open_body, owners, peers), out_shape=[ja...  26.3 us
    unnamed x35, local copies, waits for them, and re-layouts  6.81 us

profile of v6, /device:TPU:0, one launch (start us, length us, event | category | flops | bytes accessed | tf_op | source)
XLA Modules:
  0.0 217.1 jit_solution(4994160039689799985)
XLA Ops:
  0.6 0.0 copy-start.4
  0.7 0.0 copy-start.13
  0.7 0.8 sqrt_bitcast_fusion.1
  1.5 0.7 copy.39.image_ref
  2.2 26.3 %shard_map.271 = (bf16[1152,256]{1,0:T(8,128)(2,1)}, bf16[384,768]{1,0:T(8,128)(2,1)}, bf16[2304,256]{1,0:T(8,128)(2,1)}, bf16[768,768]{1,0:T(8,128)(2,1)}, bf16...) custom-call(f32[1280,256]{1,0:T(8,128)} %weight_ref.3, ...), custom_call_target="tpu_custom_call" | custom-call | tf_op jit(solution)/shard_map/pallas_call | solution.py:1378
  28.5 0.2 reduce-precision_convert_fusion.1
  28.7 0.7 pad_maximum_fusion.stemw_ref
  29.4 0.2 multiply_sine_fusion
  29.6 0.6 pad.40.time_ref
  30.2 0.6 pad_bitcast_fusion.2.vec_ref
  30.8 0.1 reshape.63
  31.0 0.7 pad.41.clone
  31.6 0.7 broadcast_in_dim.10.headb_ref
  32.3 80.8 %shard_map.272 = (f32[5376,256]{1,0:T(8,128)}, f32[16,384]{1,0:T(8,128)}) custom-call(f32[20,16,256]{2,1,0:T(8,128)} %get-tuple-element.39.noisy_ref, f32[20,16,256]{2,1,0:T(8,128)} %get-tuple-element.40.noise_ref, f32[20,16,256]{2,1,0:T(8,128)} %get-tuple-element.41.maskw_ref, bf16[32,512]{1,0:T(8,128)(2,1)} %pad.40.time_ref, ...), custom_call_target="tpu_custom_call" | custom-call | tf_op jit(solution)/shard_map/pallas_call | solution.py:722
  113.1 0.7 pad.47.head_ref
  113.8 0.7 pad.48.headm_ref
  114.5 0.6 pad.45.stem_ref
  115.1 0.6 pad.46.stemm_ref
  115.7 0.6 pad_bitcast_fusion.second_ref
  116.3 0.6 pad_bitcast_fusion.1.first_ref
  116.9 87.5 %shard_map.273 = (f32[1280,256]{1,0:T(8,128)}, f32[1280,256]{1,0:T(8,128)}, bf16[1280,256]{1,0:T(8,128)(2,1)}, f32[32,128]{1,0:T(8,128)}, f32[32,128]{1,0:T(8,12...) custom-call(f32[5376,256]{1,0:T(8,128)} %get-tuple-element.50.rows_r, ...), custom_call_target="tpu_custom_call" | custom-call | tf_op jit(solution)/shard_map/pallas_call | solution.py:1170
  204.5 1.9 fusion.4
  206.3 1.3 fusion.5
  207.6 1.3 fusion.3
  208.9 1.3 fusion.6
  210.3 2.6 %copy.48 = f32[1280,256]{1,0:T(8,128)} copy(f32[1280,256]{1,0:T(8,128)} %get-tuple-element.98) | data formatting | bytes 2621440
  212.9 1.1 copy.49
  213.9 0.5 copy-done.2
  214.4 0.8 copy.50
  215.2 0.6 copy.51
  215.8 0.6 copy.52
  216.4 0.6 copy.53
  (34 shorter events, 0.1 us)
Async XLA Ops:
  0.6 27.8 %copy-start.4 = (f32[144,27]{1,0:T(8,128)S(1)}, f32[144,27]{1,0:T(8,128)}, u32[]{:S(2)}) copy-start(f32[144,27]{1,0:T(8,128)} %constant.32.clone) | copy-start | bytes 46660
  0.7 28.7 %copy-start.13 = (s32[20]{0:T(128)S(1)}, s32[20]{0:T(128)}, u32[]{:S(2)}) copy-start(s32[20]{0:T(128)} %param.18) | copy-start | bytes 244
  0.7 27.8 %copy-start.5 = (f32[27,128]{1,0:T(8,128)S(1)}, f32[27,128]{1,0:T(8,128)}, u32[]{:S(2)}) copy-start(f32[27,128]{1,0:T(8,128)} %param.22) | copy-start | bytes 41476
  2.2 28.1 %copy-start.8 = (f32[2956]{0:T(1024)S(1)}, f32[2956]{0:T(1024)}, u32[]{:S(2)}) copy-start(f32[2956]{0:T(1024)} %param.26) | copy-start | bytes 35476
  2.2 28.7 %copy-start.1 = (f32[3456,12]{0,1:T(8,128)S(1)}, f32[3456,12]{0,1:T(8,128)}, u32[]{:S(2)}) copy-start(f32[3456,12]{0,1:T(8,128)} %param.24) | copy-start | bytes 497668
  32.3 81.5 %copy-start.3 = (f32[3456,12]{0,1:T(8,128)S(1)}, f32[3456,12]{0,1:T(8,128)}, u32[]{:S(2)}) copy-start(f32[3456,12]{0,1:T(8,128)} %param.25) | copy-start | bytes 497668
  32.3 82.8 %copy-start.6 = (f32[27,128]{1,0:T(8,128)S(1)}, f32[27,128]{1,0:T(8,128)}, u32[]{:S(2)}) copy-start(f32[27,128]{1,0:T(8,128)} %param.23) | copy-start | bytes 41476
  32.3 83.4 %copy-start.9 = (f32[2956]{0:T(1024)S(1)}, f32[2956]{0:T(1024)}, u32[]{:S(2)}) copy-start(f32[2956]{0:T(1024)} %param.28) | copy-start | bytes 35476
  32.3 84.0 %copy-start.10 = (f32[2956]{0:T(1024)S(1)}, f32[2956]{0:T(1024)}, u32[]{:S(2)}) copy-start(f32[2956]{0:T(1024)} %param.27) | copy-start | bytes 35476
  210.3 2.6 %copy-start = (f32[1280,256]{1,0:T(8,128)S(1)}, f32[1280,256]{1,0:T(8,128)}, u32[]{:S(2)}) copy-start(f32[1280,256]{1,0:T(8,128)} %get-tuple-element.99) | copy-start | bytes 3932164
  212.9 1.5 copy-start.2
  214.4 0.8 copy-start.7
  214.4 1.5 copy-start.12
  214.4 2.1 copy-start.11

commit v7 on v6

--- a/solution.py
+++ b/solution.py
@@ -123,8 +123,8 @@
     noise_ref,
     maskw_ref,
     time_ref,
-    stemw_ref,
-    headw_ref,
+    stem_ref,
+    head_ref,
     conv1_ref,
     conv1b_ref,
     conv2_ref,
@@ -134,7 +134,6 @@
     qkv_ref,
     outw_ref,
     vec_ref,
-    headb_ref,
     same128_ref,
     same256_ref,
     spread_ref,
@@ -174,6 +173,11 @@
     datt,
     dscore,
     dpool_low,
+    stemw_ref,
+    headw_ref,
+    headb_ref,
+    time_low,
+    wide_rows,
 ):
     step = pl.program_id(0)
     mid = CHANNELS_MID
@@ -195,7 +199,28 @@
                 ref[g, :SIDE, :] = jnp.zeros((SIDE, ref.shape[2]), ref.dtype)
                 ref[g, HALO - SIDE :, :] = jnp.zeros((SIDE, ref.shape[2]), ref.dtype)
         shiftf[...] = jnp.zeros_like(shiftf)
-        tproj[...] = dot_nn(time_ref[...], temb_ref[...])
+        wide_rows[...] = jnp.zeros_like(wide_rows)
+        samples = time_ref.shape[0]
+        wide_rows[:samples, :TEMB] = time_ref[...]
+        time_low[...] = wide_rows[: time_low.shape[0], :TEMB].astype(LOWTYPE)
+        tproj[...] = dot_nn(time_low[...], temb_ref[...])
+        wide_rows[:27, :C1] = stem_ref[...].astype(LOWTYPE).astype(F32)
+        spread_stem = dot_nn(spread_ref[:, :27], wide_rows[:27, :C1], EXACT_PRECISION)
+        for piece in range(3):
+            low = spread_stem.astype(LOWTYPE)
+            stemw_ref[:, piece * C1 : (piece + 1) * C1] = low
+            spread_stem = spread_stem - low.astype(F32)
+        width = mid + C1
+        wide_rows[:ROWS12, :width] = jnp.zeros((ROWS12, width), F32)
+        for tap in range(TAPS):
+            wide_rows[:12, :width] = head_ref[:, tap * width : (tap + 1) * width]
+            headw_ref[tap * ROWS12 : (tap + 1) * ROWS12, :] = wide_rows[:ROWS12, :width].astype(
+                LOWTYPE
+            )
+        row = lax.broadcasted_iota(jnp.int32, (ROWS12, C1), 0)
+        lane = lax.broadcasted_iota(jnp.int32, (ROWS12, C1), 1)
+        bias = jnp.where(row == lane, vec_ref[23:24, :], 0.0)
+        headb_ref[...] = jnp.sum(bias, axis=1, keepdims=True) + jnp.zeros((ROWS12, C1), F32)
 
     def vec(row, chans=mid):
         if chans == C1:
@@ -594,7 +619,7 @@
 
     @pl.when(step == steps - 1)
     def _():
-        acc_ref[:, SEG_OFF[3] : SEG_OFF[4]] = dot_tn(gtime[...].astype(LOWTYPE), time_ref[...])
+        acc_ref[:, SEG_OFF[3] : SEG_OFF[4]] = dot_tn(gtime[...].astype(LOWTYPE), time_low[...])
         if rows_ref.shape[0] > 5120 + SMALL_ROWS:
             rows_ref[...] = jnp.zeros_like(rows_ref)
         pieces = gradient_pieces(owners, peers)
@@ -672,7 +697,7 @@
 def unet_call(samples, owners, peers, operands):
     group = max(k for k in (1, 2, 4) if samples % k == 0)
     steps = samples // group
-    time_rows = operands[3].shape[0]
+    time_rows = -(-samples // 16) * 16
     mid = CHANNELS_MID
     places = group * PLACES
 
@@ -718,6 +743,11 @@
         ((places, mid), LOWTYPE),
         ((group, PLACES, mid), LOWTYPE),
         ((group, PLACES, C1), LOWTYPE),
+        ((TAPS * ROWS12, 3 * C1), LOWTYPE),
+        ((TAPS * ROWS12, mid + C1), LOWTYPE),
+        ((ROWS12, C1), F32),
+        ((time_rows, TEMB), LOWTYPE),
+        ((max(32, time_rows), TEMB), F32),
     ]
     return pl.pallas_call(
         functools.partial(unet_body, group, steps, owners, peers),
@@ -768,7 +798,6 @@
     second_ref,
     new_ref,
     newm_ref,
-    copy_ref,
     nstem_ref,
     nstemm_ref,
     nhead_ref,
@@ -796,6 +825,8 @@
     small,
     x_zero,
     x_one,
+    flat,
+    head_row,
     sem1,
     sem2,
     sem3,
@@ -945,16 +976,17 @@
     weight_sum = jnp.sum(misc[14:15, :mid], axis=1, keepdims=True)
     inverse = 1.0 / weight_sum
     loss_sum = jnp.sum(misc[13:14, :mid], axis=1, keepdims=True)
-    lane = lax.broadcasted_iota(jnp.int32, (8, C1), 1)
-    sums_ref[...] = jnp.where(lane == 0, loss_sum, weight_sum)
+    sums_ref[0:1, :] = loss_sum + jnp.zeros((1, C1), F32)
+    sums_ref[1:2, :] = weight_sum + jnp.zeros((1, C1), F32)
     head_bias = jnp.sum(misc[:, mid:].T, axis=0, keepdims=True)
-    nvec_ref[...] = jnp.zeros_like(nvec_ref)
-    nvec_ref[:3, :] = misc[:3, :C1]
+    for row in range(3):
+        flat[pl.ds(row * C1, C1)] = misc[row : row + 1, :C1].reshape(C1)
     for row in range(3, 13):
-        nvec_ref[2 * row - 3 : 2 * row - 2, :] = misc[row : row + 1, :C1]
-        nvec_ref[2 * row - 2 : 2 * row - 1, :] = misc[row : row + 1, C1:mid]
-    nvec_ref[23:24, :ROWS12] = head_bias
-    grad = nvec_ref[...] * inverse
+        flat[pl.ds(3 * C1 + (row - 3) * mid, mid)] = misc[row : row + 1, :mid].reshape(mid)
+    head_row[...] = jnp.zeros_like(head_row)
+    head_row[0:1, :ROWS12] = head_bias
+    flat[pl.ds(3 * C1 + 10 * mid, C1)] = head_row[0:1, :].reshape(C1)
+    grad = flat[pl.ds(0, vec_ref.shape[0])] * inverse.reshape(1)
     firsts = BETA_ONE * first_ref[...] + (1.0 - BETA_ONE) * grad
     seconds = BETA_TWO * second_ref[...] + (1.0 - BETA_TWO) * grad * grad
     nfirst_ref[...] = firsts
@@ -1014,29 +1046,30 @@
         row = tile * 16
         at = chunk + row % chunk_s
         tiles.append(gathered[slot_of(row // chunk_s, peers), at : at + 16, :] * inverse)
+    small[...] = jnp.zeros_like(small)
     for tap in range(TAPS):
         lanes = slice(tap * (mid + C1), tap * (mid + C1) + mid)
-        nheadm_ref[:, lanes] = tiles[tap]
+        small[:16, lanes] = tiles[tap]
         lanes = slice(tap * (mid + C1) + mid, (tap + 1) * (mid + C1))
         if tap < 5:
-            nheadm_ref[:, lanes] = tiles[9 + tap][:, :C1]
+            small[:16, lanes] = tiles[9 + tap][:, :C1]
         else:
-            nheadm_ref[:, lanes] = tiles[9 + tap - 5][:, C1:]
-    grad = nheadm_ref[...]
-    moment = MOMENTUM * headm_ref[...] + grad
-    nheadm_ref[...] = moment
-    turn = grad + MOMENTUM * moment
-    small[...] = jnp.zeros_like(small)
-    small[:16, :SMALL_LANES] = turn * lax.rsqrt(
-        jnp.sum(jnp.sum(turn * turn, axis=1, keepdims=True), axis=0, keepdims=True) + NORM_EPS
-    )
-    grad = jnp.concatenate([tiles[14][:, :C1], tiles[14][:, C1:]], axis=0)
-    moment = MOMENTUM * stemm_ref[...] + grad
-    nstemm_ref[...] = moment
-    turn = grad + MOMENTUM * moment
-    small[32:, SMALL_LANES:] = turn * lax.rsqrt(
-        jnp.sum(jnp.sum(turn * turn, axis=1, keepdims=True), axis=0, keepdims=True) + NORM_EPS
-    )
+            small[:16, lanes] = tiles[9 + tap - 5][:, C1:]
+    small[32:48, SMALL_LANES:] = tiles[14][:, :C1]
+    small[48:, SMALL_LANES:] = tiles[14][:, C1:]
+    head_part = (slice(0, 12), slice(0, SMALL_LANES))
+    stem_part = (slice(32, 59), slice(SMALL_LANES, SMALL_LANES + C1))
+    for part, old_ref, fresh_ref in (
+        (head_part, headm_ref, nheadm_ref),
+        (stem_part, stemm_ref, nstemm_ref),
+    ):
+        grad = small[part]
+        moment = MOMENTUM * old_ref[...] + grad
+        fresh_ref[...] = moment
+        turn = grad + MOMENTUM * moment
+        small[part] = turn * lax.rsqrt(
+            jnp.sum(jnp.sum(turn * turn, axis=1, keepdims=True), axis=0, keepdims=True) + NORM_EPS
+        )
     gram = lax.dot_general(
         small[...],
         small[...],
@@ -1045,10 +1078,10 @@
         precision=EXACT_PRECISION,
     )
     product = ns_chain(gram, identity(64))
-    turned = dot_nn(product, small[...], EXACT_PRECISION)
+    small[...] = dot_nn(product, small[...], EXACT_PRECISION)
     keep = 1.0 - LR_MUON * DECAY
-    nhead_ref[...] = head_ref[...] * keep - LR_MUON * turned[:16, :SMALL_LANES]
-    nstem_ref[...] = stem_ref[...] * keep - LR_MUON * turned[32:, SMALL_LANES:]
+    nhead_ref[...] = head_ref[...] * keep - LR_MUON * small[head_part]
+    nstem_ref[...] = stem_ref[...] * keep - LR_MUON * small[stem_part]
 
     for copy in copies:
         copy.wait_recv()
@@ -1103,7 +1136,6 @@
         rows = slice(start, start + share)
         fresh = weight_ref[rows, :] * keep - LR_MUON * buffer[task_chip, :share, :].astype(F32)
         new_ref[rows, :] = fresh
-        copy_ref[rows, :] = fresh.astype(LOWTYPE)
     for copy in started:
         copy.wait_send()
 
@@ -1120,7 +1152,6 @@
     out_shapes = [
         ((rows, mid), F32),
         ((rows, mid), F32),
-        ((rows, mid), LOWTYPE),
         (operands[4].shape, F32),
         (operands[4].shape, F32),
         (operands[6].shape, F32),
@@ -1150,6 +1181,8 @@
         ((64, SMALL_LANES + C1), F32),
         ((4, most[0], mid), LOWTYPE),
         ((4, most[1], mid), LOWTYPE),
+        ((3 * C1 + 10 * mid + C1,), F32),
+        ((8, C1), F32),
     ]
     sems = [
         (owners + 1) * chips,
@@ -1393,6 +1426,30 @@
     )(*operands)
 
 
+def close_body(*refs):
+    values, outs = refs[:10], refs[10:]
+    for source, target in zip(values[:9], outs[:9]):
+        target[...] = source[...]
+    for source, target in zip((values[0], values[2], values[4]), outs[9:12]):
+        target[...] = source[...].astype(LOWTYPE)
+    sums = values[9]
+    outs[12][...] = sums[0:1, 0:1]
+    outs[13][...] = sums[1:2, 0:1]
+
+
+def close_call(values):
+    shapes = [(v.shape, F32) for v in values[:9]]
+    shapes += [(values[k].shape, LOWTYPE) for k in (0, 2, 4)] + [((1, 1), F32)] * 2
+    vmem = pl.BlockSpec(memory_space=pltpu.VMEM)
+    return pl.pallas_call(
+        close_body,
+        out_shape=[jax.ShapeDtypeStruct(shape, kind) for shape, kind in shapes],
+        in_specs=[vmem] * len(values),
+        out_specs=[vmem] * len(shapes),
+        compiler_params=pltpu.CompilerParams(vmem_limit_bytes=VMEM_BYTES),
+    )(*values)
+
+
 def stem_spread():
     counts = np.zeros((3, 2, 3))
     for block in range(3):
@@ -1406,17 +1463,6 @@
     for c in range(3):
         full[:, :, c:12:3, :, :, c] = both
     return jnp.asarray(full.reshape(TAPS * ROWS12, 27), F32)
-
-
-def split_three(values):
-    first = lax.reduce_precision(values, 8, 7)
-    second = lax.reduce_precision(values - first, 8, 7)
-    third = values - first - second
-    return jnp.concatenate([first, second, third], axis=1).astype(LOWTYPE)
-
-
-def pad_rows(values, rows):
-    return jnp.pad(values, [(0, 0)] * (values.ndim - 2) + [(0, rows - values.shape[-2]), (0, 0)])
 
 
 def lanes_of(vector):
@@ -1460,16 +1506,8 @@
             per_image,
         ],
     )
-    time_in = pad_rows(swish(embed(timesteps)).astype(LOWTYPE), -(-samples // 16) * 16)
     spread = stem_spread()
-    stem_blocks = split_three(
-        jnp.dot(spread, lax.reduce_precision(stem_weight, 8, 7), precision=EXACT_PRECISION)
-    )
     head_turned = head_weight.T
-    head_rows = head_turned.astype(LOWTYPE).reshape(12, TAPS, CHANNELS_MID + C1)
-    head_rows = pad_rows(head_rows.transpose(1, 0, 2), ROWS12).reshape(TAPS * ROWS12, -1)
-    vec_rows = lanes_of(vectors)
-    head_bias = jnp.broadcast_to(pad_rows(vectors[-12:].reshape(12, 1), ROWS12), (ROWS12, C1))
     rows_out, misc = unet_call(
         samples,
         owners,
@@ -1478,9 +1516,9 @@
             noisy,
             noise,
             mask_weight,
-            time_in,
-            stem_blocks,
-            head_rows,
+            swish(embed(timesteps)),
+            stem_weight,
+            head_turned,
             conv1,
             conv1b,
             conv2,
@@ -1489,26 +1527,13 @@
             temb,
             qkv,
             outw,
-            vec_rows,
-            head_bias,
+            lanes_of(vectors),
             same_group(C1),
             same_group(CHANNELS_MID),
             jnp.pad(spread, ((0, 0), (0, 5))),
         ],
     )
-    (
-        new_matrices,
-        new_matrix_moms,
-        matrix_copies,
-        new_stem,
-        new_stem_moms,
-        new_head,
-        new_head_moms,
-        new_vec,
-        new_first,
-        new_second,
-        sums,
-    ) = muon_call(
+    values = muon_call(
         owners,
         peers,
         [
@@ -1516,22 +1541,33 @@
             misc,
             matrices,
             matrix_moms,
-            pad_rows(stem_weight, 32),
-            pad_rows(stem_moms, 32),
-            pad_rows(head_turned, ROWS12),
-            pad_rows(head_moms.T, ROWS12),
-            vec_rows,
-            lanes_of(vector_firsts),
-            lanes_of(vector_seconds),
+            stem_weight,
+            stem_moms,
+            head_turned,
+            head_moms.T,
+            vectors,
+            vector_firsts,
+            vector_seconds,
         ],
     )
-    count = vectors.shape[0]
-    new_stem, new_stem_moms = new_stem[:27], new_stem_moms[:27]
-    new_head, new_head_moms = new_head[:12].T, new_head_moms[:12].T
-    new_vectors = new_vec.reshape(-1)[:count]
-    new_firsts = new_first.reshape(-1)[:count]
-    new_seconds = new_second.reshape(-1)[:count]
-    loss_sum, weight_sum = sums[0, 0], sums[0, 1]
+    (
+        new_matrices,
+        new_matrix_moms,
+        new_stem,
+        new_stem_moms,
+        new_head,
+        new_head_moms,
+        new_vectors,
+        new_firsts,
+        new_seconds,
+        matrix_copies,
+        stem_copy,
+        head_copy,
+        loss_sum,
+        weight_sum,
+    ) = close_call(values)
+    loss_sum, weight_sum = loss_sum.reshape(()), weight_sum.reshape(())
+    new_head, new_head_moms, head_copy = new_head.T, new_head_moms.T, head_copy.T
     return (
         loss_sum,
         weight_sum,
@@ -1540,10 +1576,10 @@
         matrix_copies,
         new_stem,
         new_stem_moms,
-        new_stem.astype(LOWTYPE),
+        stem_copy,
         new_head,
         new_head_moms,
-        new_head.astype(LOWTYPE),
+        head_copy,
         new_vectors,
         new_firsts,
         new_seconds,

time: 217 us -> 205 us (0.945)
  local copies, waits for them, and re-layouts: 15.3 us -> 2 us
  Pallas kernels: 195 us -> 198 us
  other arithmetic: 6.15 us -> 3.51 us
    unnamed x35 -> x0, local copies, waits for them, and re-layouts: 6.81 us -> none
    pad x6 -> x0, local copies, waits for them, and re-layouts: 3.9 us -> none  [pad_rows(): jnp.pad(values, [(0, 0)] * (values.ndim - 2) + [(0, rows - values.shape[-...]
    pallas_call x0 -> x1, Pallas kernels: none -> 3.85 us  [close_call(): pl.pallas_call(close_body, out_shape=[jax.ShapeDtypeStruct(shape, kind) f...]
    convert_element_type x4 -> x0, other arithmetic: 3.22 us -> none  [the longest x1 1.86 us: shards(): new_head.astype(LOWTYPE)]
where the time goes in v7:
time: 205 us
  Pallas kernels  198 us (97%)
  other arithmetic  3.51 us (2%)
    pallas_call x1, Pallas kernels, muon_call(): pl.pallas_call(functools.partial(muon_body, owners, peers), out_shape=[ja...  87.3 us
    pallas_call x1, Pallas kernels, unet_call(): pl.pallas_call(functools.partial(unet_body, group, steps, owners, peers),...  81 us
    pallas_call x1, Pallas kernels, open_call(): pl.pallas_call(functools.partial(open_body, owners, peers), out_shape=[ja...  26.2 us

profile of v7, /device:TPU:0, one launch (start us, length us, event | category | flops | bytes accessed | tf_op | source)
XLA Modules:
  0.0 204.6 jit_solution(8865905174590704869)
XLA Ops:
  0.6 0.7 convert_element_type.9
  1.3 0.7 sqrt_bitcast_fusion.1
  2.1 0.7 copy.34.image_ref
  2.7 1.3 pad_bitcast_fusion.vec_ref
  4.1 0.2 multiply_sine_fusion
  4.2 0.6 divide_multiply_fusion.time_ref
  4.9 26.2 %shard_map.271 = (bf16[1152,256]{1,0:T(8,128)(2,1)}, bf16[384,768]{1,0:T(8,128)(2,1)}, bf16[2304,256]{1,0:T(8,128)(2,1)}, bf16[768,768]{1,0:T(8,128)(2,1)}, bf16...) custom-call(f32[1280,256]{1,0:T(8,128)} %weight_ref.3, ...), custom_call_target="tpu_custom_call" | custom-call | tf_op jit(solution)/shard_map/pallas_call | solution.py:1411
  31.1 81.0 %shard_map.272 = (f32[5376,256]{1,0:T(8,128)}, f32[16,384]{1,0:T(8,128)}) custom-call(f32[20,16,256]{2,1,0:T(8,128)} %get-tuple-element.52.noisy_ref, f32[20,16,256]{2,1,0:T(8,128)} %get-tuple-element.53.noise_ref, f32[20,16,256]{2,1,0:T(8,128)} %get-tuple-element.54.maskw_ref, f32[20,512]{1,0:T(8,128)} %divide_multiply_fusion.time_ref, f32[27,128]{1,0:T(8,128)} %stem_ref.3, ...), custom_call_target="tpu_custom_call" | custom-call | tf_op jit(solution)/shard_map/pallas_call | solution.py:752
  112.1 87.3 %shard_map.273 = (f32[1280,256]{1,0:T(8,128)}, f32[1280,256]{1,0:T(8,128)}, f32[27,128]{1,0:T(8,128)}, f32[27,128]{1,0:T(8,128)}, f32[12,3456]{1,0:T(8,128)}, /*...) custom-call(f32[5376,256]{1,0:T(8,128)} %get-tuple-element.63.rows_ref, ...), custom_call_target="tpu_custom_call" | custom-call | tf_op jit(solution)/shard_map/pallas_call | solution.py:1203
  199.5 3.8 %shard_map.274 = (f32[1280,256]{1,0:T(8,128)}, f32[1280,256]{1,0:T(8,128)}, f32[27,128]{1,0:T(8,128)}, f32[27,128]{1,0:T(8,128)}, f32[12,3456]{1,0:T(8,128)}, /*...) custom-call(f32[1280,256]{1,0:T(8,128)} %get-tuple-element.65.refs_0, ...), custom_call_target="tpu_custom_call" | custom-call | tf_op jit(solution)/shard_map/pallas_call | solution.py:1444
  203.3 1.3 convert_element_type.10
  (3 shorter events, 0.0 us)

commit v8 on v7

--- a/solution.py
+++ b/solution.py
@@ -217,16 +217,15 @@
             headw_ref[tap * ROWS12 : (tap + 1) * ROWS12, :] = wide_rows[:ROWS12, :width].astype(
                 LOWTYPE
             )
-        row = lax.broadcasted_iota(jnp.int32, (ROWS12, C1), 0)
-        lane = lax.broadcasted_iota(jnp.int32, (ROWS12, C1), 1)
-        bias = jnp.where(row == lane, vec_ref[23:24, :], 0.0)
+        row = lax.broadcasted_iota(jnp.int32, (ROWS12, 12), 0)
+        lane = lax.broadcasted_iota(jnp.int32, (ROWS12, 12), 1)
+        tail = vec_ref[pl.ds(3 * C1 + 10 * mid, 12)].reshape(1, 12)
+        bias = jnp.where(row == lane, tail, 0.0)
         headb_ref[...] = jnp.sum(bias, axis=1, keepdims=True) + jnp.zeros((ROWS12, C1), F32)
 
     def vec(row, chans=mid):
-        if chans == C1:
-            return vec_ref[row : row + 1, :]
-        row = 2 * row - 3
-        return jnp.concatenate([vec_ref[row : row + 1, :], vec_ref[row + 1 : row + 2, :]], axis=1)
+        start = row * C1 if chans == C1 else 3 * C1 + (row - 3) * mid
+        return vec_ref[pl.ds(start, chans)].reshape(1, chans)
 
     def add_vec(row, value):
         gvec_ref[row : row + 1, : value.shape[1]] += value
@@ -787,8 +786,8 @@
     peers,
     rows_ref,
     misc_ref,
-    weight_ref,
-    moment_ref,
+    weight_hbm,
+    moment_hbm,
     stem_ref,
     stemm_ref,
     head_ref,
@@ -814,6 +813,7 @@
     recv3,
     recvs3,
     gathered,
+    gathered_small,
     misc1,
     misc2,
     misc3,
@@ -827,6 +827,10 @@
     x_one,
     flat,
     head_row,
+    own_half,
+    weight_ref,
+    moment_ref,
+    sem_load,
     sem1,
     sem2,
     sem3,
@@ -840,18 +844,25 @@
     semm1,
     semm2,
     semm3,
+    semas,
+    sembs,
 ):
     mid = CHANNELS_MID
     chips = peers // 2
     chunk, small_chunk = chunk_rows(owners, peers)
     block = block_rows(owners, peers)
-    held = chunk + small_chunk
     own_rows = weight_ref.shape[0]
     z = lax.axis_index("bucket")
     peer = lax.axis_index("batch")
     chip, core = peer // 2, peer % 2
     partner = {"batch": chip * 2 + 1 - core}
     started = []
+    half_rows = pl.ds(pl.multiple_of(core * chips * block, 16), chips * block)
+    load_half = pltpu.make_async_copy(rows_ref.at[half_rows, :], own_half, sem_load.at[0])
+    load_moment = pltpu.make_async_copy(moment_hbm, moment_ref, sem_load.at[1])
+    load_weight = pltpu.make_async_copy(weight_hbm, weight_ref, sem_load.at[2])
+    for load in (load_half, load_moment, load_weight):
+        load.start()
 
     def same_core(k):
         return {"batch": lax.rem(chip + k, chips) * 2 + core}
@@ -888,9 +899,10 @@
         start = base + lax.rem(z + part, owners) * chunk
         return pl.ds(pl.multiple_of(start, 16), chunk)
 
-    def base_of(k, other_core):
-        owner_core = 1 - core if other_core else core
-        return (owner_core * chips + lax.rem(chip + k, chips)) * block
+    def base_of(k):
+        return lax.rem(chip + k, chips) * block
+
+    other_half = (1 - core) * chips * block
 
     misc_copy = send(misc_ref, misc1, semm1, 0, partner)
     order = list(range(1, chips)) + [0]
@@ -898,7 +910,7 @@
     for number, part in enumerate(parts):
         for k in order:
             first[part, k] = send(
-                rows_ref.at[part_rows(part, base_of(k, True)), :],
+                rows_ref.at[part_rows(part, other_half + base_of(k)), :],
                 recv1.at[k, part_rows(part), :],
                 sem1,
                 number * chips + k,
@@ -910,12 +922,13 @@
     misc_copies = [
         send(misc2.at[chip], misc2.at[chip], semm2, k - 1, same_core(k)) for k in range(1, chips)
     ]
+    load_half.wait()
     second = {}
     for number, part in enumerate(parts):
         rows = part_rows(part)
         for k in order:
             first[part, k].wait_recv()
-            total = rows_ref[part_rows(part, base_of(k, False)), :] + recv1[k, rows, :]
+            total = own_half[part_rows(part, base_of(k)), :] + recv1[k, rows, :]
             if k == 0:
                 own2[rows, :] = total
             else:
@@ -960,15 +973,18 @@
     for other in range(owners - 1):
         total = total + recv3[other]
     slot = core * chips + chip
-    gathered[slot, :chunk, :] = total
+    gathered[slot] = total
     total = recvs3[0]
     for other in range(1, owners):
         total = total + recvs3[other]
-    gathered[slot, chunk:, :] = total
+    gathered_small[slot] = total
 
     here = gathered.at[slot]
     plane = [send(here, here, sema, k - 1, same_core(k)) for k in range(1, chips)]
     cross = [send(here, here, semb, 0, partner)]
+    here = gathered_small.at[slot]
+    plane_small = [send(here, here, semas, k - 1, same_core(k)) for k in range(1, chips)]
+    cross_small = [send(here, here, sembs, 0, partner)]
 
     for copy in misc_copies:
         copy.wait_recv()
@@ -1005,6 +1021,8 @@
     for copy in cross:
         copy.wait_recv()
 
+    load_moment.wait()
+
     for owner_peer in range(peers):
         start = owner_peer * chunk
         size = min(chunk, own_rows - start)
@@ -1025,14 +1043,17 @@
                 mine_u[share:, :] = jnp.zeros((mine_u.shape[0] - share, mid), F32)
 
     mine = mine_u[...]
-    gram_part[...] = lax.dot_general(
+    gram = lax.dot_general(
         mine,
         mine,
         (((0,), (0,)), ((), ())),
         preferred_element_type=F32,
         precision=EXACT_PRECISION,
     )
-    part = mid // owners
+    gram_part[:C1, :] = gram[:C1, :]
+    gram_part[C1:, :C1] = gram[C1 : C1 + 64, C1:]
+    gram_part[C1:, C1:] = gram[C1 + 64 :, C1:]
+    part = gram_part.shape[0] // owners
     copies = []
     for k in range(1, owners):
         start = pl.multiple_of(lax.rem(z + k, owners) * part, 8)
@@ -1040,12 +1061,17 @@
     own_part = pl.ds(pl.multiple_of(z * part, 8), part)
     gram_recv[z] = gram_part[own_part, :]
 
-    chunk_s = small_chunk
+    for k, copy in zip(range(1, chips), plane_small):
+        copy.wait_recv()
+        other = gathered_small.at[core * chips + lax.rem(chip + chips - k, chips)]
+        cross_small.append(send(other, other, sembs, k, partner))
+    for copy in cross_small:
+        copy.wait_recv()
     tiles = []
-    for tile in range(SMALL_ROWS // 16):
-        row = tile * 16
-        at = chunk + row % chunk_s
-        tiles.append(gathered[slot_of(row // chunk_s, peers), at : at + 16, :] * inverse)
+    for row in range(0, SMALL_ROWS, 16):
+        at = row % small_chunk
+        tile = gathered_small[slot_of(row // small_chunk, peers), at : at + 16, :]
+        tiles.append(tile * inverse)
     small[...] = jnp.zeros_like(small)
     for tap in range(TAPS):
         lanes = slice(tap * (mid + C1), tap * (mid + C1) + mid)
@@ -1092,7 +1118,17 @@
     ]
     for copy in copies:
         copy.wait_recv()
-    gram = gram_all[...]
+    upper, corner = gram_all[:C1, :], gram_all[C1:, :]
+    gram = jnp.concatenate(
+        [
+            upper,
+            jnp.concatenate(
+                [upper[:, C1:].T, jnp.concatenate([corner[:, :C1], corner[:, C1:]], axis=0)],
+                axis=1,
+            ),
+        ],
+        axis=0,
+    )
     eye = identity(mid)
     trace = jnp.sum(jnp.sum(gram * eye, axis=1, keepdims=True), axis=0, keepdims=True)
     scale = lax.rsqrt(trace + NORM_EPS)
@@ -1131,6 +1167,7 @@
             for copy in plane + cross:
                 copy.wait_send()
 
+    load_weight.wait()
     for (task_chip, task_core), share, start in zip(TASKS, shares, starts):
         buffer = (x_zero, x_one)[task_core]
         rows = slice(start, start + share)
@@ -1146,7 +1183,7 @@
     chunk, small_chunk = chunk_rows(owners, peers)
     block = block_rows(owners, peers)
     rows = operands[2].shape[0]
-    part = mid // owners
+    part = 192 // owners
     shares = [seg_rows // owners for seg_rows in segment_rows()]
     most = [max(s for s, t in zip(shares, TASKS) if t[1] == core) for core in (0, 1)]
     out_shapes = [
@@ -1169,20 +1206,24 @@
         ((owners - 1, chunk, mid), F32),
         ((owners - 1, chunk, mid), F32),
         ((owners, small_chunk, mid), F32),
-        ((peers, chunk + small_chunk, mid), F32),
+        ((peers, chunk, mid), F32),
+        ((peers, small_chunk, mid), F32),
         (operands[1].shape, F32),
         ((chips,) + operands[1].shape, F32),
         ((owners,) + operands[1].shape, F32),
         ((rows, mid), F32),
         ((max(most), mid), F32),
-        ((mid, mid), F32),
+        ((192, mid), F32),
         ((owners, part, mid), F32),
-        ((mid, mid), F32),
+        ((192, mid), F32),
         ((64, SMALL_LANES + C1), F32),
         ((4, most[0], mid), LOWTYPE),
         ((4, most[1], mid), LOWTYPE),
         ((3 * C1 + 10 * mid + C1,), F32),
         ((8, C1), F32),
+        ((chips * block, mid), F32),
+        ((rows, mid), F32),
+        ((rows, mid), F32),
     ]
     sems = [
         (owners + 1) * chips,
@@ -1198,14 +1239,18 @@
         1,
         chips - 1,
         owners - 1,
+        chips - 1,
+        chips,
     ]
+    hbm = pl.BlockSpec(memory_space=pl.ANY)
     vmem = pl.BlockSpec(memory_space=pltpu.VMEM)
     return pl.pallas_call(
         functools.partial(muon_body, owners, peers),
         out_shape=[jax.ShapeDtypeStruct(shape, kind) for shape, kind in out_shapes],
-        in_specs=[vmem] * len(operands),
+        in_specs=[hbm, vmem, hbm, hbm] + [vmem] * (len(operands) - 4),
         out_specs=[vmem] * len(out_shapes),
         scratch_shapes=[pltpu.VMEM(shape, kind) for shape, kind in scratch]
+        + [pltpu.SemaphoreType.DMA((3,))]
         + [pltpu.SemaphoreType.DMA((2, count)) for count in sems],
         compiler_params=pltpu.CompilerParams(
             vmem_limit_bytes=VMEM_BYTES, collective_id=0, has_side_effects=True
@@ -1291,10 +1336,17 @@
     first = [send(here, here, sema, k - 1, along(k)) for k in range(1, owners)]
 
     samples = mask_ref.shape[0]
+    row = lax.broadcasted_iota(jnp.int32, (samples, samples), 0)
+    lane = lax.broadcasted_iota(jnp.int32, (samples, samples), 1)
+
+    def column(k):
+        return jnp.sum(jnp.where(row == lane, image_ref[k : k + 1, :], 0.0), axis=1, keepdims=True)
+
+    keep, spread, weight = column(0), column(1), column(2)
     left[...] = jnp.zeros_like(left)
     for c in range(3):
         noise = noise_ref[c]
-        noisy = image_ref[:, 0:1] * images_ref[c] + image_ref[:, 1:2] * noise
+        noisy = keep * images_ref[c] + spread * noise
         left[c, :samples, :] = noisy.astype(LOWTYPE)
         one = noise.astype(LOWTYPE)
         rest = noise - one.astype(F32)
@@ -1315,7 +1367,7 @@
         pick = jnp.where(pixel == wanted, 1.0, 0.0).astype(LOWTYPE)
         rows = left.shape[1]
         moved = dot_nn(left[...].reshape(13 * rows, S * S), pick)
-        maskw = moved[12 * rows : 12 * rows + samples] * image_ref[:, 2:3]
+        maskw = moved[12 * rows : 12 * rows + samples] * weight
         for c in range(3):
             k = quarter * 3 + c
             noisy_ref[:, k, :] = moved[c * rows : c * rows + samples]
@@ -1430,16 +1482,16 @@
     values, outs = refs[:10], refs[10:]
     for source, target in zip(values[:9], outs[:9]):
         target[...] = source[...]
-    for source, target in zip((values[0], values[2], values[4]), outs[9:12]):
+    for source, target in zip((values[0], values[2], values[4], values[6]), outs[9:13]):
         target[...] = source[...].astype(LOWTYPE)
     sums = values[9]
-    outs[12][...] = sums[0:1, 0:1]
-    outs[13][...] = sums[1:2, 0:1]
+    outs[13][...] = sums[0:1, 0:1]
+    outs[14][...] = sums[1:2, 0:1]
 
 
 def close_call(values):
     shapes = [(v.shape, F32) for v in values[:9]]
-    shapes += [(values[k].shape, LOWTYPE) for k in (0, 2, 4)] + [((1, 1), F32)] * 2
+    shapes += [(values[k].shape, LOWTYPE) for k in (0, 2, 4, 6)] + [((1, 1), F32)] * 2
     vmem = pl.BlockSpec(memory_space=pltpu.VMEM)
     return pl.pallas_call(
         close_body,
@@ -1462,18 +1514,13 @@
     both = (np.einsum("ayt,bxu->abyxtu", counts, counts) * 0.25).reshape(3, 3, 4, 3, 3)
     for c in range(3):
         full[:, :, c:12:3, :, :, c] = both
-    return jnp.asarray(full.reshape(TAPS * ROWS12, 27), F32)
-
-
-def lanes_of(vector):
-    rows = -(-vector.shape[0] // (8 * C1)) * 8
-    return jnp.pad(vector, (0, rows * C1 - vector.shape[0]), constant_values=1.0).reshape(rows, C1)
+    return np.pad(full.reshape(TAPS * ROWS12, 27), ((0, 0), (0, 5))).astype(np.float32)
 
 
 def same_group(chans):
     group = np.arange(chans) // (chans // GROUPS)
     same = (group[:, None] == group[None, :]) / (PLACES * (chans // GROUPS))
-    return jnp.asarray(same, LOWTYPE)
+    return same.astype(LOWTYPE)
 
 
 def shards(
@@ -1494,7 +1541,7 @@
     owners, peers = lax.axis_size("bucket"), lax.axis_size("batch")
     samples = images.shape[0]
     level, weight = plan(timesteps)
-    per_image = jnp.stack([jnp.sqrt(level), jnp.sqrt(1.0 - level), weight], axis=1)
+    per_image = jnp.stack([jnp.sqrt(level), jnp.sqrt(1.0 - level), weight], axis=0)
     conv1, conv1b, conv2, conv2b, skip, temb, qkv, outw, noisy, noise, mask_weight = open_call(
         owners,
         peers,
@@ -1506,7 +1553,6 @@
             per_image,
         ],
     )
-    spread = stem_spread()
     head_turned = head_weight.T
     rows_out, misc = unet_call(
         samples,
@@ -1527,10 +1573,10 @@
             temb,
             qkv,
             outw,
-            lanes_of(vectors),
+            vectors,
             same_group(C1),
             same_group(CHANNELS_MID),
-            jnp.pad(spread, ((0, 0), (0, 5))),
+            stem_spread(),
         ],
     )
     values = muon_call(
@@ -1563,6 +1609,7 @@
         matrix_copies,
         stem_copy,
         head_copy,
+        vector_copy,
         loss_sum,
         weight_sum,
     ) = close_call(values)
@@ -1583,7 +1630,7 @@
         new_vectors,
         new_firsts,
         new_seconds,
-        new_vectors.astype(LOWTYPE),
+        vector_copy,
     )
 
 

time: 205 us -> 198 us (0.966)
  Pallas kernels: 198 us -> 194 us
    pallas_call x1, Pallas kernels: 87.3 us -> 83 us  [muon_call(): pl.pallas_call(functools.partial(muon_body, owners, peers), out_shape=[ja...]
where the time goes in v8:
time: 198 us
  Pallas kernels  194 us (98%)
  other arithmetic  2.79 us (1%)
    pallas_call x1, Pallas kernels, muon_call(): pl.pallas_call(functools.partial(muon_body, owners, peers), out_shape=[ja...  83 us
    pallas_call x1, Pallas kernels, unet_call(): pl.pallas_call(functools.partial(unet_body, group, steps, owners, peers),...  81 us
    pallas_call x1, Pallas kernels, open_call(): pl.pallas_call(functools.partial(open_body, owners, peers), out_shape=[ja...  26.2 us

profile of v8, /device:TPU:0, one launch (start us, length us, event | category | flops | bytes accessed | tf_op | source)
XLA Modules:
  0.0 197.7 jit_solution(8967315017137633129)
XLA Ops:
  0.6 0.7 convert_element_type.4
  1.3 0.7 sqrt_bitcast_fusion.1
  2.0 0.6 pad_maximum_fusion.1.image_ref
  2.6 0.2 multiply_sine_fusion
  2.8 0.6 divide_multiply_fusion.time_ref
  3.4 26.2 %shard_map.271 = (bf16[1152,256]{1,0:T(8,128)(2,1)}, bf16[384,768]{1,0:T(8,128)(2,1)}, bf16[2304,256]{1,0:T(8,128)(2,1)}, bf16[768,768]{1,0:T(8,128)(2,1)}, bf16...) custom-call(f32[1280,256]{1,0:T(8,128)} %weight_hbm.1, ...), custom_call_target="tpu_custom_call" | custom-call | tf_op jit(solution)/shard_map/pallas_call | solution.py:1463
  29.7 81.0 %shard_map.272 = (f32[5376,256]{1,0:T(8,128)}, f32[16,384]{1,0:T(8,128)}) custom-call(f32[20,16,256]{2,1,0:T(8,128)} %get-tuple-element.53.noisy_ref, f32[20,16,256]{2,1,0:T(8,128)} %get-tuple-element.54.noise_ref, f32[20,16,256]{2,1,0:T(8,128)} %get-tuple-element.55.maskw_ref, f32[20,512]{1,0:T(8,128)} %divide_multiply_fusion.time_ref, f32[27,128]{1,0:T(8,128)} %stem_ref.3, ...), custom_call_target="tpu_custom_call" | custom-call | tf_op jit(solution)/shard_map/pallas_call | solution.py:751
  110.7 83.0 %shard_map.273 = (f32[1280,256]{1,0:T(8,128)}, f32[1280,256]{1,0:T(8,128)}, f32[27,128]{1,0:T(8,128)}, f32[27,128]{1,0:T(8,128)}, f32[12,3456]{1,0:T(8,128)}, /*...) custom-call(f32[5376,256]{1,0:T(8,128)} %get-tuple-element.64.rows_ref, ...), custom_call_target="tpu_custom_call" | custom-call | tf_op jit(solution)/shard_map/pallas_call | solution.py:1247
  193.7 3.9 %shard_map.274 = (f32[1280,256]{1,0:T(8,128)}, f32[1280,256]{1,0:T(8,128)}, f32[27,128]{1,0:T(8,128)}, f32[27,128]{1,0:T(8,128)}, f32[12,3456]{1,0:T(8,128)}, /*...) custom-call(f32[1280,256]{1,0:T(8,128)} %get-tuple-element.66.refs_0, ...), custom_call_target="tpu_custom_call" | custom-call | tf_op jit(solution)/shard_map/pallas_call | solution.py:1496
  (2 shorter events, 0.0 us)

commit v9 on v8

--- a/solution.py
+++ b/solution.py
@@ -781,6 +781,28 @@
     return (rows == cols).astype(F32)
 
 
+def task_pieces(owners, peers):
+    chunk, _ = chunk_rows(owners, peers)
+    pieces = []
+    packed = 0
+    for seg, seg_rows in enumerate(segment_rows()):
+        share = seg_rows // owners
+        done, number = 0, 0
+        while done < share:
+            row = packed + done
+            size = min(share - done, chunk - row % chunk)
+            pieces.append((seg, number, row // chunk, row % chunk, size, done))
+            done += size
+            number += 1
+        packed += share
+    return pieces
+
+
+def task_peers(seg, peers):
+    chip, core = TASKS[seg]
+    return [(base + chip) * 2 + core for base in range(0, peers // 2, 4)]
+
+
 def muon_body(
     owners,
     peers,
@@ -817,7 +839,7 @@
     misc1,
     misc2,
     misc3,
-    direction,
+    mine_g,
     mine_u,
     gram_part,
     gram_recv,
@@ -846,6 +868,7 @@
     semm3,
     semas,
     sembs,
+    semp,
 ):
     mid = CHANNELS_MID
     chips = peers // 2
@@ -885,7 +908,7 @@
         return copy
 
     barrier = pltpu.get_barrier_semaphore()
-    friends = [partner] + [same_core(k) for k in range(1, chips)]
+    friends = [{"batch": lax.rem(peer + k, peers)} for k in range(1, peers)]
     friends += [along(k) for k in range(1, owners)]
     for friend in friends:
         pl.semaphore_signal(barrier, inc=1, device_id=friend, device_id_type=MESH)
@@ -979,12 +1002,34 @@
         total = total + recvs3[other]
     gathered_small[slot] = total
 
-    here = gathered.at[slot]
-    plane = [send(here, here, sema, k - 1, same_core(k)) for k in range(1, chips)]
-    cross = [send(here, here, semb, 0, partner)]
-    here = gathered_small.at[slot]
-    plane_small = [send(here, here, semas, k - 1, same_core(k)) for k in range(1, chips)]
-    cross_small = [send(here, here, sembs, 0, partner)]
+    pieces = task_pieces(owners, peers)
+
+    def piece_copy(piece, index, target):
+        seg, number, source, row, size, place = piece
+        return pltpu.make_async_remote_copy(
+            src_ref=gathered.at[slot_of(source, peers), pl.ds(row, size), :],
+            dst_ref=mine_g.at[pl.ds(place, size), :],
+            send_sem=semp.at[0, index],
+            recv_sem=semp.at[1, number],
+            device_id={"batch": target},
+            device_id_type=MESH,
+        )
+
+    def from_peer(source):
+        copies = []
+        for piece in pieces:
+            if piece[2] == source:
+                for target in task_peers(piece[0], peers):
+                    if target != source:
+                        copies.append(piece_copy(piece, len(copies), target))
+        return copies
+
+    for source in range(peers):
+
+        @pl.when(peer == source)
+        def _(source=source):
+            for copy in from_peer(source):
+                copy.start()
 
     for copy in misc_copies:
         copy.wait_recv()
@@ -1014,31 +1059,30 @@
     )
     nvec_ref[...] = vec_ref[...] - LR_ADAM * change
 
-    for k, copy in zip(range(1, chips), plane):
-        copy.wait_recv()
-        other = gathered.at[core * chips + lax.rem(chip + chips - k, chips)]
-        cross.append(send(other, other, semb, k, partner))
-    for copy in cross:
-        copy.wait_recv()
-
     load_moment.wait()
-
-    for owner_peer in range(peers):
-        start = owner_peer * chunk
-        size = min(chunk, own_rows - start)
-        if size > 0:
-            grad = gathered[slot_of(owner_peer, peers), :size, :] * inverse
-            rows = slice(start, start + size)
-            moment = MOMENTUM * moment_ref[rows, :] + grad
-            newm_ref[rows, :] = moment
-            direction[rows, :] = grad + MOMENTUM * moment
+    for target in range(peers):
+
+        @pl.when(peer == target)
+        def _(target=target):
+            for piece in pieces:
+                seg, number, source, row, size, place = piece
+                if target in task_peers(seg, peers):
+                    if source == target:
+                        mine_g[place : place + size, :] = gathered[
+                            slot_of(source, peers), row : row + size, :
+                        ]
+                    else:
+                        piece_copy(piece, 0, target).wait_recv()
+
     shares = [rows // owners for rows in segment_rows()]
     starts = [sum(shares[:k]) for k in range(len(shares))]
     for (task_chip, task_core), share, start in zip(TASKS, shares, starts):
 
         @pl.when((lax.rem(chip, 4) == task_chip) & (core == task_core))
         def _(share=share, start=start):
-            mine_u[:share, :] = direction[start : start + share, :]
+            grad = mine_g[:share, :] * inverse
+            moment = MOMENTUM * moment_ref[start : start + share, :] + grad
+            mine_u[:share, :] = grad + MOMENTUM * moment
             if share < mine_u.shape[0]:
                 mine_u[share:, :] = jnp.zeros((mine_u.shape[0] - share, mid), F32)
 
@@ -1061,10 +1105,89 @@
     own_part = pl.ds(pl.multiple_of(z * part, 8), part)
     gram_recv[z] = gram_part[own_part, :]
 
+    here = gathered.at[slot]
+    plane = [send(here, here, sema, k - 1, same_core(k)) for k in range(1, chips)]
+    cross = [send(here, here, semb, 0, partner)]
+    here = gathered_small.at[slot]
+    plane_small = [send(here, here, semas, k - 1, same_core(k)) for k in range(1, chips)]
+    cross_small = [send(here, here, sembs, 0, partner)]
+
+    for copy in copies:
+        copy.wait_recv()
+    gram_all[own_part, :] = sum([gram_recv[k] for k in range(1, owners)], gram_recv[0])
+    copies = [
+        send(gram_all.at[own_part, :], gram_all.at[own_part, :], semh, k - 1, along(k))
+        for k in range(1, owners)
+    ]
+    for copy in copies:
+        copy.wait_recv()
+    upper, corner = gram_all[:C1, :], gram_all[C1:, :]
+    gram = jnp.concatenate(
+        [
+            upper,
+            jnp.concatenate(
+                [upper[:, C1:].T, jnp.concatenate([corner[:, :C1], corner[:, C1:]], axis=0)],
+                axis=1,
+            ),
+        ],
+        axis=0,
+    )
+    eye = identity(mid)
+    trace = jnp.sum(jnp.sum(gram * eye, axis=1, keepdims=True), axis=0, keepdims=True)
+    scale = lax.rsqrt(trace + NORM_EPS)
+    product = ns_chain(gram * (scale * scale), eye) * scale
+    for k, copy in zip(range(1, chips), plane):
+        copy.wait_recv()
+        other = gathered.at[core * chips + lax.rem(chip + chips - k, chips)]
+        cross.append(send(other, other, semb, k, partner))
     for k, copy in zip(range(1, chips), plane_small):
         copy.wait_recv()
         other = gathered_small.at[core * chips + lax.rem(chip + chips - k, chips)]
         cross_small.append(send(other, other, sembs, k, partner))
+    turned = dot_nn(mine_u[...], product, EXACT_PRECISION)
+
+    place = lax.rem(chip, 4)
+    base = chip - place
+
+    def in_group(k):
+        return {"batch": (base + lax.rem(place + k, 4)) * 2 + core}
+
+    buffers = (x_zero, x_one)
+
+    def step_copy(buffer, index, sems, slot, device):
+        there = buffer.at[index]
+        return pltpu.make_async_remote_copy(
+            src_ref=there,
+            dst_ref=there,
+            send_sem=sems.at[0, slot],
+            recv_sem=sems.at[1, slot],
+            device_id=device,
+            device_id_type=MESH,
+        )
+
+    def step_copies(buffer):
+        copies = [step_copy(buffer, place, semx, k - 1, in_group(k)) for k in range(1, 4)]
+        return copies, step_copy(buffer, place, semy, 0, partner)
+
+    for task_core, buffer in enumerate(buffers):
+
+        @pl.when(core == task_core)
+        def _(buffer=buffer):
+            buffer[place] = turned[: buffer.shape[1]].astype(LOWTYPE)
+            copies, own = step_copies(buffer)
+            for copy in copies:
+                copy.start()
+            own.start()
+
+    for copy in cross:
+        copy.wait_recv()
+    for owner_peer in range(peers):
+        start = owner_peer * chunk
+        size = min(chunk, own_rows - start)
+        if size > 0:
+            grad = gathered[slot_of(owner_peer, peers), :size, :] * inverse
+            rows = slice(start, start + size)
+            newm_ref[rows, :] = MOMENTUM * moment_ref[rows, :] + grad
     for copy in cross_small:
         copy.wait_recv()
     tiles = []
@@ -1109,62 +1232,22 @@
     nhead_ref[...] = head_ref[...] * keep - LR_MUON * small[head_part]
     nstem_ref[...] = stem_ref[...] * keep - LR_MUON * small[stem_part]
 
-    for copy in copies:
-        copy.wait_recv()
-    gram_all[own_part, :] = sum([gram_recv[k] for k in range(1, owners)], gram_recv[0])
-    copies = [
-        send(gram_all.at[own_part, :], gram_all.at[own_part, :], semh, k - 1, along(k))
-        for k in range(1, owners)
-    ]
-    for copy in copies:
-        copy.wait_recv()
-    upper, corner = gram_all[:C1, :], gram_all[C1:, :]
-    gram = jnp.concatenate(
-        [
-            upper,
-            jnp.concatenate(
-                [upper[:, C1:].T, jnp.concatenate([corner[:, :C1], corner[:, C1:]], axis=0)],
-                axis=1,
-            ),
-        ],
-        axis=0,
-    )
-    eye = identity(mid)
-    trace = jnp.sum(jnp.sum(gram * eye, axis=1, keepdims=True), axis=0, keepdims=True)
-    scale = lax.rsqrt(trace + NORM_EPS)
-    product = ns_chain(gram * (scale * scale), eye) * scale
-    turned = dot_nn(mine_u[...], product, EXACT_PRECISION)
-
-    place = lax.rem(chip, 4)
-    base = chip - place
-
-    def in_group(k):
-        return {"batch": (base + lax.rem(place + k, 4)) * 2 + core}
-
-    for task_core, buffer in ((0, x_zero), (1, x_one)):
+
+    for task_core, buffer in enumerate(buffers):
 
         @pl.when(core == task_core)
-        def _(buffer=buffer, other_buffer=(x_one, x_zero)[task_core]):
-            size = buffer.shape[1]
-            buffer[place] = turned[:size].astype(LOWTYPE)
-            here = buffer.at[place]
-            plane = [send(here, here, semx, k - 1, in_group(k), False) for k in range(1, 4)]
-            cross = [send(here, here, semy, 0, partner, False)]
+        def _(buffer=buffer, other_buffer=buffers[1 - task_core]):
+            copies, own = step_copies(buffer)
+            forwards = [own]
             for k in range(1, 4):
-                plane[k - 1].wait_recv()
-                other = buffer.at[lax.rem(place + 4 - k, 4)]
-                cross.append(send(other, other, semy, k, partner, False))
+                copies[k - 1].wait_recv()
+                forwards.append(
+                    step_copy(buffer, lax.rem(place + 4 - k, 4), semy, k, partner)
+                )
+                forwards[-1].start()
             for k in range(4):
-                there = other_buffer.at[lax.rem(place + 4 - k, 4)]
-                pltpu.make_async_remote_copy(
-                    src_ref=there,
-                    dst_ref=there,
-                    send_sem=semy.at[0, k],
-                    recv_sem=semy.at[1, k],
-                    device_id=partner,
-                    device_id_type=MESH,
-                ).wait_recv()
-            for copy in plane + cross:
+                step_copy(other_buffer, lax.rem(place + 4 - k, 4), semy, k, partner).wait_recv()
+            for copy in copies + forwards:
                 copy.wait_send()
 
     load_weight.wait()
@@ -1175,6 +1258,12 @@
         new_ref[rows, :] = fresh
     for copy in started:
         copy.wait_send()
+    for source in range(peers):
+
+        @pl.when(peer == source)
+        def _(source=source):
+            for copy in from_peer(source):
+                copy.wait_send()
 
 
 def muon_call(owners, peers, operands):
@@ -1184,6 +1273,7 @@
     block = block_rows(owners, peers)
     rows = operands[2].shape[0]
     part = 192 // owners
+    pieces = task_pieces(owners, peers)
     shares = [seg_rows // owners for seg_rows in segment_rows()]
     most = [max(s for s, t in zip(shares, TASKS) if t[1] == core) for core in (0, 1)]
     out_shapes = [
@@ -1211,7 +1301,7 @@
         (operands[1].shape, F32),
         ((chips,) + operands[1].shape, F32),
         ((owners,) + operands[1].shape, F32),
-        ((rows, mid), F32),
+        ((max(most), mid), F32),
         ((max(most), mid), F32),
         ((192, mid), F32),
         ((owners, part, mid), F32),
@@ -1241,6 +1331,7 @@
         owners - 1,
         chips - 1,
         chips,
+        len(pieces) * (peers // 8),
     ]
     hbm = pl.BlockSpec(memory_space=pl.ANY)
     vmem = pl.BlockSpec(memory_space=pltpu.VMEM)

time: 198 us -> 192 us (0.970)
  Pallas kernels: 194 us -> 187 us
    pallas_call x1, Pallas kernels: 83 us -> 76 us  [muon_call(): pl.pallas_call(functools.partial(muon_body, owners, peers), out_shape=[ja...]
where the time goes in v9:
time: 192 us; the launch traced here: 191 us
  Pallas kernels  187 us (97%)
  other arithmetic  2.79 us (1%)
    pallas_call x1, Pallas kernels, unet_call(): pl.pallas_call(functools.partial(unet_body, group, steps, owners, peers),...  81 us
    pallas_call x1, Pallas kernels, muon_call(): pl.pallas_call(functools.partial(muon_body, owners, peers), out_shape=[ja...  76 us
    pallas_call x1, Pallas kernels, open_call(): pl.pallas_call(functools.partial(open_body, owners, peers), out_shape=[ja...  26.2 us
    pallas_call x1, Pallas kernels, close_call(): pl.pallas_call(close_body, out_shape=[jax.ShapeDtypeStruct(shape, kind) f...  3.85 us

profile of v9, /device:TPU:0, one launch (start us, length us, event | category | flops | bytes accessed | tf_op | source)
XLA Modules:
  0.0 190.8 jit_solution(15753522944365931991)
XLA Ops:
  0.6 0.7 convert_element_type.4
  1.3 0.7 sqrt_bitcast_fusion.1
  2.0 0.6 pad_maximum_fusion.1.image_ref
  2.6 0.2 multiply_sine_fusion
  2.8 0.6 divide_multiply_fusion.time_ref
  3.4 26.2 %shard_map.271 = (bf16[1152,256]{1,0:T(8,128)(2,1)}, bf16[384,768]{1,0:T(8,128)(2,1)}, bf16[2304,256]{1,0:T(8,128)(2,1)}, bf16[768,768]{1,0:T(8,128)(2,1)}, bf16...) custom-call(f32[1280,256]{1,0:T(8,128)} %weight_hbm.1, ...), custom_call_target="tpu_custom_call" | custom-call | tf_op jit(solution)/shard_map/pallas_call | solution.py:1554
  29.7 81.0 %shard_map.272 = (f32[5376,256]{1,0:T(8,128)}, f32[16,384]{1,0:T(8,128)}) custom-call(f32[20,16,256]{2,1,0:T(8,128)} %get-tuple-element.53.noisy_ref, f32[20,16,256]{2,1,0:T(8,128)} %get-tuple-element.54.noise_ref, f32[20,16,256]{2,1,0:T(8,128)} %get-tuple-element.55.maskw_ref, f32[20,512]{1,0:T(8,128)} %divide_multiply_fusion.time_ref, f32[27,128]{1,0:T(8,128)} %stem_ref.3, ...), custom_call_target="tpu_custom_call" | custom-call | tf_op jit(solution)/shard_map/pallas_call | solution.py:751
  110.7 76.0 %shard_map.273 = (f32[1280,256]{1,0:T(8,128)}, f32[1280,256]{1,0:T(8,128)}, f32[27,128]{1,0:T(8,128)}, f32[27,128]{1,0:T(8,128)}, f32[12,3456]{1,0:T(8,128)}, /*...) custom-call(f32[5376,256]{1,0:T(8,128)} %get-tuple-element.64.rows_ref, ...), custom_call_target="tpu_custom_call" | custom-call | tf_op jit(solution)/shard_map/pallas_call | solution.py:1338
  186.7 3.9 %shard_map.274 = (f32[1280,256]{1,0:T(8,128)}, f32[1280,256]{1,0:T(8,128)}, f32[27,128]{1,0:T(8,128)}, f32[27,128]{1,0:T(8,128)}, f32[12,3456]{1,0:T(8,128)}, /*...) custom-call(f32[1280,256]{1,0:T(8,128)} %get-tuple-element.66.refs_0, ...), custom_call_target="tpu_custom_call" | custom-call | tf_op jit(solution)/shard_map/pallas_call | solution.py:1587
  (2 shorter events, 0.0 us)

commit v10 on v9

--- a/solution.py
+++ b/solution.py
@@ -134,8 +134,6 @@
     qkv_ref,
     outw_ref,
     vec_ref,
-    same128_ref,
-    same256_ref,
     spread_ref,
     rows_ref,
     misc_ref,
@@ -178,6 +176,8 @@
     headb_ref,
     time_low,
     wide_rows,
+    same128_ref,
+    same256_ref,
 ):
     step = pl.program_id(0)
     mid = CHANNELS_MID
@@ -199,9 +199,14 @@
                 ref[g, :SIDE, :] = jnp.zeros((SIDE, ref.shape[2]), ref.dtype)
                 ref[g, HALO - SIDE :, :] = jnp.zeros((SIDE, ref.shape[2]), ref.dtype)
         shiftf[...] = jnp.zeros_like(shiftf)
+        for ref in (same128_ref, same256_ref):
+            width = ref.shape[0] // GROUPS
+            row = lax.broadcasted_iota(jnp.int32, ref.shape, 0) // width
+            lane = lax.broadcasted_iota(jnp.int32, ref.shape, 1) // width
+            ref[...] = jnp.where(row == lane, 1.0 / (PLACES * width), 0.0).astype(LOWTYPE)
         wide_rows[...] = jnp.zeros_like(wide_rows)
         samples = time_ref.shape[0]
-        wide_rows[:samples, :TEMB] = time_ref[...]
+        wide_rows[:samples, :TEMB] = time_ref[:, :TEMB]
         time_low[...] = wide_rows[: time_low.shape[0], :TEMB].astype(LOWTYPE)
         tproj[...] = dot_nn(time_low[...], temb_ref[...])
         wide_rows[:27, :C1] = stem_ref[...].astype(LOWTYPE).astype(F32)
@@ -747,6 +752,8 @@
         ((ROWS12, C1), F32),
         ((time_rows, TEMB), LOWTYPE),
         ((max(32, time_rows), TEMB), F32),
+        ((C1, C1), LOWTYPE),
+        ((mid, mid), LOWTYPE),
     ]
     return pl.pallas_call(
         functools.partial(unet_body, group, steps, owners, peers),
@@ -761,6 +768,7 @@
 
 TASKS = ((1, 0), (0, 0), (0, 1), (2, 0), (1, 1), (2, 1), (3, 0), (3, 1))
 MESH = pl.DeviceIdType.MESH
+LEAD = 2
 SMALL_LANES = 9 * (CHANNELS_MID + C1)
 
 
@@ -829,6 +837,7 @@
     sums_ref,
     recv1,
     own2,
+    passed,
     send2,
     recv2,
     send3,
@@ -916,14 +925,28 @@
 
     parts = [None] + list(range(1, owners)) + [0]
 
-    def part_rows(part, base=0):
-        if part is None:
-            return pl.ds(pl.multiple_of(base + owners * chunk, 16), small_chunk)
-        start = base + lax.rem(z + part, owners) * chunk
-        return pl.ds(pl.multiple_of(start, 16), chunk)
+    def part_rows(part, base=0, half=None):
+        start = base + (owners * chunk if part is None else lax.rem(z + part, owners) * chunk)
+        size = small_chunk if part is None else chunk
+        if half is not None:
+            size = size // 2
+            start = start + half * size
+        return pl.ds(pl.multiple_of(start, 8), size)
+
+    square = chips == 4
+    across_x = chip + 1 - 2 * lax.rem(chip, 2)
+    across_y = lax.rem(chip + 2, 4)
+
+    def near(k):
+        if not square:
+            return lax.rem(chip + k, chips)
+        return (chip, across_x, across_y, lax.rem(across_x + 2, 4))[k]
+
+    def at_chip(k):
+        return {"batch": near(k) * 2 + core}
 
     def base_of(k):
-        return lax.rem(chip + k, chips) * block
+        return near(k) * block
 
     other_half = (1 - core) * chips * block
 
@@ -947,42 +970,62 @@
     ]
     load_half.wait()
     second = {}
-    for number, part in enumerate(parts):
+    third = []
+
+    def add_cores(number):
+        part = parts[number]
         rows = part_rows(part)
         for k in order:
             first[part, k].wait_recv()
             total = own_half[part_rows(part, base_of(k)), :] + recv1[k, rows, :]
             if k == 0:
                 own2[rows, :] = total
-            else:
-                send2[k - 1, rows, :] = total
+                continue
+            send2[k - 1, rows, :] = total
+            if not square:
                 second[part, k] = send(
                     send2.at[k - 1, rows, :],
                     recv2.at[k - 1, rows, :],
                     sem2,
                     number * (chips - 1) + k - 1,
-                    same_core(k),
+                    at_chip(k),
                 )
-
-    for copy in misc_copies:
-        copy.wait_recv()
-    misc3[z] = sum([misc2[k] for k in range(1, chips)], misc2[0])
-    misc_copies = [
-        send(misc3.at[z], misc3.at[z], semm3, k - 1, along(k)) for k in range(1, owners)
-    ]
-    third = []
-    for part in parts:
-        for k in range(1, chips):
+        if square:
+            for index, (half, source, into, target) in enumerate(
+                ((0, 2, 1, 1), (1, 2, 1, 2), (0, 0, 0, 1), (1, 1, 0, 2))
+            ):
+                rows = part_rows(part, 0, half)
+                second[part, index] = send(
+                    send2.at[source, rows, :],
+                    recv2.at[into, rows, :],
+                    sem2,
+                    number * 6 + index,
+                    at_chip(target),
+                )
+
+    def pass_on(number):
+        part = parts[number]
+        for half, source, target in ((0, 1, 2), (1, 0, 1)):
+            second[part, half].wait_recv()
+            rows = part_rows(part, 0, half)
+            passed[rows, :] = send2[source, rows, :] + recv2[1, rows, :]
+            second[part, 4 + half] = send(
+                passed.at[rows, :], recv2.at[2, rows, :], sem2, number * 6 + 4 + half, at_chip(target)
+            )
+
+    def add_chips(number):
+        part = parts[number]
+        for k in (2, 3, 4, 5) if square else range(1, chips):
             second[part, k].wait_recv()
         rows = part_rows(part)
         total = own2[rows, :]
-        for other in range(chips - 1):
+        for other in (0, 2) if square else range(chips - 1):
             total = total + recv2[other, rows, :]
         if part is None:
             recvs3[z] = total
-            third += [
+            third.extend(
                 send(recvs3.at[z], recvs3.at[z], sems3, k - 1, along(k)) for k in range(1, owners)
-            ]
+            )
         elif part == 0:
             own2[rows, :] = total
         else:
@@ -990,6 +1033,22 @@
             third.append(
                 send(send3.at[part - 1], recv3.at[part - 1], sem3, part - 1, along(part))
             )
+
+    lead = LEAD if square else len(parts)
+    for turn in range(len(parts) + lead):
+        if turn < len(parts):
+            add_cores(turn)
+        if square and 0 <= turn - 1 < len(parts):
+            pass_on(turn - 1)
+        if turn == min(2, len(parts)):
+            for copy in misc_copies:
+                copy.wait_recv()
+            misc3[z] = sum([misc2[k] for k in range(1, chips)], misc2[0])
+            misc_copies = [
+                send(misc3.at[z], misc3.at[z], semm3, k - 1, along(k)) for k in range(1, owners)
+            ]
+        if 0 <= turn - lead < len(parts):
+            add_chips(turn - lead)
     for copy in third:
         copy.wait_recv()
     total = own2[pl.ds(pl.multiple_of(z * chunk, 16), chunk), :]
@@ -1291,6 +1350,7 @@
     scratch = [
         ((chips, block, mid), F32),
         ((block, mid), F32),
+        ((block, mid), F32),
         ((chips - 1, block, mid), F32),
         ((chips - 1, block, mid), F32),
         ((owners - 1, chunk, mid), F32),
@@ -1317,7 +1377,7 @@
     ]
     sems = [
         (owners + 1) * chips,
-        (owners + 1) * (chips - 1),
+        (owners + 1) * max(6, chips - 1),
         owners - 1,
         owners - 1,
         chips - 1,
@@ -1427,13 +1487,9 @@
     first = [send(here, here, sema, k - 1, along(k)) for k in range(1, owners)]
 
     samples = mask_ref.shape[0]
-    row = lax.broadcasted_iota(jnp.int32, (samples, samples), 0)
-    lane = lax.broadcasted_iota(jnp.int32, (samples, samples), 1)
-
-    def column(k):
-        return jnp.sum(jnp.where(row == lane, image_ref[k : k + 1, :], 0.0), axis=1, keepdims=True)
-
-    keep, spread, weight = column(0), column(1), column(2)
+    keep = image_ref[:, TEMB : TEMB + 1]
+    spread = image_ref[:, TEMB + 1 : TEMB + 2]
+    weight = image_ref[:, TEMB + 2 : TEMB + 3]
     left[...] = jnp.zeros_like(left)
     for c in range(3):
         noise = noise_ref[c]
@@ -1608,12 +1664,6 @@
     return np.pad(full.reshape(TAPS * ROWS12, 27), ((0, 0), (0, 5))).astype(np.float32)
 
 
-def same_group(chans):
-    group = np.arange(chans) // (chans // GROUPS)
-    same = (group[:, None] == group[None, :]) / (PLACES * (chans // GROUPS))
-    return same.astype(LOWTYPE)
-
-
 def shards(
     images,
     pixel_mask,
@@ -1632,7 +1682,8 @@
     owners, peers = lax.axis_size("bucket"), lax.axis_size("batch")
     samples = images.shape[0]
     level, weight = plan(timesteps)
-    per_image = jnp.stack([jnp.sqrt(level), jnp.sqrt(1.0 - level), weight], axis=0)
+    lone = [v[:, None] for v in (jnp.sqrt(level), jnp.sqrt(1.0 - level), weight)]
+    per_image = jnp.concatenate([swish(embed(timesteps))] + lone, axis=1)
     conv1, conv1b, conv2, conv2b, skip, temb, qkv, outw, noisy, noise, mask_weight = open_call(
         owners,
         peers,
@@ -1653,7 +1704,7 @@
             noisy,
             noise,
             mask_weight,
-            swish(embed(timesteps)),
+            per_image,
             stem_weight,
             head_turned,
             conv1,
@@ -1665,8 +1716,6 @@
             qkv,
             outw,
             vectors,
-            same_group(C1),
-            same_group(CHANNELS_MID),
             stem_spread(),
         ],
     )

time: 192 us -> 190 us (0.990)
  no operation moved by 1% of the time
where the time goes in v10:
time: 190 us; the launch traced here: 189 us
  Pallas kernels  186 us (98%)
  other arithmetic  2.28 us (1%)
    pallas_call x1, Pallas kernels, unet_call(): pl.pallas_call(functools.partial(unet_body, group, steps, owners, peers),...  80.9 us
    pallas_call x1, Pallas kernels, muon_call(): pl.pallas_call(functools.partial(muon_body, owners, peers), out_shape=[ja...  74.6 us
    pallas_call x1, Pallas kernels, open_call(): pl.pallas_call(functools.partial(open_body, owners, peers), out_shape=[ja...  26.2 us
    pallas_call x1, Pallas kernels, close_call(): pl.pallas_call(close_body, out_shape=[jax.ShapeDtypeStruct(shape, kind) f...  3.85 us

profile of v10, /device:TPU:0, one launch (start us, length us, event | category | flops | bytes accessed | tf_op | source)
XLA Modules:
  0.0 189.1 jit_solution(17502133477868275249)
XLA Ops:
  0.6 0.7 convert_element_type.4
  1.3 0.7 sqrt_bitcast_fusion.1
  2.0 0.1 copy.30
  2.1 0.1 copy.29
  2.2 0.1 copy.31
  2.3 0.2 multiply_sine_fusion
  2.5 0.7 pad_maximum_fusion.image_ref.time_ref
  3.2 26.2 %shard_map.253 = (bf16[1152,256]{1,0:T(8,128)(2,1)}, bf16[384,768]{1,0:T(8,128)(2,1)}, bf16[2304,256]{1,0:T(8,128)(2,1)}, bf16[768,768]{1,0:T(8,128)(2,1)}, bf16...) custom-call(f32[1280,256]{1,0:T(8,128)} %weight_hbm.1, ...), custom_call_target="tpu_custom_call" | custom-call | tf_op jit(solution)/shard_map/pallas_call | solution.py:1610
  29.5 80.9 %shard_map.254 = (f32[5376,256]{1,0:T(8,128)}, f32[16,384]{1,0:T(8,128)}) custom-call(f32[20,16,256]{2,1,0:T(8,128)} %get-tuple-element.53.noisy_ref, f32[20,16,256]{2,1,0:T(8,128)} %get-tuple-element.54.noise_ref, f32[20,16,256]{2,1,0:T(8,128)} %get-tuple-element.55.maskw_ref, f32[20,515]{1,0:T(8,128)} %pad_maximum_fusion.image_ref.time_ref, ...), custom_call_target="tpu_custom_call" | custom-call | tf_op jit(solution)/shard_map/pallas_call | solution.py:758
  110.4 74.6 %shard_map.255 = (f32[1280,256]{1,0:T(8,128)}, f32[1280,256]{1,0:T(8,128)}, f32[27,128]{1,0:T(8,128)}, f32[27,128]{1,0:T(8,128)}, f32[12,3456]{1,0:T(8,128)}, /*...) custom-call(f32[5376,256]{1,0:T(8,128)} %get-tuple-element.64.rows_ref, ...), custom_call_target="tpu_custom_call" | custom-call | tf_op jit(solution)/shard_map/pallas_call | solution.py:1398
  185.0 3.9 %shard_map.256 = (f32[1280,256]{1,0:T(8,128)}, f32[1280,256]{1,0:T(8,128)}, f32[27,128]{1,0:T(8,128)}, f32[27,128]{1,0:T(8,128)}, f32[12,3456]{1,0:T(8,128)}, /*...) custom-call(f32[1280,256]{1,0:T(8,128)} %get-tuple-element.66.refs_0, ...), custom_call_target="tpu_custom_call" | custom-call | tf_op jit(solution)/shard_map/pallas_call | solution.py:1643
  (3 shorter events, 0.0 us)

commit v11 on v10

--- a/solution.py
+++ b/solution.py
@@ -1626,27 +1626,34 @@
 
 
 def close_body(*refs):
-    values, outs = refs[:10], refs[10:]
-    for source, target in zip(values[:9], outs[:9]):
+    large, values, outs, sems = refs[:2], refs[2:12], refs[12:-1], refs[-1]
+    copies = [pltpu.make_async_copy(large[k], outs[k], sems.at[k]) for k in range(2)]
+    for copy in copies:
+        copy.start()
+    for source, target in zip(values[2:9], outs[2:9]):
         target[...] = source[...]
     for source, target in zip((values[0], values[2], values[4], values[6]), outs[9:13]):
         target[...] = source[...].astype(LOWTYPE)
     sums = values[9]
     outs[13][...] = sums[0:1, 0:1]
     outs[14][...] = sums[1:2, 0:1]
+    for copy in copies:
+        copy.wait()
 
 
 def close_call(values):
     shapes = [(v.shape, F32) for v in values[:9]]
     shapes += [(values[k].shape, LOWTYPE) for k in (0, 2, 4, 6)] + [((1, 1), F32)] * 2
+    hbm = pl.BlockSpec(memory_space=pl.ANY)
     vmem = pl.BlockSpec(memory_space=pltpu.VMEM)
     return pl.pallas_call(
         close_body,
         out_shape=[jax.ShapeDtypeStruct(shape, kind) for shape, kind in shapes],
-        in_specs=[vmem] * len(values),
-        out_specs=[vmem] * len(shapes),
+        in_specs=[hbm, hbm, vmem, hbm] + [vmem] * (len(values) - 2),
+        out_specs=[hbm, hbm] + [vmem] * (len(shapes) - 2),
+        scratch_shapes=[pltpu.SemaphoreType.DMA((2,))],
         compiler_params=pltpu.CompilerParams(vmem_limit_bytes=VMEM_BYTES),
-    )(*values)
+    )(values[0], values[1], *values)
 
 
 def stem_spread():

time: 190 us -> 270 us (1.42)
  Pallas kernels: 186 us -> 265 us
    pallas_call x1, Pallas kernels: 3.85 us -> 83.1 us  [close_call(): pl.pallas_call(close_body, out_shape=[jax.ShapeDtypeStruct(shape, kind) f...]
where the time goes in v11:
time: 270 us; the launch traced here: 268 us
  Pallas kernels  265 us (98%)
    pallas_call x1, Pallas kernels, close_call(): pl.pallas_call(close_body, out_shape=[jax.ShapeDtypeStruct(shape, kind) f...  83.1 us
    pallas_call x1, Pallas kernels, unet_call(): pl.pallas_call(functools.partial(unet_body, group, steps, owners, peers),...  80.9 us
    pallas_call x1, Pallas kernels, muon_call(): pl.pallas_call(functools.partial(muon_body, owners, peers), out_shape=[ja...  74.6 us
    pallas_call x1, Pallas kernels, open_call(): pl.pallas_call(functools.partial(open_body, owners, peers), out_shape=[ja...  26.2 us

profile of v11, /device:TPU:0, one launch (start us, length us, event | category | flops | bytes accessed | tf_op | source)
XLA Modules:
  0.0 268.3 jit_solution(3234936549461135316)
XLA Ops:
  0.6 0.7 convert_element_type.4
  1.3 0.7 sqrt_bitcast_fusion.1
  2.0 0.1 copy.30
  2.1 0.1 copy.29
  2.2 0.1 copy.31
  2.3 0.2 multiply_sine_fusion
  2.5 0.7 pad_maximum_fusion.image_ref.time_ref
  3.2 26.2 %shard_map.253 = (bf16[1152,256]{1,0:T(8,128)(2,1)}, bf16[384,768]{1,0:T(8,128)(2,1)}, bf16[2304,256]{1,0:T(8,128)(2,1)}, bf16[768,768]{1,0:T(8,128)(2,1)}, bf16...) custom-call(f32[1280,256]{1,0:T(8,128)} %weight_hbm.1, ...), custom_call_target="tpu_custom_call" | custom-call | tf_op jit(solution)/shard_map/pallas_call | solution.py:1610
  29.5 80.9 %shard_map.254 = (f32[5376,256]{1,0:T(8,128)}, f32[16,384]{1,0:T(8,128)}) custom-call(f32[20,16,256]{2,1,0:T(8,128)} %get-tuple-element.53.noisy_ref, f32[20,16,256]{2,1,0:T(8,128)} %get-tuple-element.54.noise_ref, f32[20,16,256]{2,1,0:T(8,128)} %get-tuple-element.55.maskw_ref, f32[20,515]{1,0:T(8,128)} %pad_maximum_fusion.image_ref.time_ref, ...), custom_call_target="tpu_custom_call" | custom-call | tf_op jit(solution)/shard_map/pallas_call | solution.py:758
  110.4 74.6 %shard_map.255 = (f32[1280,256]{1,0:T(8,128)}, f32[1280,256]{1,0:T(8,128)}, f32[27,128]{1,0:T(8,128)}, f32[27,128]{1,0:T(8,128)}, f32[12,3456]{1,0:T(8,128)}, /*...) custom-call(f32[5376,256]{1,0:T(8,128)} %get-tuple-element.64.rows_ref, ...), custom_call_target="tpu_custom_call" | custom-call | tf_op jit(solution)/shard_map/pallas_call | solution.py:1398
  185.0 83.1 %shard_map.256 = (f32[1280,256]{1,0:T(8,128)}, f32[1280,256]{1,0:T(8,128)}, f32[27,128]{1,0:T(8,128)}, f32[27,128]{1,0:T(8,128)}, f32[12,3456]{1,0:T(8,128)}, /*...) custom-call(f32[1280,256]{1,0:T(8,128)} %get-tuple-element.66.refs_0, ...), custom_call_target="tpu_custom_call" | custom-call | tf_op jit(solution)/shard_map/pallas_call | solution.py:1649
  (3 shorter events, 0.0 us)
